TPU v7x, 128 devices: a whole 4x4x4 slice. The times are simulated.
128 devices in a mesh: enc: 8 (over y, z_hi), ctx: 16 (over x, z_lo, core).
Axes of the slice: x: 4, y: 4, z: 4 (z_hi: 2, z_lo: 2; z = z_hi * 2 + z_lo), core: 2. Of those that a mesh axis runs over, the one named last changes fastest.
Arguments:
- self_queries: bfloat16 [4096, 4096], P('ctx', 'enc'), may hold values from -88 to 88
- self_keys: bfloat16 [4096, 4096], P('ctx', 'enc'), may hold values from -5 to 5
- self_values: bfloat16 [4096, 4096], P('ctx', 'enc'), may hold values from -6 to 6
- hidden_in: bfloat16 [4096, 4096], P('ctx', 'enc'), may hold values from -6 to 6
- query_gain: bfloat16 [4096], replicated, may hold values from 0.25 to 1.75
- store_gain: bfloat16 [4096], replicated, may hold values from 0.25 to 1.75
- store_table: bfloat16 [65536, 4096], P(('enc', 'ctx')), may hold values from -6 to 6
- cross_query_weight: bfloat16 [4096, 4096], P(None, 'enc'), may hold values from -0.0625 to 0.0625
- cross_kv_weight: bfloat16 [4096, 2, 4096], P(None, None, 'enc'), may hold values from -1.9375 to 1.9375
- self_out_weight: bfloat16 [4096, 4096], P('enc'), may hold values from -0.75 to 0.75
- cross_out_weight: bfloat16 [4096, 4096], P('enc'), may hold values from -0.75 to 0.75
- neighbour_ids: int32 [64, 2, 128], P('ctx', None, 'enc'), may hold values from 0 to 65535, as said below
- neighbour_counts: int32 [64], P('ctx'), may hold values from 1 to 2
Outputs:
- layer_out: bfloat16 [4096, 4096], P('ctx', 'enc')
Inputs may be any that keep to these rules, and one draw needn't show every extreme that they name: `neighbour_ids`: store shard s is the block of 512 consecutive rows held by device s in the mesh order enc, ctx. Of the ids held by one device, at most 2 fall into one shard, and in every draw some shards receive exactly 2 ids from every device.
All inputs are finite; a program needn't handle non-finite values.
Results may differ from a plain program's by a relative error of at most 0.019.
The roundings to bfloat16 on the way count: a program that leaves them out, or rounds other values in their place, can miss the bound.
Values may be sent and summed in bfloat16 or wider, within the bound.
No kernel may reach another device: no remote copies, remote signals or barrier semaphores. Data moves between devices by JAX's collectives and lax.ppermute only.
A program may use at most 192 MiB of HBM per device.

v0:
```python
import functools
import math

import jax
import jax.numpy as jnp
from jax import lax
from jax.experimental import pallas as pl
from jax.experimental.pallas import tpu as pltpu
from jax.sharding import PartitionSpec as P

HD = 128
SPAN = 64
NEIGH = 2
NLEN = 128
EPS = 1e-06

NY = 4
NX = 4
BF = jnp.bfloat16
F32 = jnp.float32
SHORT = pl.CostEstimate(flops=1024, bytes_accessed=1024, transcendentals=0)


def along_y(block, step):
    route = [(y * 2 + z, (y + step) % NY * 2 + z) for y in range(NY) for z in range(2)]
    return lax.ppermute(block, "enc", route)


def swap_z_hi(block):
    return lax.ppermute(block, "enc", [(e, e ^ 1) for e in range(2 * NY)])


def along_x(block, step):
    route = [(x * 4 + r, (x + step) % NX * 4 + r) for x in range(NX) for r in range(4)]
    return lax.ppermute(block, "ctx", route)


def swap_rest(block, bits):
    return lax.ppermute(block, "ctx", [(c, c ^ bits) for c in range(4 * NX)])


def next_ctx(block, step):
    size = 4 * NX
    route = [(c, c + step) for c in range(size) if 0 <= c + step < size]
    return lax.ppermute(block, "ctx", route)


def after(values, *done):
    return jax.tree.map(lambda value: lax.optimization_barrier((value, *done))[0], values)


def gather_rows(block, done):
    half = block.shape[0] // 2
    above, below = along_y(block, -1), along_y(block, 1)
    side = swap_z_hi(block)
    onward = after((below, above), done)
    far = along_y(onward[0][:half], 1), along_y(onward[1][half:], -1)
    side_onward = after(side, done)
    side_above, side_below = along_y(side_onward, -1), along_y(side_onward, 1)
    side_far = swap_z_hi(far[0]), swap_z_hi(far[1])
    return (block, above, *far, below), (side, side_above, *side_far, side_below)


def rms_norm(rows, gain):
    values = rows.astype(F32)
    factor = lax.rsqrt(jnp.mean(values * values, axis=-1, keepdims=True) + EPS)
    return (values * factor * gain.astype(F32)).astype(BF)


def ask(wanted, shard_rows):
    device_count = lax.axis_size("enc") * lax.axis_size("ctx")
    count = wanted.shape[0]
    owner = wanted // shard_rows
    local_row = wanted - owner * shard_rows
    order = jnp.arange(count, dtype=jnp.int32)
    same = (owner[:, None] == owner[None, :]) & (order[None, :] < order[:, None])
    slot = jnp.sum(same.astype(jnp.int32), axis=1)
    destination = owner * 2 + slot
    place = destination[:, None] == jnp.arange(device_count * 2, dtype=jnp.int32)[None, :]
    buffer = jnp.sum(jnp.where(place, local_row[:, None], 0), axis=0)
    return buffer.reshape(device_count, 2), destination


def lookup(asked, store_table):
    return store_table.reshape(-1, store_table.shape[1] // HD, HD)[asked]


def answer(found, destination):
    came = lax.all_to_all(found, ("enc", "ctx"), split_axis=0, concat_axis=0, tiled=True)
    return came[destination].reshape(destination.shape[0], -1)


def causal_kernel(q_blocks, k_blocks, q_ref, near_ref, side_ref, far_ref, o_ref, s_ref, top_ref, acc_ref):
    rows = q_ref.shape[0]
    step = pl.program_id(0)
    mine = q_blocks[step]
    scale = 1.0 / math.sqrt(HD)
    query = q_ref[...]
    parts = [(near_ref, i) for i in range(4)] + [(side_ref, i) for i in range(4)]
    parts = parts + [(far_ref, i) for i in range(8)]
    top_ref[...] = jnp.full(top_ref.shape, -1e30, F32)
    for j, (ref, i) in enumerate(parts):
        @pl.when(k_blocks[j] <= mine)
        def _(j=j, ref=ref, i=i):
            key = ref[i * rows : (i + 1) * rows, :HD]
            s = lax.dot_general(query, key, (((1,), (1,)), ((), ())), preferred_element_type=F32) * scale
            offset = jnp.where(k_blocks[j] == mine, 0, rows)
            q_pos = lax.broadcasted_iota(jnp.int32, s.shape, 0) + offset
            k_pos = lax.broadcasted_iota(jnp.int32, s.shape, 1)
            s = jnp.where(q_pos >= k_pos, s, -1e30)
            s_ref[j] = s
            best = top_ref[...]
            for part in range(rows // HD):
                best = jnp.maximum(best, s[:, part * HD : (part + 1) * HD])
            top_ref[...] = best
    top = jnp.max(top_ref[...], axis=1, keepdims=True)
    acc_ref[...] = jnp.zeros(acc_ref.shape, F32)
    top_ref[...] = jnp.zeros(top_ref.shape, F32)
    for j, (ref, i) in enumerate(parts):
        @pl.when(k_blocks[j] <= mine)
        def _(j=j, ref=ref, i=i):
            value = ref[i * rows : (i + 1) * rows, HD:]
            w = jnp.exp(s_ref[j] - top)
            total = top_ref[...]
            for part in range(rows // HD):
                total = total + w[:, part * HD : (part + 1) * HD]
            top_ref[...] = total
            acc_ref[...] += jnp.dot(w.astype(BF), value, preferred_element_type=F32)
    total = jnp.sum(top_ref[...], axis=1, keepdims=True)
    o_ref[...] = (acc_ref[...] / total).astype(BF)


def causal_attention(queries, near, side, far, q_blocks, k_blocks, rows):
    steps = queries.shape[0] // rows
    whole = lambda a: pl.BlockSpec(a.shape, lambda i, *_: (0, 0))
    return pl.pallas_call(
        causal_kernel,
        grid_spec=pltpu.PrefetchScalarGridSpec(
            num_scalar_prefetch=2,
            grid=(steps,),
            in_specs=[
                pl.BlockSpec((rows, HD), lambda i, *_: (i, 0)),
                whole(near),
                whole(side),
                whole(far),
            ],
            out_specs=pl.BlockSpec((rows, HD), lambda i, *_: (i, 0)),
            scratch_shapes=[
                pltpu.VMEM((16, rows, rows), F32),
                pltpu.VMEM((rows, HD), F32),
                pltpu.VMEM((rows, HD), F32),
            ],
        ),
        out_shape=jax.ShapeDtypeStruct(queries.shape, BF),
        compiler_params=pltpu.CompilerParams(vmem_limit_bytes=32 * 1024 * 1024),
        cost_estimate=SHORT,
    )(q_blocks, k_blocks, queries, near, side, far)


def deal_heads(self_queries, self_keys, self_values):
    x = lax.axis_index("ctx") // 4

    def head(k):
        col = (x + k) % NX * HD
        return jnp.concatenate(
            [lax.dynamic_slice_in_dim(a, col, HD, 1) for a in (self_queries, self_keys, self_values)], axis=1
        )

    return [head(0)] + [along_x(head(k), k) for k in (1, 2, 3)]


def near_attention(pieces, near, side):
    rows = pieces[0].shape[0]
    ctx = lax.axis_index("ctx")
    x, rest = ctx // 4, ctx % 4
    queries = jnp.concatenate([p[:, :HD] for p in pieces], axis=0)
    far = swap_rest(jnp.concatenate([near, side], axis=0), 1)
    source_x = jnp.stack([(x - k) % NX for k in range(4)]).astype(jnp.int32)
    q_blocks = source_x * 4 + rest
    k_blocks = jnp.concatenate([source_x * 4 + (rest ^ bits) for bits in (0, 2, 1, 3)])
    return causal_attention(queries, near, side, far, q_blocks, k_blocks, rows)


def return_heads(context):
    x = lax.axis_index("ctx") // 4
    rows = context.shape[0] // NX
    back = [context[:rows]] + [along_x(context[k * rows : (k + 1) * rows], -k) for k in (1, 2, 3)]
    result = jnp.zeros((rows, NX * HD), BF)
    for k in range(4):
        result = lax.dynamic_update_slice(result, back[k], (0, (x + k) % NX * HD))
    return result


def query_kernel(order, gain_ref, w_ref, *refs):
    count = 2 * NY
    piece_refs, (out_ref, w_buf, sems) = refs[:-3], refs[-3:]
    width = w_buf.shape[1]
    copies = []
    for k in range(count):
        first = pl.multiple_of(order[k] * width, width)
        copies.append(pltpu.make_async_copy(w_ref.at[pl.ds(first, width)], w_buf.at[k], sems.at[k]))
    for copy in copies:
        copy.start()

    def block(k):
        return piece_refs[k // NY][:, k % NY * width : (k % NY + 1) * width].astype(F32)

    square = jnp.zeros((out_ref.shape[0], 1), F32)
    for k in range(count):
        values = block(k)
        square = square + jnp.sum(values * values, axis=1, keepdims=True)
    factor = lax.rsqrt(square * (1.0 / (count * width)) + EPS)
    total = jnp.zeros(out_ref.shape, F32)
    for k in range(count):
        normed = (block(k) * factor * gain_ref[pl.ds(order[k], 1), :]).astype(BF)
        copies[k].wait()
        total = total + jnp.dot(normed, w_buf[k], preferred_element_type=F32)
    out_ref[...] = total.astype(BF)


def project_queries(pieces, gain, weight, order):
    rows, width = pieces[0].shape[0], pieces[0].shape[1] // NY
    vmem = pl.BlockSpec(memory_space=pltpu.VMEM)
    return pl.pallas_call(
        query_kernel,
        in_specs=[pl.BlockSpec(memory_space=pltpu.SMEM), vmem, pl.BlockSpec(memory_space=pl.ANY)] + [vmem] * len(pieces),
        out_specs=vmem,
        out_shape=jax.ShapeDtypeStruct((rows, weight.shape[1]), BF),
        scratch_shapes=[
            pltpu.VMEM((2 * NY, width, weight.shape[1]), BF),
            pltpu.SemaphoreType.DMA((2 * NY,)),
        ],
        compiler_params=pltpu.CompilerParams(vmem_limit_bytes=24 * 1024 * 1024),
        cost_estimate=SHORT,
    )(order, gain.astype(F32).reshape(2 * NY, width), weight, *pieces)


def project_rows(n_refs, w_ref, n_buf, w_buf, acc, n_sems, w_sems):
    deep = w_buf.shape[1]
    copies, first = [], 0
    for i, ref in enumerate(n_refs):
        copies.append(pltpu.make_async_copy(ref, n_buf.at[pl.ds(first, ref.shape[0])], n_sems.at[i]))
        first += ref.shape[0]
    w_copies = [
        pltpu.make_async_copy(w_ref.at[pl.ds(k * deep, deep)], w_buf.at[k], w_sems.at[k]) for k in range(w_buf.shape[0])
    ]
    for copy in copies + w_copies:
        copy.start()
    for copy in copies:
        copy.wait()
    for k, copy in enumerate(w_copies):
        copy.wait()
        part = jnp.dot(n_buf[:, k * deep : (k + 1) * deep], w_buf[k], preferred_element_type=F32)
        if k == 0:
            acc[...] = part
        else:
            acc[...] += part


def rows_kernel(w_ref, *refs):
    n_refs, (out_ref, *scratch) = refs[:-6], refs[-6:]
    project_rows(n_refs, w_ref, *scratch)
    out_ref[...] = scratch[2][...].astype(BF)


def span_kernel(counts, q_ref, kv_ref, w_ref, *refs):
    n_refs, (out_ref, tail_ref, *scratch) = refs[:-7], refs[-7:]
    project_rows(n_refs, w_ref, *scratch)
    acc = scratch[2]
    queries, keys = q_ref.shape[0], acc.shape[0]
    width = q_ref.shape[1]
    heads = width // HD
    spans = queries // SPAN
    rows = keys // NY
    token_rows = rows // spans
    q_span = lax.broadcasted_iota(jnp.int32, (queries, keys), 0) // SPAN
    column = lax.broadcasted_iota(jnp.int32, (queries, keys), 1)
    k_span = column % rows // token_rows
    k_neighbour = column % token_rows // (token_rows // NEIGH)
    used = jnp.zeros((queries, keys), jnp.int32)
    for i in range(spans):
        used = jnp.where(q_span == i, counts[i], used)
    allowed = (q_span == k_span) & (k_neighbour < used)

    def score(query, key):
        s = lax.dot_general(query, key, (((1,), (1,)), ((), ())), preferred_element_type=F32)
        return jnp.where(allowed, s * (1.0 / math.sqrt(HD)), -1e30)

    for h in range(heads):
        cols = slice(h * HD, (h + 1) * HD)
        value_cols = slice(width + h * HD, width + (h + 1) * HD)
        query = q_ref[:, cols]
        first, second = score(query, kv_ref[:, cols]), score(query, acc[:, cols].astype(BF))
        top = jnp.max(jnp.maximum(first, second), axis=1, keepdims=True)
        first, second = jnp.exp(first - top), jnp.exp(second - top)
        total = jnp.sum(first + second, axis=1, keepdims=True)
        context = jnp.dot(first.astype(BF), kv_ref[:, value_cols], preferred_element_type=F32)
        context = context + jnp.dot(
            second.astype(BF), acc[:, value_cols].astype(BF), preferred_element_type=F32
        )
        context = (context / total).astype(BF)
        out_ref[:, cols] = context
        tail_ref[:, cols] = context[queries - SPAN :]


def rows_scratch(normed, weight, steps=8):
    key_rows = sum(piece.shape[0] for piece in normed)
    depth, width = weight.shape
    return [
        pltpu.VMEM((key_rows, depth), BF),
        pltpu.VMEM((steps, depth // steps, width), BF),
        pltpu.VMEM((key_rows, width), F32),
        pltpu.SemaphoreType.DMA((len(normed),)),
        pltpu.SemaphoreType.DMA((steps,)),
    ]


def keys_values(weight, normed):
    any_space = pl.BlockSpec(memory_space=pl.ANY)
    key_rows = sum(piece.shape[0] for piece in normed)
    return pl.pallas_call(
        rows_kernel,
        in_specs=[any_space] * (1 + len(normed)),
        out_specs=pl.BlockSpec(memory_space=pltpu.VMEM),
        out_shape=jax.ShapeDtypeStruct((key_rows, weight.shape[1]), BF),
        scratch_shapes=rows_scratch(normed, weight),
        compiler_params=pltpu.CompilerParams(vmem_limit_bytes=28 * 1024 * 1024),
        cost_estimate=SHORT,
    )(weight, *normed)


def attend_spans(queries, counts, kv, weight, normed):
    rows, width = queries.shape
    any_space = pl.BlockSpec(memory_space=pl.ANY)
    vmem = pl.BlockSpec(memory_space=pltpu.VMEM)
    return pl.pallas_call(
        span_kernel,
        in_specs=[pl.BlockSpec(memory_space=pltpu.SMEM), vmem, vmem] + [any_space] * (1 + len(normed)),
        out_specs=(vmem, vmem),
        out_shape=(jax.ShapeDtypeStruct((rows, width), BF), jax.ShapeDtypeStruct((SPAN, width), BF)),
        scratch_shapes=rows_scratch(normed, weight),
        compiler_params=pltpu.CompilerParams(vmem_limit_bytes=32 * 1024 * 1024),
        cost_estimate=SHORT,
    )(counts, queries, kv, weight, *normed)


def scatter_sum(projected):
    rows, width = projected.shape
    enc = lax.axis_index("enc")
    y, z = enc // 2, enc % 2
    part = width // (2 * NY)
    half = rows // 2
    top, low = projected[:half], projected[half:]

    def take(a, yy, zz):
        return lax.dynamic_slice_in_dim(a, (yy * 2 + zz) * part, part, 1)

    def pair(a, k):
        return lax.dynamic_slice_in_dim(a, (y + k) % NY * 2 * part, 2 * part, 1)

    low_far = jnp.concatenate([take(low, yy, 1 - z) for yy in range(NY)], axis=1)
    low_near = jnp.concatenate([take(low, yy, z) for yy in range(NY)], axis=1)
    low_got = swap_z_hi(low_far.astype(BF))
    top_got = [along_y(pair(top, k).astype(BF), k) for k in (1, 3, 2)]
    low_sum = low_near + low_got.astype(F32)

    def column(k):
        return lax.dynamic_slice_in_dim(low_sum, (y + k) % NY * part, part, 1)

    last_got = [along_y(column(k).astype(BF), k) for k in (1, 3, 2)]
    top_sum = pair(top, 0)
    for got in top_got:
        top_sum = top_sum + got.astype(F32)
    far = lax.dynamic_slice_in_dim(top_sum, (1 - z) * part, part, 1)
    near = lax.dynamic_slice_in_dim(top_sum, z * part, part, 1)
    top_out = near + swap_z_hi(far.astype(BF)).astype(F32)
    low_out = column(0)
    for got in last_got:
        low_out = low_out + got.astype(F32)
    return jnp.concatenate([top_out, low_out], axis=0)


def per_device(
    self_queries,
    self_keys,
    self_values,
    hidden_in,
    query_gain,
    store_gain,
    store_table,
    cross_query_weight,
    cross_kv_weight,
    self_out_weight,
    cross_out_weight,
    neighbour_ids,
    neighbour_counts,
):
    rows, local_width = self_queries.shape
    enc = lax.axis_index("enc")
    y, z = enc // 2, enc % 2

    request, destination = ask(neighbour_ids.reshape(-1), store_table.shape[0])
    asked = lax.all_to_all(request, ("enc", "ctx"), split_axis=0, concat_axis=0, tiled=True).reshape(-1)
    dealt = deal_heads(*after((self_queries, self_keys, self_values), request))
    near = jnp.concatenate([p[:, HD:] for p in dealt], axis=0)
    found = lookup(after(asked, near), store_table)
    near, hidden, cross_kv_weight = after((near, hidden_in, cross_kv_weight), found)
    side = swap_rest(near, 2)
    hidden = [hidden, along_y(hidden, -1), along_y(hidden, 2), along_y(hidden, 1)]
    kv_weight = cross_kv_weight.reshape(-1, 2 * local_width)

    own_rows = rms_norm(answer(found, destination), store_gain)
    own_rows = after(own_rows, kv_weight, side, *hidden)
    near, side, hidden = after((near, side, hidden), own_rows)
    near_context = near_attention(dealt, near, side)
    normed, side_normed = gather_rows(own_rows, near_context)
    kv = keys_values(kv_weight, normed)
    self_context = return_heads(after(near_context, kv))
    self_projected = jnp.dot(self_context, self_out_weight, preferred_element_type=F32)

    hidden = jnp.concatenate(after(hidden, near_context), axis=1)
    far_hidden = swap_z_hi(after(hidden, side_normed[0]))
    turn = jnp.stack([(y + k) % NY for k in range(NY)]).astype(jnp.int32)
    hidden_order = jnp.concatenate([turn * 2 + z, turn * 2 + 1 - z])
    cross_queries = project_queries([hidden, far_hidden], query_gain, cross_query_weight, hidden_order)
    later = next_ctx(cross_queries[:SPAN], -1)
    queries = jnp.concatenate([cross_queries[SPAN - 1 :], later[: SPAN - 1]], axis=0)

    counts = neighbour_counts.astype(jnp.int32)
    queries = after(queries, kv, self_projected)
    context, tail = attend_spans(queries, counts, kv, kv_weight, side_normed)
    earlier = next_ctx(tail, 1)
    cross_context = jnp.concatenate([earlier[1:], context[: rows - SPAN + 1]], axis=0)

    projected = self_projected + jnp.dot(cross_context, cross_out_weight, preferred_element_type=F32)
    return (hidden_in.astype(F32) + scatter_sum(projected)).astype(BF)


def solution(mesh):
    placed = (
        P("ctx", "enc"),
        P("ctx", "enc"),
        P("ctx", "enc"),
        P("ctx", "enc"),
        P(),
        P(),
        P(("enc", "ctx"), None),
        P(None, "enc"),
        P(None, None, "enc"),
        P("enc", None),
        P("enc", None),
        P("ctx", None, "enc"),
        P("ctx"),
    )
    return jax.shard_map(
        per_device, mesh=mesh, in_specs=placed, out_specs=P("ctx", "enc"), check_vma=False
    )
```

profile of v0, /device:TPU:6, one launch (start us, length us, event | category | flops | bytes accessed | tf_op | source)
XLA Modules:
  0.0 219.7 jit_solution(15842727011744792029)
XLA Ops:
  3.8 2.6 %collective-permute-start.1 = (bf16[256,384]{1,0:T(8,128)(2,1)S(1)}, bf16[256,384]{1,0:T(8,128)(2,1)S(1)}, u32[]{:S(2)}, u32[]{:S(2)}) collective-permute-start(bf16[256,384]{1,0:T(8,128)(2,1)S(1)} %pad_maximum_fusion.6), channel_id=1, source_target_pairs={{0,8},{1,9},{2,10},{3,11},{4,12},{5,13},{6,14},{7,15},{8,0},{9,1},... | collective-permute-start | bytes 589832 | tf_op jit(solution)/shard_map/ppermute | solution.py:35
  7.2 10.8 %all-to-all-start = ((s32[128,1,2]{2,1,0:T(1,128)}), s32[128,1,2]{2,1,0:T(1,128)S(1)}, u32[]{:S(2)}, u32[]{:S(2)}) async-start(s32[128,1,2]{2,1,0:T(1,128)} %bitcast.4), calls=%async_computation | async-start | bytes 131072 | tf_op jit(solution)/shard_map/all_to_all | solution.py:403
  18.0 5.5 %copy.16 = bf16[64,8,32,128]{3,2,1,0:T(8,128)(2,1)} copy(bf16[64,8,32,128]{3,1,2,0:T(8,128)(2,1)} %bitcast.38) | data formatting | bytes 8388608
  23.5 2.9 %all-to-all-done = s32[128,1,2]{2,1,0:T(1,128)S(1)} async-done(((s32[128,1,2]{2,1,0:T(1,128)}), s32[128,1,2]{2,1,0:T(1,128)S(1)}, u32[]{:S(2)}, u32[]{:S(2)}) %all-to-all-start) | async-done | bytes 1056 | tf_op jit(solution)/shard_map/all_to_all | solution.py:403
  28.0 4.4 %gather_fusion = bf16[256,32,128]{2,1,0:T(8,128)(2,1)} fusion(bf16[512,32,128]{2,1,0:T(8,128)(2,1)} %bitcast.35, s32[1024]{0:T(1024)S(1)} %pad_clamp_fusion.1), kind=kCustom, calls=%fused_computation | custom fusion | bytes 4195328 | tf_op jit(solution)/shard_map/gather | solution.py:85
  32.4 7.3 %all-to-all-start.1 = ((bf16[256,32,128]{2,1,0:T(8,128)(2,1)}), bf16[256,32,128]{2,1,0:T(8,128)(2,1)}, u32[]{:S(2)}, u32[]{:S(2)}) async-start(bf16[256,32,128]{2,1,0:T(8,128)(2,1)} %gather_fusion), calls=%async_computation.1 | async-start | bytes 4194304 | tf_op jit(solution)/shard_map/all_to_all | solution.py:89
  39.9 1.5 collective-permute-start.6
  41.4 2.8 %collective-permute-start.5 = (bf16[256,512]{1,0:T(8,128)(2,1)S(1)}, bf16[256,512]{1,0:T(8,128)(2,1)S(1)}, u32[]{:S(2)}, u32[]{:S(2)}) collective-permute-start(bf16[256,512]{1,0:T(8,128)(2,1)S(1)} %copy-done.5), channel_id=1, source_target_pairs={{0,64},{16,80},{32,96},{48,112},{64,0},{80,16},{96,32},{112,48},{1... | collective-permute-start | bytes 786440 | tf_op jit(solution)/shard_map/ppermute | solution.py:26
  44.2 1.4 collective-permute-start.4
  45.6 1.7 collective-permute-start.3
  47.3 9.4 %copy.18 = bf16[512,8,2,512]{3,1,2,0:T(8,128)(2,1)} copy(bf16[512,8,2,512]{3,2,1,0:T(2,128)(2,1)} %bitcast.37) | data formatting | bytes 16777216
  56.7 11.4 %all-to-all-done.1 = bf16[256,32,128]{2,1,0:T(8,128)(2,1)} async-done(((bf16[256,32,128]{2,1,0:T(8,128)(2,1)}), bf16[256,32,128]{2,1,0:T(8,128)(2,1)}, u32[]{:S(2)}, u32[]{:S(2)}) %all-to-all-start.1) | async-done | bytes 2097184 | tf_op jit(solution)/shard_map/all_to_all | solution.py:89
  68.1 2.4 %gather_fusion.1 = bf16[128,32,128]{2,1,0:T(8,128)(2,1)S(1)} fusion(bf16[256,32,128]{2,1,0:T(8,128)(2,1)} %all-to-all-done.1, s32[1024]{0:T(1024)S(1)} %pad_clamp_fusion), kind=kCustom, calls=%fused_computation.1 | custom fusion | bytes 2097664 | tf_op jit(solution)/shard_map/gather | solution.py:90
  71.8 1.8 fusion.1.refs_0_
  73.7 2.6 %collective-permute-done.5 = bf16[256,512]{1,0:T(8,128)(2,1)S(1)} collective-permute-done((bf16[256,512]{1,0:T(8,128)(2,1)S(1)}, bf16[256,512]{1,0:T(8,128)(2,1)S(1)}, u32[]{:S(2)}, u32[]{:S(2)}) %collective-permute-start.5) | collective-permute-done | bytes 262176 | tf_op jit(solution)/shard_map/ppermute | solution.py:26
  78.4 2.7 %collective-permute-start.8 = (bf16[128,4096]{1,0:T(8,128)(2,1)S(1)}, bf16[128,4096]{1,0:T(8,128)(2,1)}, u32[]{:S(2)}, u32[]{:S(2)}) collective-permute-start(bf16[128,4096]{1,0:T(8,128)(2,1)S(1)} %fusion.1.refs_0_), channel_id=1, source_target_pairs={{0,96},{16,112},{32,0},{48,16},{64,32},{80,48},{96,64},{112,80},{1... | collective-permute-start | bytes 3145736 | tf_op jit(solution)/shard_map/ppermute | solution.py:26
  81.1 3.5 %collective-permute-start.15 = (bf16[128,4096]{1,0:T(8,128)(2,1)S(1)}, bf16[128,4096]{1,0:T(8,128)(2,1)}, u32[]{:S(2)}, u32[]{:S(2)}) collective-permute-start(bf16[128,4096]{1,0:T(8,128)(2,1)S(1)} %fusion.1.refs_0_), channel_id=1, source_target_pairs={{0,16},{16,0},{32,48},{48,32},{64,80},{80,64},{96,112},{112,96},{1... | collective-permute-start | bytes 3145736 | tf_op jit(solution)/shard_map/ppermute | solution.py:30
  86.5 13.8 %shard_map.127 = bf16[1024,128]{1,0:T(8,128)(2,1)S(1)} custom-call(s32[4]{0:T(128)S(1)} %get-tuple-element.97.q_blocks, s32[16]{0:T(128)S(1)} %pad_add_fusion.k_blocks, bf16[1024,128]{1,0:T(8,128)(2,1)S(1)} %pad_maximum_fusion.3.q_ref, bf16[1024,256]{1,0:T(8,128)(2,1)S(1)} %pad_maximum_fusion.1.near_ref, ...), custom_call_target="tpu_custom_call" | custom-call | flops 1024 | bytes 1024 | tf_op jit(solution)/shard_map/pallas_call | solution.py:136
  100.4 4.0 %collective-permute-done.9.refs_4_ = bf16[128,4096]{1,0:T(8,128)(2,1)S(1)} collective-permute-done((bf16[128,4096]{1,0:T(8,128)(2,1)S(1)}, bf16[128,4096]{1,0:T(8,128)(2,1)S(1)}, u32[]{:S(2)}, u32[]{:S(2)}) %collective-permute-start.9) | collective-permute-done | bytes 1048608 | tf_op jit(solution)/shard_map/ppermute | solution.py:26
  105.3 1.9 slice.64
  107.1 3.2 %collective-permute-start.11 = (bf16[64,4096]{1,0:T(8,128)(2,1)}, bf16[64,4096]{1,0:T(8,128)(2,1)S(1)}, u32[]{:S(2)}, u32[]{:S(2)}) collective-permute-start(bf16[64,4096]{1,0:T(8,128)(2,1)} %slice.64), channel_id=1, source_target_pairs={{0,96},{16,112},{32,0},{48,16},{64,32},{80,48},{96,64},{112,80},{1... | collective-permute-start | bytes 1572872 | tf_op jit(solution)/shard_map/ppermute | solution.py:26
  113.4 3.5 %collective-permute-start.16 = (bf16[256,2048]{1,0:T(8,128)(2,1)}, bf16[256,2048]{1,0:T(8,128)(2,1)}, u32[]{:S(2)}, u32[]{:S(2)}) collective-permute-start(bf16[256,2048]{1,0:T(8,128)(2,1)} %constant_dynamic-update-slice_fusion.3.refs_0_), channel_id=1, source_target_pairs={{0,16},{16,0},{32,48},{48,32},{64,80},{80,64},{96,112},{112,96},{1... | collective-permute-start | bytes 3145736 | tf_op jit(solution)/shard_map/ppermute | solution.py:30
  117.1 3.2 %collective-permute-start.18 = (bf16[128,4096]{1,0:T(8,128)(2,1)}, bf16[128,4096]{1,0:T(8,128)(2,1)S(1)}, u32[]{:S(2)}, u32[]{:S(2)}) collective-permute-start(bf16[128,4096]{1,0:T(8,128)(2,1)} %collective-permute-done.15.refs_0_), channel_id=1, source_target_pairs={{0,96},{16,112},{32,0},{48,16},{64,32},{80,48},{96,64},{112,80},{1... | collective-permute-start | bytes 3145736 | tf_op jit(solution)/shard_map/ppermute | solution.py:26
  120.4 2.7 %collective-permute-done.11.refs_3_ = bf16[64,4096]{1,0:T(8,128)(2,1)S(1)} collective-permute-done((bf16[64,4096]{1,0:T(8,128)(2,1)}, bf16[64,4096]{1,0:T(8,128)(2,1)S(1)}, u32[]{:S(2)}, u32[]{:S(2)}) %collective-permute-start.11) | collective-permute-done | bytes 524320 | tf_op jit(solution)/shard_map/ppermute | solution.py:26
  123.1 3.4 %copy-done = bf16[512,8,2,512]{3,1,2,0:T(8,128)(2,1)S(1)} copy-done((bf16[512,8,2,512]{3,1,2,0:T(8,128)(2,1)S(1)}, bf16[512,8,2,512]{3,1,2,0:T(8,128)(2,1)}, u32[]{:S(2)}) %copy-start) | copy-done | bytes 8388632
  126.5 6.4 %shard_map.128.kv_ref = bf16[512,1024]{1,0:T(8,128)(2,1)S(1)} custom-call(bf16[4096,1024]{1,0:T(8,128)(2,1)S(1)} %bitcast.31, bf16[128,4096]{1,0:T(8,128)(2,1)S(1)} %fusion.1.refs_0_, bf16[128,4096]{1,0:T(8,128)(2,1)} %collective-permute-done.8.refs_1_, bf16[64,4096]{1,0:T(8,128)(2,1)S(1)} %collective-permute-done.10.refs_2_, ...), custom_call_target="tpu_custom_call" | custom-call | flops 1024 | bytes 1024 | tf_op jit(solution)/shard_map/pallas_call | solution.py:321
  134.0 2.4 %collective-permute-start.14 = (bf16[256,128]{1,0:T(8,128)(2,1)S(1)}, bf16[256,128]{1,0:T(8,128)(2,1)S(1)}, u32[]{:S(2)}, u32[]{:S(2)}) collective-permute-start(bf16[256,128]{1,0:T(8,128)(2,1)S(1)} %get-tuple-element.79), channel_id=1, source_target_pairs={{0,4},{1,5},{2,6},{3,7},{4,8},{5,9},{6,10},{7,11},{8,12},{9,13},{1... | collective-permute-start | bytes 196616 | tf_op jit(solution)/shard_map/ppermute | solution.py:35
  136.4 2.2 collective-permute-done.12
  138.8 5.5 %collective-permute-done.13 = bf16[256,128]{1,0:T(8,128)(2,1)S(1)} collective-permute-done((bf16[256,128]{1,0:T(8,128)(2,1)S(1)}, bf16[256,128]{1,0:T(8,128)(2,1)S(1)}, u32[]{:S(2)}, u32[]{:S(2)}) %collective-permute-start.13) | collective-permute-done | bytes 65568 | tf_op jit(solution)/shard_map/ppermute | solution.py:35
  144.3 4.2 %collective-permute-start.19 = (bf16[64,4096]{1,0:T(8,128)(2,1)S(1)}, bf16[64,4096]{1,0:T(8,128)(2,1)S(1)}, u32[]{:S(2)}, u32[]{:S(2)}) collective-permute-start(bf16[64,4096]{1,0:T(8,128)(2,1)S(1)} %collective-permute-done.10.refs_2_), channel_id=1, source_target_pairs={{0,16},{16,0},{32,48},{48,32},{64,80},{80,64},{96,112},{112,96},{1... | collective-permute-start | bytes 1572872 | tf_op jit(solution)/shard_map/ppermute | solution.py:30
  149.0 4.6 %shard_map.129 = bf16[256,512]{1,0:T(8,128)(2,1)S(1)} custom-call(s32[8]{0:T(128)S(1)} %pad_add_fusion.1.order, f32[8,512]{1,0:T(8,128)S(1)} %reshape.199.gain_ref, bf16[4096,512]{1,0:T(8,128)(2,1)S(1)} %copy-done.1, bf16[256,2048]{1,0:T(8,128)(2,1)} %constant_dynamic-update-slice_fusion.3.refs_0_, bf16[256,2048]{1,0:T(8,128)(2,1)} %collective-permute-done.16.refs_1_), custom_call_target="tpu_custom_call" | custom-call | flops 1024 | bytes 1024 | tf_op jit(solution)/shard_map/pallas_call | solution.py:224
  153.6 2.2 collective-permute-start.17
  155.8 3.4 %fusion.11 = f32[256,4096]{1,0:T(8,128)} fusion(bf16[256,512]{1,0:T(8,128)(2,1)S(1)} %constant_dynamic-update-slice_fusion, bf16[512,4096]{1,0:T(8,128)(2,1)S(1)} %copy-done.3), kind=kOutput, calls=%fused_computation.94 | convolution fusion | flops 1073741824 | bytes 8650752 | tf_op jit(solution)/shard_map/dot_general | solution.py:419
  160.3 5.6 %collective-permute-done.20.refs_3_ = bf16[64,4096]{1,0:T(8,128)(2,1)S(1)} collective-permute-done((bf16[64,4096]{1,0:T(8,128)(2,1)S(1)}, bf16[64,4096]{1,0:T(8,128)(2,1)S(1)}, u32[]{:S(2)}, u32[]{:S(2)}) %collective-permute-start.20) | collective-permute-done | bytes 524320 | tf_op jit(solution)/shard_map/ppermute | solution.py:30
  166.0 8.9 %shard_map.130 = (bf16[256,512]{1,0:T(8,128)(2,1)S(1)}, bf16[64,512]{1,0:T(8,128)(2,1)S(1)}) custom-call(s32[4]{0:T(128)S(1)} %copy-done.2, bf16[256,512]{1,0:T(8,128)(2,1)S(1)} %pad_maximum_fusion.4.q_ref, bf16[512,1024]{1,0:T(8,128)(2,1)S(1)} %shard_map.128.kv_ref, bf16[4096,1024]{1,0:T(8,128)(2,1)S(1)} %bitcast.34, ...), custom_call_target="tpu_custom_call" | custom-call | flops 1024 | bytes 1024 | tf_op jit(solution)/shard_map/pallas_call | solution.py:336
  174.8 3.3 %collective-permute-start.22 = (bf16[64,512]{1,0:T(8,128)(2,1)S(1)}, bf16[64,512]{1,0:T(8,128)(2,1)S(1)}, u32[]{:S(2)}, u32[]{:S(2)}) collective-permute-start(bf16[64,512]{1,0:T(8,128)(2,1)S(1)} %get-tuple-element.55), channel_id=1, source_target_pairs={{0,1},{1,2},{2,3},{3,4},{4,5},{5,6},{6,7},{7,8},{8,9},{9,10},{10,1... | collective-permute-start | bytes 196616 | tf_op jit(solution)/shard_map/ppermute | solution.py:45
  178.2 3.1 %collective-permute-done.22 = bf16[64,512]{1,0:T(8,128)(2,1)S(1)} collective-permute-done((bf16[64,512]{1,0:T(8,128)(2,1)S(1)}, bf16[64,512]{1,0:T(8,128)(2,1)S(1)}, u32[]{:S(2)}, u32[]{:S(2)}) %collective-permute-start.22) | collective-permute-done | bytes 65568 | tf_op jit(solution)/shard_map/ppermute | solution.py:45
  181.3 4.8 %convolution_add_fusion = f32[256,4096]{1,0:T(8,128)S(1)} fusion(f32[256,4096]{1,0:T(8,128)} %fusion.11, bf16[512,4096]{1,0:T(8,128)(2,1)} %param.23, bf16[193,512]{1,0:T(8,128)(2,1)S(1)} %slice.73, bf16[63,512]{1,0:T(8,128)(2,1)S(1)} %slice.89), kind=kOutput, calls=%fused_computation.2 | convolution fusion | flops 1075314688 | bytes 12845056 | tf_op jit(solution)/shard_map/dot_general | solution.py:435
  186.6 1.3 copy-done.4
  188.8 4.7 %collective-permute-start.25 = (bf16[128,1024]{1,0:T(8,128)(2,1)}, bf16[128,1024]{1,0:T(8,128)(2,1)}, u32[]{:S(2)}, u32[]{:S(2)}) collective-permute-start(bf16[128,1024]{1,0:T(8,128)(2,1)} %get-tuple-element.66), channel_id=1, source_target_pairs={{0,64},{16,80},{32,96},{48,112},{64,0},{80,16},{96,32},{112,48},{1... | collective-permute-start | bytes 786440 | tf_op jit(solution)/shard_map/ppermute | solution.py:26
  193.7 3.3 %collective-permute-start.27 = (bf16[128,2048]{1,0:T(8,128)(2,1)S(1)}, bf16[128,2048]{1,0:T(8,128)(2,1)S(1)}, u32[]{:S(2)}, u32[]{:S(2)}) collective-permute-start(bf16[128,2048]{1,0:T(8,128)(2,1)S(1)} %pad_maximum_fusion.2), channel_id=1, source_target_pairs={{0,16},{16,0},{32,48},{48,32},{64,80},{80,64},{96,112},{112,96},{1... | collective-permute-start | bytes 1572872 | tf_op jit(solution)/shard_map/ppermute | solution.py:30
  197.1 1.6 collective-permute-done.23
  198.8 5.3 %collective-permute-done.25 = bf16[128,1024]{1,0:T(8,128)(2,1)} collective-permute-done((bf16[128,1024]{1,0:T(8,128)(2,1)}, bf16[128,1024]{1,0:T(8,128)(2,1)}, u32[]{:S(2)}, u32[]{:S(2)}) %collective-permute-start.25) | collective-permute-done | bytes 262176 | tf_op jit(solution)/shard_map/ppermute | solution.py:26
  204.0 1.4 convert_add_fusion
  205.5 3.6 %collective-permute-start.26 = (bf16[128,512]{1,0:T(8,128)(2,1)S(1)}, bf16[128,512]{1,0:T(8,128)(2,1)S(1)}, u32[]{:S(2)}, u32[]{:S(2)}) collective-permute-start(bf16[128,512]{1,0:T(8,128)(2,1)S(1)} %dynamic-slice_convert_fusion.10), channel_id=1, source_target_pairs={{0,16},{16,0},{32,48},{48,32},{64,80},{80,64},{96,112},{112,96},{1... | collective-permute-start | bytes 393224 | tf_op jit(solution)/shard_map/ppermute | solution.py:30
  209.9 3.0 %collective-permute-start.30 = (bf16[128,512]{1,0:T(8,128)(2,1)S(1)}, bf16[128,512]{1,0:T(8,128)(2,1)S(1)}, u32[]{:S(2)}, u32[]{:S(2)}) collective-permute-start(bf16[128,512]{1,0:T(8,128)(2,1)S(1)} %get-tuple-element.77), channel_id=1, source_target_pairs={{0,64},{16,80},{32,96},{48,112},{64,0},{80,16},{96,32},{112,48},{1... | collective-permute-start | bytes 393224 | tf_op jit(solution)/shard_map/ppermute | solution.py:26
  213.2 3.1 %collective-permute-done.28 = bf16[128,512]{1,0:T(8,128)(2,1)S(1)} collective-permute-done((bf16[128,512]{1,0:T(8,128)(2,1)S(1)}, bf16[128,512]{1,0:T(8,128)(2,1)S(1)}, u32[]{:S(2)}, u32[]{:S(2)}) %collective-permute-start.28) | collective-permute-done | bytes 131104 | tf_op jit(solution)/shard_map/ppermute | solution.py:26
  216.4 2.5 %collective-permute-done.30 = bf16[128,512]{1,0:T(8,128)(2,1)S(1)} collective-permute-done((bf16[128,512]{1,0:T(8,128)(2,1)S(1)}, bf16[128,512]{1,0:T(8,128)(2,1)S(1)}, u32[]{:S(2)}, u32[]{:S(2)}) %collective-permute-start.30) | collective-permute-done | bytes 131104 | tf_op jit(solution)/shard_map/ppermute | solution.py:26
  (138 shorter events, 22.1 us)
Async XLA Ops:
  3.3 24.6 %collective-permute-start = (bf16[256,384]{1,0:T(8,128)(2,1)S(1)}, bf16[256,384]{1,0:T(8,128)(2,1)S(1)}, u32[]{:S(2)}, u32[]{:S(2)}) collective-permute-start(bf16[256,384]{1,0:T(8,128)(2,1)S(1)} %pad_maximum_fusion.5), channel_id=1, source_target_pairs={{0,4},{1,5},{2,6},{3,7},{4,8},{5,9},{6,10},{7,11},{8,12},{9,13},{1... | collective-permute-start | bytes 589832 | tf_op jit(solution)/shard_map/ppermute | solution.py:35
  3.8 24.1 %collective-permute-start.1 = (bf16[256,384]{1,0:T(8,128)(2,1)S(1)}, bf16[256,384]{1,0:T(8,128)(2,1)S(1)}, u32[]{:S(2)}, u32[]{:S(2)}) collective-permute-start(bf16[256,384]{1,0:T(8,128)(2,1)S(1)} %pad_maximum_fusion.6), channel_id=1, source_target_pairs={{0,8},{1,9},{2,10},{3,11},{4,12},{5,13},{6,14},{7,15},{8,0},{9,1},... | collective-permute-start | bytes 589832 | tf_op jit(solution)/shard_map/ppermute | solution.py:35
  6.4 21.5 %collective-permute-start.2 = (bf16[256,384]{1,0:T(8,128)(2,1)S(1)}, bf16[256,384]{1,0:T(8,128)(2,1)S(1)}, u32[]{:S(2)}, u32[]{:S(2)}) collective-permute-start(bf16[256,384]{1,0:T(8,128)(2,1)S(1)} %pad_maximum_fusion.7), channel_id=1, source_target_pairs={{0,12},{1,13},{2,14},{3,15},{4,0},{5,1},{6,2},{7,3},{8,4},{9,5},{1... | collective-permute-start | bytes 589832 | tf_op jit(solution)/shard_map/ppermute | solution.py:35
  7.2 19.2 %all-to-all-start = ((s32[128,1,2]{2,1,0:T(1,128)}), s32[128,1,2]{2,1,0:T(1,128)S(1)}, u32[]{:S(2)}, u32[]{:S(2)}) async-start(s32[128,1,2]{2,1,0:T(1,128)} %bitcast.4), calls=%async_computation | async-start | bytes 131072 | tf_op jit(solution)/shard_map/all_to_all | solution.py:403
  27.9 28.8 %copy-start.14 = (bf16[256,384]{1,0:T(8,128)(2,1)}, bf16[256,384]{1,0:T(8,128)(2,1)S(1)}, u32[]{:S(2)}) copy-start(bf16[256,384]{1,0:T(8,128)(2,1)S(1)} %collective-permute-done.1) | copy-start | bytes 589828
  32.4 7.3 %copy-start.16 = (s32[4,2,16]{2,1,0:T(2,128)S(1)}, s32[4,2,16]{2,1,0:T(2,128)}, u32[]{:S(2)}) copy-start(s32[4,2,16]{2,1,0:T(2,128)} %param.24) | copy-start | bytes 1540
  32.4 7.4 %copy-start.17 = (bf16[4096]{0:T(1024)(128)(2,1)S(1)}, bf16[4096]{0:T(1024)(128)(2,1)}, u32[]{:S(2)}) copy-start(bf16[4096]{0:T(1024)(128)(2,1)} %param.18) | copy-start | bytes 24580
  32.4 7.5 %copy-start.5 = (bf16[256,512]{1,0:T(8,128)(2,1)S(1)}, bf16[256,512]{1,0:T(8,128)(2,1)}, u32[]{:S(2)}) copy-start(bf16[256,512]{1,0:T(8,128)(2,1)} %param.16) | copy-start | bytes 786436
  32.4 35.7 %all-to-all-start.1 = ((bf16[256,32,128]{2,1,0:T(8,128)(2,1)}), bf16[256,32,128]{2,1,0:T(8,128)(2,1)}, u32[]{:S(2)}, u32[]{:S(2)}) async-start(bf16[256,32,128]{2,1,0:T(8,128)(2,1)} %gather_fusion), calls=%async_computation.1 | async-start | bytes 4194304 | tf_op jit(solution)/shard_map/all_to_all | solution.py:89
  39.9 33.8 %collective-permute-start.6 = (bf16[256,512]{1,0:T(8,128)(2,1)S(1)}, bf16[256,512]{1,0:T(8,128)(2,1)S(1)}, u32[]{:S(2)}, u32[]{:S(2)}) collective-permute-start(bf16[256,512]{1,0:T(8,128)(2,1)S(1)} %copy-done.5), channel_id=1, source_target_pairs={{0,32},{16,48},{32,64},{48,80},{64,96},{80,112},{96,0},{112,16},{1... | collective-permute-start | bytes 786440 | tf_op jit(solution)/shard_map/ppermute | solution.py:26
  41.4 34.9 %collective-permute-start.5 = (bf16[256,512]{1,0:T(8,128)(2,1)S(1)}, bf16[256,512]{1,0:T(8,128)(2,1)S(1)}, u32[]{:S(2)}, u32[]{:S(2)}) collective-permute-start(bf16[256,512]{1,0:T(8,128)(2,1)S(1)} %copy-done.5), channel_id=1, source_target_pairs={{0,64},{16,80},{32,96},{48,112},{64,0},{80,16},{96,32},{112,48},{1... | collective-permute-start | bytes 786440 | tf_op jit(solution)/shard_map/ppermute | solution.py:26
  44.2 32.1 %collective-permute-start.4 = (bf16[256,512]{1,0:T(8,128)(2,1)S(1)}, bf16[256,512]{1,0:T(8,128)(2,1)S(1)}, u32[]{:S(2)}, u32[]{:S(2)}) collective-permute-start(bf16[256,512]{1,0:T(8,128)(2,1)S(1)} %copy-done.5), channel_id=1, source_target_pairs={{0,96},{16,112},{32,0},{48,16},{64,32},{80,48},{96,64},{112,80},{1... | collective-permute-start | bytes 786440 | tf_op jit(solution)/shard_map/ppermute | solution.py:26
  45.6 30.7 %collective-permute-start.3 = (bf16[1024,256]{1,0:T(8,128)(2,1)S(1)}, bf16[1024,256]{1,0:T(8,128)(2,1)S(1)}, u32[]{:S(2)}, u32[]{:S(2)}) collective-permute-start(bf16[1024,256]{1,0:T(8,128)(2,1)S(1)} %pad_maximum_fusion.1.near_ref), channel_id=1, source_target_pairs={{0,2},{1,3},{2,0},{3,1},{4,6},{5,7},{6,4},{7,5},{8,10},{9,11},{10,... | collective-permute-start | bytes 1572872 | tf_op jit(solution)/shard_map/ppermute | solution.py:39
  77.5 9.0 %collective-permute-start.7 = (bf16[2048,256]{1,0:T(8,128)(2,1)}, bf16[2048,256]{1,0:T(8,128)(2,1)}, u32[]{:S(2)}, u32[]{:S(2)}) collective-permute-start(bf16[2048,256]{1,0:T(8,128)(2,1)} %pad_maximum_fusion), channel_id=1, source_target_pairs={{0,1},{1,0},{2,3},{3,2},{4,5},{5,4},{6,7},{7,6},{8,9},{9,8},{10,11... | collective-permute-start | bytes 3145736 | tf_op jit(solution)/shard_map/ppermute | solution.py:39
  77.6 26.8 %collective-permute-start.9 = (bf16[128,4096]{1,0:T(8,128)(2,1)S(1)}, bf16[128,4096]{1,0:T(8,128)(2,1)S(1)}, u32[]{:S(2)}, u32[]{:S(2)}) collective-permute-start(bf16[128,4096]{1,0:T(8,128)(2,1)S(1)} %fusion.1.refs_0_), channel_id=1, source_target_pairs={{0,32},{16,48},{32,64},{48,80},{64,96},{80,112},{96,0},{112,16},{1... | collective-permute-start | bytes 3145736 | tf_op jit(solution)/shard_map/ppermute | solution.py:26
  78.4 26.9 %collective-permute-start.8 = (bf16[128,4096]{1,0:T(8,128)(2,1)S(1)}, bf16[128,4096]{1,0:T(8,128)(2,1)}, u32[]{:S(2)}, u32[]{:S(2)}) collective-permute-start(bf16[128,4096]{1,0:T(8,128)(2,1)S(1)} %fusion.1.refs_0_), channel_id=1, source_target_pairs={{0,96},{16,112},{32,0},{48,16},{64,32},{80,48},{96,64},{112,80},{1... | collective-permute-start | bytes 3145736 | tf_op jit(solution)/shard_map/ppermute | solution.py:26
  81.1 32.3 %collective-permute-start.15 = (bf16[128,4096]{1,0:T(8,128)(2,1)S(1)}, bf16[128,4096]{1,0:T(8,128)(2,1)}, u32[]{:S(2)}, u32[]{:S(2)}) collective-permute-start(bf16[128,4096]{1,0:T(8,128)(2,1)S(1)} %fusion.1.refs_0_), channel_id=1, source_target_pairs={{0,16},{16,0},{32,48},{48,32},{64,80},{80,64},{96,112},{112,96},{1... | collective-permute-start | bytes 3145736 | tf_op jit(solution)/shard_map/ppermute | solution.py:30
  86.5 23.9 %copy-start.6 = (bf16[256,512]{1,0:T(8,128)(2,1)S(1)}, bf16[256,512]{1,0:T(8,128)(2,1)}, u32[]{:S(2)}) copy-start(bf16[256,512]{1,0:T(8,128)(2,1)} %param.16) | copy-start | bytes 786436
  86.5 24.6 %copy-start.13 = (bf16[256,512]{1,0:T(8,128)(2,1)S(1)}, bf16[256,512]{1,0:T(8,128)(2,1)}, u32[]{:S(2)}) copy-start(bf16[256,512]{1,0:T(8,128)(2,1)} %copy-done.12) | copy-start | bytes 786436
  100.3 11.6 %copy-start.11 = (bf16[256,512]{1,0:T(8,128)(2,1)S(1)}, bf16[256,512]{1,0:T(8,128)(2,1)}, u32[]{:S(2)}) copy-start(bf16[256,512]{1,0:T(8,128)(2,1)} %copy-done.10) | copy-start | bytes 786436
  100.3 12.3 %copy-start.9 = (bf16[256,512]{1,0:T(8,128)(2,1)S(1)}, bf16[256,512]{1,0:T(8,128)(2,1)}, u32[]{:S(2)}) copy-start(bf16[256,512]{1,0:T(8,128)(2,1)} %copy-done.8) | copy-start | bytes 786436
  100.4 16.6 %copy-start.18 = (bf16[4096]{0:T(1024)(128)(2,1)S(1)}, bf16[4096]{0:T(1024)(128)(2,1)}, u32[]{:S(2)}) copy-start(bf16[4096]{0:T(1024)(128)(2,1)} %param.17) | copy-start | bytes 24580
  105.3 15.1 %collective-permute-start.10 = (bf16[64,4096]{1,0:T(8,128)(2,1)}, bf16[64,4096]{1,0:T(8,128)(2,1)S(1)}, u32[]{:S(2)}, u32[]{:S(2)}) collective-permute-start(bf16[64,4096]{1,0:T(8,128)(2,1)} %slice.63), channel_id=1, source_target_pairs={{0,32},{16,48},{32,64},{48,80},{64,96},{80,112},{96,0},{112,16},{1... | collective-permute-start | bytes 1572872 | tf_op jit(solution)/shard_map/ppermute | solution.py:26
  107.1 15.9 %collective-permute-start.11 = (bf16[64,4096]{1,0:T(8,128)(2,1)}, bf16[64,4096]{1,0:T(8,128)(2,1)S(1)}, u32[]{:S(2)}, u32[]{:S(2)}) collective-permute-start(bf16[64,4096]{1,0:T(8,128)(2,1)} %slice.64), channel_id=1, source_target_pairs={{0,96},{16,112},{32,0},{48,16},{64,32},{80,48},{96,64},{112,80},{1... | collective-permute-start | bytes 1572872 | tf_op jit(solution)/shard_map/ppermute | solution.py:26
  113.4 35.5 %collective-permute-start.16 = (bf16[256,2048]{1,0:T(8,128)(2,1)}, bf16[256,2048]{1,0:T(8,128)(2,1)}, u32[]{:S(2)}, u32[]{:S(2)}) collective-permute-start(bf16[256,2048]{1,0:T(8,128)(2,1)} %constant_dynamic-update-slice_fusion.3.refs_0_), channel_id=1, source_target_pairs={{0,16},{16,0},{32,48},{48,32},{64,80},{80,64},{96,112},{112,96},{1... | collective-permute-start | bytes 3145736 | tf_op jit(solution)/shard_map/ppermute | solution.py:30
  117.0 48.9 %collective-permute-start.21 = (bf16[128,4096]{1,0:T(8,128)(2,1)}, bf16[128,4096]{1,0:T(8,128)(2,1)S(1)}, u32[]{:S(2)}, u32[]{:S(2)}) collective-permute-start(bf16[128,4096]{1,0:T(8,128)(2,1)} %collective-permute-done.15.refs_0_), channel_id=1, source_target_pairs={{0,32},{16,48},{32,64},{48,80},{64,96},{80,112},{96,0},{112,16},{1... | collective-permute-start | bytes 3145736 | tf_op jit(solution)/shard_map/ppermute | solution.py:26
  117.1 48.8 %collective-permute-start.18 = (bf16[128,4096]{1,0:T(8,128)(2,1)}, bf16[128,4096]{1,0:T(8,128)(2,1)S(1)}, u32[]{:S(2)}, u32[]{:S(2)}) collective-permute-start(bf16[128,4096]{1,0:T(8,128)(2,1)} %collective-permute-done.15.refs_0_), channel_id=1, source_target_pairs={{0,96},{16,112},{32,0},{48,16},{64,32},{80,48},{96,64},{112,80},{1... | collective-permute-start | bytes 3145736 | tf_op jit(solution)/shard_map/ppermute | solution.py:26
  126.5 22.5 %copy-start.1 = (bf16[4096,512]{1,0:T(8,128)(2,1)S(1)}, bf16[4096,512]{1,0:T(8,128)(2,1)}, u32[]{:S(2)}) copy-start(bf16[4096,512]{1,0:T(8,128)(2,1)} %w_ref.1) | copy-start | bytes 12582916
  133.0 5.6 %collective-permute-start.12 = (bf16[256,128]{1,0:T(8,128)(2,1)S(1)}, bf16[256,128]{1,0:T(8,128)(2,1)S(1)}, u32[]{:S(2)}, u32[]{:S(2)}) collective-permute-start(bf16[256,128]{1,0:T(8,128)(2,1)S(1)} %get-tuple-element.81), channel_id=1, source_target_pairs={{0,12},{1,13},{2,14},{3,15},{4,0},{5,1},{6,2},{7,3},{8,4},{9,5},{1... | collective-permute-start | bytes 196616 | tf_op jit(solution)/shard_map/ppermute | solution.py:35
  134.0 14.6 %collective-permute-start.14 = (bf16[256,128]{1,0:T(8,128)(2,1)S(1)}, bf16[256,128]{1,0:T(8,128)(2,1)S(1)}, u32[]{:S(2)}, u32[]{:S(2)}) collective-permute-start(bf16[256,128]{1,0:T(8,128)(2,1)S(1)} %get-tuple-element.79), channel_id=1, source_target_pairs={{0,4},{1,5},{2,6},{3,7},{4,8},{5,9},{6,10},{7,11},{8,12},{9,13},{1... | collective-permute-start | bytes 196616 | tf_op jit(solution)/shard_map/ppermute | solution.py:35
  138.5 5.8 %collective-permute-start.13 = (bf16[256,128]{1,0:T(8,128)(2,1)S(1)}, bf16[256,128]{1,0:T(8,128)(2,1)S(1)}, u32[]{:S(2)}, u32[]{:S(2)}) collective-permute-start(bf16[256,128]{1,0:T(8,128)(2,1)S(1)} %get-tuple-element.80), channel_id=1, source_target_pairs={{0,8},{1,9},{2,10},{3,11},{4,12},{5,13},{6,14},{7,15},{8,0},{9,1},... | collective-permute-start | bytes 196616 | tf_op jit(solution)/shard_map/ppermute | solution.py:35
  144.3 16.0 %collective-permute-start.19 = (bf16[64,4096]{1,0:T(8,128)(2,1)S(1)}, bf16[64,4096]{1,0:T(8,128)(2,1)S(1)}, u32[]{:S(2)}, u32[]{:S(2)}) collective-permute-start(bf16[64,4096]{1,0:T(8,128)(2,1)S(1)} %collective-permute-done.10.refs_2_), channel_id=1, source_target_pairs={{0,16},{16,0},{32,48},{48,32},{64,80},{80,64},{96,112},{112,96},{1... | collective-permute-start | bytes 1572872 | tf_op jit(solution)/shard_map/ppermute | solution.py:30
  148.6 17.4 %collective-permute-start.20 = (bf16[64,4096]{1,0:T(8,128)(2,1)S(1)}, bf16[64,4096]{1,0:T(8,128)(2,1)S(1)}, u32[]{:S(2)}, u32[]{:S(2)}) collective-permute-start(bf16[64,4096]{1,0:T(8,128)(2,1)S(1)} %collective-permute-done.11.refs_3_), channel_id=1, source_target_pairs={{0,16},{16,0},{32,48},{48,32},{64,80},{80,64},{96,112},{112,96},{1... | collective-permute-start | bytes 1572872 | tf_op jit(solution)/shard_map/ppermute | solution.py:30
  148.9 6.9 %copy-start.3 = (bf16[512,4096]{1,0:T(8,128)(2,1)S(1)}, bf16[512,4096]{1,0:T(8,128)(2,1)}, u32[]{:S(2)}) copy-start(bf16[512,4096]{1,0:T(8,128)(2,1)} %param.22) | copy-start | bytes 12582916
  148.9 17.0 %slice-start = ((s8[8388608]{0:T(1024)(128)(4,1)}), s8[4194304]{0:T(1024)(128)(4,1)S(1)}, s32[]{:S(2)}) async-start(s8[8388608]{0:T(1024)(128)(4,1)} %bitcast.32), calls=%async_computation.2 | async-start | bytes 8388608
  153.6 12.3 %slice-start.1 = ((s8[8388608]{0:T(1024)(128)(4,1)}), s8[4194304]{0:T(1024)(128)(4,1)S(1)}, s32[]{:S(2)}) async-start(s8[8388608]{0:T(1024)(128)(4,1)} %bitcast.32), calls=%async_computation.3 | async-start | bytes 8388608
  153.6 12.3 %copy-start.2 = (s32[4]{0:T(128)S(1)}, s32[4]{0:T(128)}, u32[]{:S(2)}) copy-start(s32[4]{0:T(128)} %counts.1) | copy-start | bytes 52
  153.6 5.7 %collective-permute-start.17 = (bf16[64,512]{1,0:T(8,128)(2,1)S(1)}, bf16[64,512]{1,0:T(8,128)(2,1)S(1)}, u32[]{:S(2)}, u32[]{:S(2)}) collective-permute-start(bf16[64,512]{1,0:T(8,128)(2,1)S(1)} %slice.87), channel_id=1, source_target_pairs={{1,0},{2,1},{3,2},{4,3},{5,4},{6,5},{7,6},{8,7},{9,8},{10,9},{11,1... | collective-permute-start | bytes 196616 | tf_op jit(solution)/shard_map/ppermute | solution.py:45
  174.8 6.5 %collective-permute-start.22 = (bf16[64,512]{1,0:T(8,128)(2,1)S(1)}, bf16[64,512]{1,0:T(8,128)(2,1)S(1)}, u32[]{:S(2)}, u32[]{:S(2)}) collective-permute-start(bf16[64,512]{1,0:T(8,128)(2,1)S(1)} %get-tuple-element.55), channel_id=1, source_target_pairs={{0,1},{1,2},{2,3},{3,4},{4,5},{5,6},{6,7},{7,8},{8,9},{9,10},{10,1... | collective-permute-start | bytes 196616 | tf_op jit(solution)/shard_map/ppermute | solution.py:45
  188.8 9.9 %collective-permute-start.23 = (bf16[128,1024]{1,0:T(8,128)(2,1)}, bf16[128,1024]{1,0:T(8,128)(2,1)}, u32[]{:S(2)}, u32[]{:S(2)}) collective-permute-start(bf16[128,1024]{1,0:T(8,128)(2,1)} %get-tuple-element.65), channel_id=1, source_target_pairs={{0,32},{16,48},{32,64},{48,80},{64,96},{80,112},{96,0},{112,16},{1... | collective-permute-start | bytes 786440 | tf_op jit(solution)/shard_map/ppermute | solution.py:26
  188.8 15.2 %collective-permute-start.25 = (bf16[128,1024]{1,0:T(8,128)(2,1)}, bf16[128,1024]{1,0:T(8,128)(2,1)}, u32[]{:S(2)}, u32[]{:S(2)}) collective-permute-start(bf16[128,1024]{1,0:T(8,128)(2,1)} %get-tuple-element.66), channel_id=1, source_target_pairs={{0,64},{16,80},{32,96},{48,112},{64,0},{80,16},{96,32},{112,48},{1... | collective-permute-start | bytes 786440 | tf_op jit(solution)/shard_map/ppermute | solution.py:26
  193.6 10.4 %collective-permute-start.24 = (bf16[128,1024]{1,0:T(8,128)(2,1)S(1)}, bf16[128,1024]{1,0:T(8,128)(2,1)}, u32[]{:S(2)}, u32[]{:S(2)}) collective-permute-start(bf16[128,1024]{1,0:T(8,128)(2,1)S(1)} %get-tuple-element.67), channel_id=1, source_target_pairs={{0,96},{16,112},{32,0},{48,16},{64,32},{80,48},{96,64},{112,80},{1... | collective-permute-start | bytes 786440 | tf_op jit(solution)/shard_map/ppermute | solution.py:26
  193.7 15.4 %collective-permute-start.27 = (bf16[128,2048]{1,0:T(8,128)(2,1)S(1)}, bf16[128,2048]{1,0:T(8,128)(2,1)S(1)}, u32[]{:S(2)}, u32[]{:S(2)}) collective-permute-start(bf16[128,2048]{1,0:T(8,128)(2,1)S(1)} %pad_maximum_fusion.2), channel_id=1, source_target_pairs={{0,16},{16,0},{32,48},{48,32},{64,80},{80,64},{96,112},{112,96},{1... | collective-permute-start | bytes 1572872 | tf_op jit(solution)/shard_map/ppermute | solution.py:30
  205.5 7.7 %collective-permute-start.26 = (bf16[128,512]{1,0:T(8,128)(2,1)S(1)}, bf16[128,512]{1,0:T(8,128)(2,1)S(1)}, u32[]{:S(2)}, u32[]{:S(2)}) collective-permute-start(bf16[128,512]{1,0:T(8,128)(2,1)S(1)} %dynamic-slice_convert_fusion.10), channel_id=1, source_target_pairs={{0,16},{16,0},{32,48},{48,32},{64,80},{80,64},{96,112},{112,96},{1... | collective-permute-start | bytes 393224 | tf_op jit(solution)/shard_map/ppermute | solution.py:30
  209.1 9.9 %copy-start.7 = (bf16[256,512]{1,0:T(8,128)(2,1)S(1)}, bf16[256,512]{1,0:T(8,128)(2,1)}, u32[]{:S(2)}) copy-start(bf16[256,512]{1,0:T(8,128)(2,1)} %param.16) | copy-start | bytes 786436
  209.3 7.1 %collective-permute-start.28 = (bf16[128,512]{1,0:T(8,128)(2,1)S(1)}, bf16[128,512]{1,0:T(8,128)(2,1)S(1)}, u32[]{:S(2)}, u32[]{:S(2)}) collective-permute-start(bf16[128,512]{1,0:T(8,128)(2,1)S(1)} %get-tuple-element.76), channel_id=1, source_target_pairs={{0,32},{16,48},{32,64},{48,80},{64,96},{80,112},{96,0},{112,16},{1... | collective-permute-start | bytes 393224 | tf_op jit(solution)/shard_map/ppermute | solution.py:26
  209.9 8.9 %collective-permute-start.30 = (bf16[128,512]{1,0:T(8,128)(2,1)S(1)}, bf16[128,512]{1,0:T(8,128)(2,1)S(1)}, u32[]{:S(2)}, u32[]{:S(2)}) collective-permute-start(bf16[128,512]{1,0:T(8,128)(2,1)S(1)} %get-tuple-element.77), channel_id=1, source_target_pairs={{0,64},{16,80},{32,96},{48,112},{64,0},{80,16},{96,32},{112,48},{1... | collective-permute-start | bytes 393224 | tf_op jit(solution)/shard_map/ppermute | solution.py:26
  212.9 6.0 %collective-permute-start.29 = (bf16[128,512]{1,0:T(8,128)(2,1)S(1)}, bf16[128,512]{1,0:T(8,128)(2,1)S(1)}, u32[]{:S(2)}, u32[]{:S(2)}) collective-permute-start(bf16[128,512]{1,0:T(8,128)(2,1)S(1)} %get-tuple-element.78), channel_id=1, source_target_pairs={{0,96},{16,112},{32,0},{48,16},{64,32},{80,48},{96,64},{112,80},{1... | collective-permute-start | bytes 393224 | tf_op jit(solution)/shard_map/ppermute | solution.py:26
  (6 other events, 15.5 us)
where the time goes:
time: 221 us; the launch traced here: 220 us
  starting transfers between devices  75 us (34%)
  waiting for transfers between devices  53.6 us (24%)
  local copies, waits for them, and re-layouts  40.1 us (18%)
  Pallas kernels  33.7 us (15%)
  other arithmetic  8.38 us (4%)
  matrix products  8.17 us (4%)
    ppermute x15, starting transfers between devices, along_y(): return lax.ppermute(block, 'enc', route)  24.4 us
    ppermute x15, waiting for transfers between devices, along_y(): return lax.ppermute(block, 'enc', route)  22 us
    unnamed x47, local copies, waits for them, and re-layouts  21.9 us
    ppermute x6, starting transfers between devices, swap_z_hi(): return lax.ppermute(block, 'enc', [(e, e ^ 1) for e in range(2 * NY)])  18.5 us
    pallas_call x1, Pallas kernels, causal_attention(): pl.pallas_call(causal_kernel, grid_spec=pltpu.PrefetchScalarGridSpec(num_...  13.8 us
    all_to_all x1, waiting for transfers between devices, answer(): lax.all_to_all(found, ('enc', 'ctx'), split_axis=0, concat_axis=0, tiled=...  11.4 us
    all_to_all x1, starting transfers between devices, per_device(): lax.all_to_all(request, ('enc', 'ctx'), split_axis=0, concat_axis=0, tile...  10.8 us
    pallas_call x1, Pallas kernels, attend_spans(): pl.pallas_call(span_kernel, in_specs=[pl.BlockSpec(memory_space=pltpu.SME...  8.88 us
  transfers between devices with their start and end apart: 33, of which 16 were waited for; matrix products, arithmetic and copies ran while one was open for 16% of the time, Pallas kernels for 11%

commit v1 on v0

--- a/solution.py
+++ b/solution.py
@@ -19,6 +19,7 @@
 BF = jnp.bfloat16
 F32 = jnp.float32
 SHORT = pl.CostEstimate(flops=1024, bytes_accessed=1024, transcendentals=0)
+LONG = pl.CostEstimate(flops=1 << 36, bytes_accessed=1 << 28, transcendentals=0)
 
 
 def along_y(block, step):
@@ -49,16 +50,16 @@
     return jax.tree.map(lambda value: lax.optimization_barrier((value, *done))[0], values)
 
 
-def gather_rows(block, done):
+def gather_rows(block, fellow, done):
     half = block.shape[0] // 2
     above, below = along_y(block, -1), along_y(block, 1)
-    side = swap_z_hi(block)
+    swapped = swap_z_hi(jnp.concatenate([block, fellow], axis=0))
+    side = swapped[: 2 * half]
     onward = after((below, above), done)
     far = along_y(onward[0][:half], 1), along_y(onward[1][half:], -1)
-    side_onward = after(side, done)
-    side_above, side_below = along_y(side_onward, -1), along_y(side_onward, 1)
-    side_far = swap_z_hi(far[0]), swap_z_hi(far[1])
-    return (block, above, *far, below), (side, side_above, *side_far, side_below)
+    far = jnp.concatenate(far, axis=0)
+    side_above, side_below = along_y(side, -1), along_y(side, 1)
+    return (block, above, far, below), (side, side_above, swap_z_hi(far), side_below), swapped[2 * half :]
 
 
 def rms_norm(rows, gain):
@@ -152,8 +153,8 @@
             ],
         ),
         out_shape=jax.ShapeDtypeStruct(queries.shape, BF),
-        compiler_params=pltpu.CompilerParams(vmem_limit_bytes=32 * 1024 * 1024),
-        cost_estimate=SHORT,
+        compiler_params=pltpu.CompilerParams(vmem_limit_bytes=14 * 1024 * 1024),
+        cost_estimate=LONG,
     )(q_blocks, k_blocks, queries, near, side, far)
 
 
@@ -202,8 +203,14 @@
     for copy in copies:
         copy.start()
 
+    near_ref, far_ref = piece_refs
+
     def block(k):
-        return piece_refs[k // NY][:, k % NY * width : (k % NY + 1) * width].astype(F32)
+        col = k % NY * width
+        if k < NY:
+            return near_ref[:, col : col + width].astype(F32)
+        low = NY * width + col
+        return jnp.concatenate([far_ref[:, col : col + width], far_ref[:, low : low + width]], axis=0).astype(F32)
 
     square = jnp.zeros((out_ref.shape[0], 1), F32)
     for k in range(count):
@@ -230,7 +237,7 @@
             pltpu.VMEM((2 * NY, width, weight.shape[1]), BF),
             pltpu.SemaphoreType.DMA((2 * NY,)),
         ],
-        compiler_params=pltpu.CompilerParams(vmem_limit_bytes=24 * 1024 * 1024),
+        compiler_params=pltpu.CompilerParams(vmem_limit_bytes=14 * 1024 * 1024),
         cost_estimate=SHORT,
     )(order, gain.astype(F32).reshape(2 * NY, width), weight, *pieces)
 
@@ -324,8 +331,8 @@
         out_specs=pl.BlockSpec(memory_space=pltpu.VMEM),
         out_shape=jax.ShapeDtypeStruct((key_rows, weight.shape[1]), BF),
         scratch_shapes=rows_scratch(normed, weight),
-        compiler_params=pltpu.CompilerParams(vmem_limit_bytes=28 * 1024 * 1024),
-        cost_estimate=SHORT,
+        compiler_params=pltpu.CompilerParams(vmem_limit_bytes=20 * 1024 * 1024),
+        cost_estimate=LONG,
     )(weight, *normed)
 
 
@@ -339,30 +346,33 @@
         out_specs=(vmem, vmem),
         out_shape=(jax.ShapeDtypeStruct((rows, width), BF), jax.ShapeDtypeStruct((SPAN, width), BF)),
         scratch_shapes=rows_scratch(normed, weight),
-        compiler_params=pltpu.CompilerParams(vmem_limit_bytes=32 * 1024 * 1024),
+        compiler_params=pltpu.CompilerParams(vmem_limit_bytes=20 * 1024 * 1024),
         cost_estimate=SHORT,
     )(counts, queries, kv, weight, *normed)
 
 
-def scatter_sum(projected):
-    rows, width = projected.shape
+def split_z(rows):
+    z = lax.axis_index("enc") % 2
+    part = rows.shape[1] // (2 * NY)
+
+    def take(zz):
+        parts = [lax.dynamic_slice_in_dim(rows, (yy * 2 + zz) * part, part, 1) for yy in range(NY)]
+        return jnp.concatenate(parts, axis=1)
+
+    return take(z), take(1 - z).astype(BF)
+
+
+def scatter_sum(top, low, low_far):
     enc = lax.axis_index("enc")
     y, z = enc // 2, enc % 2
-    part = width // (2 * NY)
-    half = rows // 2
-    top, low = projected[:half], projected[half:]
-
-    def take(a, yy, zz):
-        return lax.dynamic_slice_in_dim(a, (yy * 2 + zz) * part, part, 1)
+    part = low_far.shape[1] // NY
 
     def pair(a, k):
         return lax.dynamic_slice_in_dim(a, (y + k) % NY * 2 * part, 2 * part, 1)
 
-    low_far = jnp.concatenate([take(low, yy, 1 - z) for yy in range(NY)], axis=1)
-    low_near = jnp.concatenate([take(low, yy, z) for yy in range(NY)], axis=1)
-    low_got = swap_z_hi(low_far.astype(BF))
+    low_got = swap_z_hi(low_far)
     top_got = [along_y(pair(top, k).astype(BF), k) for k in (1, 3, 2)]
-    low_sum = low_near + low_got.astype(F32)
+    low_sum = low + low_got.astype(F32)
 
     def column(k):
         return lax.dynamic_slice_in_dim(low_sum, (y + k) % NY * part, part, 1)
@@ -413,13 +423,14 @@
     own_rows = after(own_rows, kv_weight, side, *hidden)
     near, side, hidden = after((near, side, hidden), own_rows)
     near_context = near_attention(dealt, near, side)
-    normed, side_normed = gather_rows(own_rows, near_context)
+    self_context = return_heads(near_context)
+    hidden = jnp.concatenate(hidden, axis=1)
+    folded = jnp.concatenate([hidden[: rows // 2], hidden[rows // 2 :]], axis=1)
+    normed, side_normed, far_hidden = gather_rows(own_rows, folded, self_context)
     kv = keys_values(kv_weight, normed)
-    self_context = return_heads(after(near_context, kv))
+    self_context = after(self_context, side_normed[2])
     self_projected = jnp.dot(self_context, self_out_weight, preferred_element_type=F32)
 
-    hidden = jnp.concatenate(after(hidden, near_context), axis=1)
-    far_hidden = swap_z_hi(after(hidden, side_normed[0]))
     turn = jnp.stack([(y + k) % NY for k in range(NY)]).astype(jnp.int32)
     hidden_order = jnp.concatenate([turn * 2 + z, turn * 2 + 1 - z])
     cross_queries = project_queries([hidden, far_hidden], query_gain, cross_query_weight, hidden_order)
@@ -430,10 +441,14 @@
     queries = after(queries, kv, self_projected)
     context, tail = attend_spans(queries, counts, kv, kv_weight, side_normed)
     earlier = next_ctx(tail, 1)
-    cross_context = jnp.concatenate([earlier[1:], context[: rows - SPAN + 1]], axis=0)
-
-    projected = self_projected + jnp.dot(cross_context, cross_out_weight, preferred_element_type=F32)
-    return (hidden_in.astype(F32) + scatter_sum(projected)).astype(BF)
+    half = rows // 2
+    low = self_projected[half:] + jnp.dot(
+        context[half - SPAN + 1 : rows - SPAN + 1], cross_out_weight, preferred_element_type=F32
+    )
+    low, low_far = split_z(low)
+    cross_context = jnp.concatenate([earlier[1:], after(context, low_far)[: half - SPAN + 1]], axis=0)
+    top = self_projected[:half] + jnp.dot(cross_context, cross_out_weight, preferred_element_type=F32)
+    return (hidden_in.astype(F32) + scatter_sum(top, low, low_far)).astype(BF)
 
 
 def solution(mesh):

time: 221 us -> 212 us (0.959)
  starting transfers between devices: 75 us -> 62.9 us
  waiting for transfers between devices: 53.6 us -> 64.9 us
  matrix products: 8.17 us -> 2.7 us
  Pallas kernels: 33.7 us -> 30.9 us
    ppermute x15, waiting for transfers between devices: 22 us -> 34.5 us  [along_y(): return lax.ppermute(block, 'enc', route)]
    ppermute x6 -> x4, starting transfers between devices: 18.5 us -> 10.8 us  [swap_z_hi(): return lax.ppermute(block, 'enc', [(e, e ^ 1) for e in range(2 * NY)])]
    dot_general x1, matrix products: 4.77 us -> 0.73 us  [per_device(): jnp.dot(cross_context, cross_out_weight, preferred_element_type=F32)]
    ppermute x15, starting transfers between devices: 24.4 us -> 20.5 us  [along_y(): return lax.ppermute(block, 'enc', route)]
    ppermute x6 -> x4, waiting for transfers between devices: 6.6 us -> 3.94 us  [swap_z_hi(): return lax.ppermute(block, 'enc', [(e, e ^ 1) for e in range(2 * NY)])]
    unnamed x47 -> x40, local copies, waits for them, and re-layouts: 21.9 us -> 22.6 us
  transfers between devices with their start and end apart: 33 -> 31, of which waited for: 16 -> 15; matrix products, arithmetic and copies ran while one was open for 16% -> 16% of each run, Pallas kernels for 11% -> 11%
where the time goes in v1:
time: 212 us; the launch traced here: 211 us
  waiting for transfers between devices  64.9 us (31%)
  starting transfers between devices  62.9 us (30%)
  local copies, waits for them, and re-layouts  39.9 us (19%)
  Pallas kernels  30.9 us (15%)
  other arithmetic  8.71 us (4%)
  matrix products  2.7 us (1%)
    ppermute x15, waiting for transfers between devices, along_y(): return lax.ppermute(block, 'enc', route)  34.5 us
    unnamed x40, local copies, waits for them, and re-layouts  22.6 us
    ppermute x15, starting transfers between devices, along_y(): return lax.ppermute(block, 'enc', route)  20.5 us
    pallas_call x1, Pallas kernels, causal_attention(): pl.pallas_call(causal_kernel, grid_spec=pltpu.PrefetchScalarGridSpec(num_...  12.5 us
    all_to_all x1, waiting for transfers between devices, answer(): lax.all_to_all(found, ('enc', 'ctx'), split_axis=0, concat_axis=0, tiled=...  12.2 us
    ppermute x4, starting transfers between devices, swap_z_hi(): return lax.ppermute(block, 'enc', [(e, e ^ 1) for e in range(2 * NY)])  10.8 us
    all_to_all x1, starting transfers between devices, per_device(): lax.all_to_all(request, ('enc', 'ctx'), split_axis=0, concat_axis=0, tile...  10.8 us
    pallas_call x1, Pallas kernels, attend_spans(): pl.pallas_call(span_kernel, in_specs=[pl.BlockSpec(memory_space=pltpu.SME...  8.48 us
  transfers between devices with their start and end apart: 31, of which 15 were waited for; matrix products, arithmetic and copies ran while one was open for 16% of the time, Pallas kernels for 11%

profile of v1, /device:TPU:6, one launch (start us, length us, event | category | flops | bytes accessed | tf_op | source)
XLA Modules:
  0.0 210.8 jit_solution(1696444851306527136)
XLA Ops:
  2.1 1.1 constant_dynamic-slice_fusion.4
  3.8 2.6 %collective-permute-start.1 = (bf16[256,384]{1,0:T(8,128)(2,1)S(1)}, bf16[256,384]{1,0:T(8,128)(2,1)S(1)}, u32[]{:S(2)}, u32[]{:S(2)}) collective-permute-start(bf16[256,384]{1,0:T(8,128)(2,1)S(1)} %pad_maximum_fusion.6), channel_id=1, source_target_pairs={{0,8},{1,9},{2,10},{3,11},{4,12},{5,13},{6,14},{7,15},{8,0},{9,1},... | collective-permute-start | bytes 589832 | tf_op jit(solution)/shard_map/ppermute | solution.py:36
  7.2 10.8 %all-to-all-start = ((s32[128,1,2]{2,1,0:T(1,128)}), s32[128,1,2]{2,1,0:T(1,128)S(1)}, u32[]{:S(2)}, u32[]{:S(2)}) async-start(s32[128,1,2]{2,1,0:T(1,128)} %bitcast.4), calls=%async_computation | async-start | bytes 131072 | tf_op jit(solution)/shard_map/all_to_all | solution.py:413
  18.0 5.4 %copy.16 = bf16[64,8,32,128]{3,2,1,0:T(8,128)(2,1)} copy(bf16[64,8,32,128]{3,1,2,0:T(8,128)(2,1)} %bitcast.37) | data formatting | bytes 8388608
  23.4 2.9 %all-to-all-done = s32[128,1,2]{2,1,0:T(1,128)S(1)} async-done(((s32[128,1,2]{2,1,0:T(1,128)}), s32[128,1,2]{2,1,0:T(1,128)S(1)}, u32[]{:S(2)}, u32[]{:S(2)}) %all-to-all-start) | async-done | bytes 1056 | tf_op jit(solution)/shard_map/all_to_all | solution.py:413
  28.0 4.4 %gather_fusion = bf16[256,32,128]{2,1,0:T(8,128)(2,1)} fusion(bf16[512,32,128]{2,1,0:T(8,128)(2,1)} %bitcast.34, s32[1024]{0:T(1024)S(1)} %pad_clamp_fusion.1), kind=kCustom, calls=%fused_computation | custom fusion | bytes 4195328 | tf_op jit(solution)/shard_map/gather | solution.py:86
  32.4 7.3 %all-to-all-start.1 = ((bf16[256,32,128]{2,1,0:T(8,128)(2,1)}), bf16[256,32,128]{2,1,0:T(8,128)(2,1)}, u32[]{:S(2)}, u32[]{:S(2)}) async-start(bf16[256,32,128]{2,1,0:T(8,128)(2,1)} %gather_fusion), calls=%async_computation.1 | async-start | bytes 4194304 | tf_op jit(solution)/shard_map/all_to_all | solution.py:90
  40.1 2.8 %collective-permute-start.4 = (bf16[256,512]{1,0:T(8,128)(2,1)S(1)}, bf16[256,512]{1,0:T(8,128)(2,1)S(1)}, u32[]{:S(2)}, u32[]{:S(2)}) collective-permute-start(bf16[256,512]{1,0:T(8,128)(2,1)S(1)} %copy-done.8), channel_id=1, source_target_pairs={{0,96},{16,112},{32,0},{48,16},{64,32},{80,48},{96,64},{112,80},{1... | collective-permute-start | bytes 786440 | tf_op jit(solution)/shard_map/ppermute | solution.py:27
  44.6 9.4 %copy.18 = bf16[512,8,2,512]{3,1,2,0:T(8,128)(2,1)} copy(bf16[512,8,2,512]{3,2,1,0:T(2,128)(2,1)} %bitcast.36) | data formatting | bytes 16777216
  54.0 1.7 collective-permute-start.3
  55.8 12.2 %all-to-all-done.1 = bf16[256,32,128]{2,1,0:T(8,128)(2,1)} async-done(((bf16[256,32,128]{2,1,0:T(8,128)(2,1)}), bf16[256,32,128]{2,1,0:T(8,128)(2,1)}, u32[]{:S(2)}, u32[]{:S(2)}) %all-to-all-start.1) | async-done | bytes 2097184 | tf_op jit(solution)/shard_map/all_to_all | solution.py:90
  68.0 2.3 %gather_fusion.1 = bf16[128,32,128]{2,1,0:T(8,128)(2,1)S(1)} fusion(bf16[256,32,128]{2,1,0:T(8,128)(2,1)} %all-to-all-done.1, s32[1024]{0:T(1024)S(1)} %pad_clamp_fusion), kind=kCustom, calls=%fused_computation.1 | custom fusion | bytes 2097664 | tf_op jit(solution)/shard_map/gather | solution.py:91
  71.7 1.8 fusion.1.refs_0_
  73.6 2.4 %collective-permute-done.6 = bf16[256,512]{1,0:T(8,128)(2,1)S(1)} collective-permute-done((bf16[256,512]{1,0:T(8,128)(2,1)S(1)}, bf16[256,512]{1,0:T(8,128)(2,1)S(1)}, u32[]{:S(2)}, u32[]{:S(2)}) %collective-permute-start.6) | collective-permute-done | bytes 262176 | tf_op jit(solution)/shard_map/ppermute | solution.py:27
  76.0 1.9 collective-permute-start.13
  81.4 1.5 maximum_maximum_fusion
  82.8 3.7 %collective-permute-start.16 = (bf16[256,4096]{1,0:T(8,128)(2,1)}, bf16[256,4096]{1,0:T(8,128)(2,1)}, u32[]{:S(2)}, u32[]{:S(2)}) collective-permute-start(bf16[256,4096]{1,0:T(8,128)(2,1)} %maximum_maximum_fusion), channel_id=1, source_target_pairs={{0,16},{16,0},{32,48},{48,32},{64,80},{80,64},{96,112},{112,96},{1... | collective-permute-start | bytes 6291464 | tf_op jit(solution)/shard_map/ppermute | solution.py:31
  86.5 12.5 %shard_map.127 = bf16[1024,128]{1,0:T(8,128)(2,1)S(1)} custom-call(s32[4]{0:T(128)S(1)} %get-tuple-element.89.q_blocks, s32[16]{0:T(128)S(1)} %pad_add_fusion.k_blocks, bf16[1024,128]{1,0:T(8,128)(2,1)S(1)} %pad_maximum_fusion.3.q_ref, bf16[1024,256]{1,0:T(8,128)(2,1)S(1)} %pad_maximum_fusion.1.near_ref, ...), custom_call_target="tpu_custom_call" | custom-call | flops 68719476736 | bytes 268435456 | tf_op jit(solution)/shard_map/pallas_call | solution.py:137
  99.9 1.4 collective-permute-start.9
  101.3 3.4 %collective-permute-done.8 = bf16[256,128]{1,0:T(8,128)(2,1)S(1)} collective-permute-done((bf16[256,128]{1,0:T(8,128)(2,1)S(1)}, bf16[256,128]{1,0:T(8,128)(2,1)S(1)}, u32[]{:S(2)}, u32[]{:S(2)}) %collective-permute-start.8) | collective-permute-done | bytes 65568 | tf_op jit(solution)/shard_map/ppermute | solution.py:36
  104.8 1.1 collective-permute-done.9
  105.9 3.1 %collective-permute-done.10 = bf16[256,128]{1,0:T(8,128)(2,1)S(1)} collective-permute-done((bf16[256,128]{1,0:T(8,128)(2,1)S(1)}, bf16[256,128]{1,0:T(8,128)(2,1)S(1)}, u32[]{:S(2)}, u32[]{:S(2)}) %collective-permute-start.10) | collective-permute-done | bytes 65568 | tf_op jit(solution)/shard_map/ppermute | solution.py:36
  113.0 2.4 %collective-permute-start.14 = (bf16[64,4096]{1,0:T(8,128)(2,1)S(1)}, bf16[64,4096]{1,0:T(8,128)(2,1)S(1)}, u32[]{:S(2)}, u32[]{:S(2)}) collective-permute-start(bf16[64,4096]{1,0:T(8,128)(2,1)S(1)} %slice.83), channel_id=1, source_target_pairs={{0,96},{16,112},{32,0},{48,16},{64,32},{80,48},{96,64},{112,80},{1... | collective-permute-start | bytes 1572872 | tf_op jit(solution)/shard_map/ppermute | solution.py:27
  115.4 11.2 %collective-permute-done.12 = bf16[64,4096]{1,0:T(8,128)(2,1)S(1)} collective-permute-done((bf16[64,4096]{1,0:T(8,128)(2,1)}, bf16[64,4096]{1,0:T(8,128)(2,1)S(1)}, u32[]{:S(2)}, u32[]{:S(2)}) %collective-permute-start.12) | collective-permute-done | bytes 524320 | tf_op jit(solution)/shard_map/ppermute | solution.py:27
  127.6 1.8 collective-permute-start.15
  129.4 3.9 %collective-permute-done.16 = bf16[256,4096]{1,0:T(8,128)(2,1)} collective-permute-done((bf16[256,4096]{1,0:T(8,128)(2,1)}, bf16[256,4096]{1,0:T(8,128)(2,1)}, u32[]{:S(2)}, u32[]{:S(2)}) %collective-permute-start.16) | collective-permute-done | bytes 2097184 | tf_op jit(solution)/shard_map/ppermute | solution.py:31
  133.3 1.7 fusion.16
  135.1 2.5 %collective-permute-start.18 = (bf16[128,4096]{1,0:T(8,128)(2,1)S(1)}, bf16[128,4096]{1,0:T(8,128)(2,1)S(1)}, u32[]{:S(2)}, u32[]{:S(2)}) collective-permute-start(bf16[128,4096]{1,0:T(8,128)(2,1)S(1)} %get-tuple-element.64.refs_0_), channel_id=1, source_target_pairs={{0,96},{16,112},{32,0},{48,16},{64,32},{80,48},{96,64},{112,80},{1... | collective-permute-start | bytes 3145736 | tf_op jit(solution)/shard_map/ppermute | solution.py:27
  137.6 3.4 %shard_map.128 = bf16[256,512]{1,0:T(8,128)(2,1)S(1)} custom-call(s32[8]{0:T(128)S(1)} %pad_add_fusion.1.order, f32[8,512]{1,0:T(8,128)S(1)} %reshape.199.gain_ref, bf16[4096,512]{1,0:T(8,128)(2,1)S(1)} %copy-done.1, bf16[256,2048]{1,0:T(8,128)(2,1)S(1)} %constant_dynamic-update-slice_fusion.2.refs_0_, bf16[128,4096]{1,0:T(8,128)(2,1)S(1)} %get-tuple-element.65.refs_1_), custom_call_target="tpu_custom_call" | custom-call | flops 1024 | bytes 1024 | tf_op jit(solution)/shard_map/pallas_call | solution.py:231
  141.0 4.4 %collective-permute-start.17 = (bf16[64,512]{1,0:T(8,128)(2,1)S(1)}, bf16[64,512]{1,0:T(8,128)(2,1)S(1)}, u32[]{:S(2)}, u32[]{:S(2)}) collective-permute-start(bf16[64,512]{1,0:T(8,128)(2,1)S(1)} %slice.115), channel_id=1, source_target_pairs={{1,0},{2,1},{3,2},{4,3},{5,4},{6,5},{7,6},{8,7},{9,8},{10,9},{11,1... | collective-permute-start | bytes 196616 | tf_op jit(solution)/shard_map/ppermute | solution.py:46
  145.5 3.4 %copy-done = bf16[512,8,2,512]{3,1,2,0:T(8,128)(2,1)S(1)} copy-done((bf16[512,8,2,512]{3,1,2,0:T(8,128)(2,1)S(1)}, bf16[512,8,2,512]{3,1,2,0:T(8,128)(2,1)}, u32[]{:S(2)}) %copy-start) | copy-done | bytes 8388632
  148.9 6.4 %shard_map.129.kv_ref = bf16[512,1024]{1,0:T(8,128)(2,1)S(1)} custom-call(bf16[4096,1024]{1,0:T(8,128)(2,1)S(1)} %bitcast.32, bf16[128,4096]{1,0:T(8,128)(2,1)S(1)} %fusion.1.refs_0_, bf16[128,4096]{1,0:T(8,128)(2,1)} %collective-permute-done.13.refs_1_, bf16[128,4096]{1,0:T(8,128)(2,1)S(1)} %constant_dynamic-update-slice_fusion.refs_2_, ...), custom_call_target="tpu_custom_call" | custom-call | flops 68719476736 | bytes 268435456 | tf_op jit(solution)/shard_map/pallas_call | solution.py:328
  155.5 1.3 fusion.19
  156.7 3.2 %collective-permute-done.18.refs_1_ = bf16[128,4096]{1,0:T(8,128)(2,1)S(1)} collective-permute-done((bf16[128,4096]{1,0:T(8,128)(2,1)S(1)}, bf16[128,4096]{1,0:T(8,128)(2,1)S(1)}, u32[]{:S(2)}, u32[]{:S(2)}) %collective-permute-start.18) | collective-permute-done | bytes 1048608 | tf_op jit(solution)/shard_map/ppermute | solution.py:27
  159.9 3.4 %collective-permute-done.19.refs_3_ = bf16[128,4096]{1,0:T(8,128)(2,1)S(1)} collective-permute-done((bf16[128,4096]{1,0:T(8,128)(2,1)S(1)}, bf16[128,4096]{1,0:T(8,128)(2,1)S(1)}, u32[]{:S(2)}, u32[]{:S(2)}) %collective-permute-start.19) | collective-permute-done | bytes 1048608 | tf_op jit(solution)/shard_map/ppermute | solution.py:27
  163.3 8.5 %shard_map.130 = (bf16[256,512]{1,0:T(8,128)(2,1)S(1)}, bf16[64,512]{1,0:T(8,128)(2,1)S(1)}) custom-call(s32[4]{0:T(128)S(1)} %copy-done.4, bf16[256,512]{1,0:T(8,128)(2,1)S(1)} %pad_maximum_fusion.4.q_ref, bf16[512,1024]{1,0:T(8,128)(2,1)S(1)} %shard_map.129.kv_ref, bf16[4096,1024]{1,0:T(8,128)(2,1)S(1)} %bitcast.33, ...), custom_call_target="tpu_custom_call" | custom-call | flops 1024 | bytes 1024 | tf_op jit(solution)/shard_map/pallas_call | solution.py:343
  171.8 1.9 collective-permute-start.20
  174.6 3.7 %collective-permute-done.20 = bf16[64,512]{1,0:T(8,128)(2,1)S(1)} collective-permute-done((bf16[64,512]{1,0:T(8,128)(2,1)S(1)}, bf16[64,512]{1,0:T(8,128)(2,1)S(1)}, u32[]{:S(2)}, u32[]{:S(2)}) %collective-permute-start.20) | collective-permute-done | bytes 65568 | tf_op jit(solution)/shard_map/ppermute | solution.py:46
  179.0 1.3 copy-done.7
  181.3 3.2 %collective-permute-start.22 = (bf16[128,1024]{1,0:T(8,128)(2,1)}, bf16[128,1024]{1,0:T(8,128)(2,1)}, u32[]{:S(2)}, u32[]{:S(2)}) collective-permute-start(bf16[128,1024]{1,0:T(8,128)(2,1)} %get-tuple-element.55), channel_id=1, source_target_pairs={{0,96},{16,112},{32,0},{48,16},{64,32},{80,48},{96,64},{112,80},{1... | collective-permute-start | bytes 786440 | tf_op jit(solution)/shard_map/ppermute | solution.py:27
  184.5 3.2 %collective-permute-start.25 = (bf16[128,2048]{1,0:T(8,128)(2,1)S(1)}, bf16[128,2048]{1,0:T(8,128)(2,1)S(1)}, u32[]{:S(2)}, u32[]{:S(2)}) collective-permute-start(bf16[128,2048]{1,0:T(8,128)(2,1)S(1)} %pad_maximum_fusion.2), channel_id=1, source_target_pairs={{0,16},{16,0},{32,48},{48,32},{64,80},{80,64},{96,112},{112,96},{1... | collective-permute-start | bytes 1572872 | tf_op jit(solution)/shard_map/ppermute | solution.py:31
  187.8 8.5 %collective-permute-done.21 = bf16[128,1024]{1,0:T(8,128)(2,1)} collective-permute-done((bf16[128,1024]{1,0:T(8,128)(2,1)}, bf16[128,1024]{1,0:T(8,128)(2,1)}, u32[]{:S(2)}, u32[]{:S(2)}) %collective-permute-start.21) | collective-permute-done | bytes 262176 | tf_op jit(solution)/shard_map/ppermute | solution.py:27
  196.4 1.4 convert_add_fusion
  197.8 2.1 %collective-permute-start.24 = (bf16[128,512]{1,0:T(8,128)(2,1)S(1)}, bf16[128,512]{1,0:T(8,128)(2,1)S(1)}, u32[]{:S(2)}, u32[]{:S(2)}) collective-permute-start(bf16[128,512]{1,0:T(8,128)(2,1)S(1)} %dynamic-slice_convert_fusion.6), channel_id=1, source_target_pairs={{0,16},{16,0},{32,48},{48,32},{64,80},{80,64},{96,112},{112,96},{1... | collective-permute-start | bytes 393224 | tf_op jit(solution)/shard_map/ppermute | solution.py:31
  201.1 2.4 %collective-permute-start.27 = (bf16[128,512]{1,0:T(8,128)(2,1)S(1)}, bf16[128,512]{1,0:T(8,128)(2,1)S(1)}, u32[]{:S(2)}, u32[]{:S(2)}) collective-permute-start(bf16[128,512]{1,0:T(8,128)(2,1)S(1)} %get-tuple-element.68), channel_id=1, source_target_pairs={{0,96},{16,112},{32,0},{48,16},{64,32},{80,48},{96,64},{112,80},{1... | collective-permute-start | bytes 393224 | tf_op jit(solution)/shard_map/ppermute | solution.py:27
  203.5 1.6 collective-permute-start.28
  205.1 2.0 collective-permute-done.26
  207.1 2.8 %collective-permute-done.28 = bf16[128,512]{1,0:T(8,128)(2,1)S(1)} collective-permute-done((bf16[128,512]{1,0:T(8,128)(2,1)S(1)}, bf16[128,512]{1,0:T(8,128)(2,1)S(1)}, u32[]{:S(2)}, u32[]{:S(2)}) %collective-permute-start.28) | collective-permute-done | bytes 131104 | tf_op jit(solution)/shard_map/ppermute | solution.py:27
  (130 shorter events, 22.2 us)
Async XLA Ops:
  3.3 24.6 %collective-permute-start = (bf16[256,384]{1,0:T(8,128)(2,1)S(1)}, bf16[256,384]{1,0:T(8,128)(2,1)S(1)}, u32[]{:S(2)}, u32[]{:S(2)}) collective-permute-start(bf16[256,384]{1,0:T(8,128)(2,1)S(1)} %pad_maximum_fusion.5), channel_id=1, source_target_pairs={{0,4},{1,5},{2,6},{3,7},{4,8},{5,9},{6,10},{7,11},{8,12},{9,13},{1... | collective-permute-start | bytes 589832 | tf_op jit(solution)/shard_map/ppermute | solution.py:36
  3.8 24.1 %collective-permute-start.1 = (bf16[256,384]{1,0:T(8,128)(2,1)S(1)}, bf16[256,384]{1,0:T(8,128)(2,1)S(1)}, u32[]{:S(2)}, u32[]{:S(2)}) collective-permute-start(bf16[256,384]{1,0:T(8,128)(2,1)S(1)} %pad_maximum_fusion.6), channel_id=1, source_target_pairs={{0,8},{1,9},{2,10},{3,11},{4,12},{5,13},{6,14},{7,15},{8,0},{9,1},... | collective-permute-start | bytes 589832 | tf_op jit(solution)/shard_map/ppermute | solution.py:36
  6.4 21.5 %collective-permute-start.2 = (bf16[256,384]{1,0:T(8,128)(2,1)S(1)}, bf16[256,384]{1,0:T(8,128)(2,1)S(1)}, u32[]{:S(2)}, u32[]{:S(2)}) collective-permute-start(bf16[256,384]{1,0:T(8,128)(2,1)S(1)} %pad_maximum_fusion.7), channel_id=1, source_target_pairs={{0,12},{1,13},{2,14},{3,15},{4,0},{5,1},{6,2},{7,3},{8,4},{9,5},{1... | collective-permute-start | bytes 589832 | tf_op jit(solution)/shard_map/ppermute | solution.py:36
  7.2 19.2 %all-to-all-start = ((s32[128,1,2]{2,1,0:T(1,128)}), s32[128,1,2]{2,1,0:T(1,128)S(1)}, u32[]{:S(2)}, u32[]{:S(2)}) async-start(s32[128,1,2]{2,1,0:T(1,128)} %bitcast.4), calls=%async_computation | async-start | bytes 131072 | tf_op jit(solution)/shard_map/all_to_all | solution.py:413
  32.4 7.3 %copy-start.14 = (s32[4,2,16]{2,1,0:T(2,128)S(1)}, s32[4,2,16]{2,1,0:T(2,128)}, u32[]{:S(2)}) copy-start(s32[4,2,16]{2,1,0:T(2,128)} %param.24) | copy-start | bytes 1540
  32.4 7.5 %copy-start.15 = (bf16[4096]{0:T(1024)(128)(2,1)S(1)}, bf16[4096]{0:T(1024)(128)(2,1)}, u32[]{:S(2)}) copy-start(bf16[4096]{0:T(1024)(128)(2,1)} %param.18) | copy-start | bytes 24580
  32.4 7.8 %copy-start.8 = (bf16[256,512]{1,0:T(8,128)(2,1)S(1)}, bf16[256,512]{1,0:T(8,128)(2,1)}, u32[]{:S(2)}) copy-start(bf16[256,512]{1,0:T(8,128)(2,1)} %param.16) | copy-start | bytes 786436
  32.4 35.7 %all-to-all-start.1 = ((bf16[256,32,128]{2,1,0:T(8,128)(2,1)}), bf16[256,32,128]{2,1,0:T(8,128)(2,1)}, u32[]{:S(2)}, u32[]{:S(2)}) async-start(bf16[256,32,128]{2,1,0:T(8,128)(2,1)} %gather_fusion), calls=%async_computation.1 | async-start | bytes 4194304 | tf_op jit(solution)/shard_map/all_to_all | solution.py:90
  40.1 33.4 %collective-permute-start.4 = (bf16[256,512]{1,0:T(8,128)(2,1)S(1)}, bf16[256,512]{1,0:T(8,128)(2,1)S(1)}, u32[]{:S(2)}, u32[]{:S(2)}) collective-permute-start(bf16[256,512]{1,0:T(8,128)(2,1)S(1)} %copy-done.8), channel_id=1, source_target_pairs={{0,96},{16,112},{32,0},{48,16},{64,32},{80,48},{96,64},{112,80},{1... | collective-permute-start | bytes 786440 | tf_op jit(solution)/shard_map/ppermute | solution.py:27
  43.0 30.6 %collective-permute-start.5 = (bf16[256,512]{1,0:T(8,128)(2,1)S(1)}, bf16[256,512]{1,0:T(8,128)(2,1)S(1)}, u32[]{:S(2)}, u32[]{:S(2)}) collective-permute-start(bf16[256,512]{1,0:T(8,128)(2,1)S(1)} %copy-done.8), channel_id=1, source_target_pairs={{0,64},{16,80},{32,96},{48,112},{64,0},{80,16},{96,32},{112,48},{1... | collective-permute-start | bytes 786440 | tf_op jit(solution)/shard_map/ppermute | solution.py:27
  43.7 32.3 %collective-permute-start.6 = (bf16[256,512]{1,0:T(8,128)(2,1)S(1)}, bf16[256,512]{1,0:T(8,128)(2,1)S(1)}, u32[]{:S(2)}, u32[]{:S(2)}) collective-permute-start(bf16[256,512]{1,0:T(8,128)(2,1)S(1)} %copy-done.8), channel_id=1, source_target_pairs={{0,32},{16,48},{32,64},{48,80},{64,96},{80,112},{96,0},{112,16},{1... | collective-permute-start | bytes 786440 | tf_op jit(solution)/shard_map/ppermute | solution.py:27
  54.0 22.0 %collective-permute-start.3 = (bf16[1024,256]{1,0:T(8,128)(2,1)S(1)}, bf16[1024,256]{1,0:T(8,128)(2,1)S(1)}, u32[]{:S(2)}, u32[]{:S(2)}) collective-permute-start(bf16[1024,256]{1,0:T(8,128)(2,1)S(1)} %pad_maximum_fusion.1.near_ref), channel_id=1, source_target_pairs={{0,2},{1,3},{2,0},{3,1},{4,6},{5,7},{6,4},{7,5},{8,10},{9,11},{10,... | collective-permute-start | bytes 1572872 | tf_op jit(solution)/shard_map/ppermute | solution.py:40
  71.7 6.5 %copy-start.9 = (bf16[256,512]{1,0:T(8,128)(2,1)S(1)}, bf16[256,512]{1,0:T(8,128)(2,1)}, u32[]{:S(2)}) copy-start(bf16[256,512]{1,0:T(8,128)(2,1)} %param.16) | copy-start | bytes 786436
  73.6 4.5 %copy-start.11 = (bf16[256,512]{1,0:T(8,128)(2,1)}, bf16[256,512]{1,0:T(8,128)(2,1)S(1)}, u32[]{:S(2)}) copy-start(bf16[256,512]{1,0:T(8,128)(2,1)S(1)} %collective-permute-done.4) | copy-start | bytes 786436
  73.6 4.5 %copy-start.12 = (bf16[256,512]{1,0:T(8,128)(2,1)}, bf16[256,512]{1,0:T(8,128)(2,1)S(1)}, u32[]{:S(2)}) copy-start(bf16[256,512]{1,0:T(8,128)(2,1)S(1)} %collective-permute-done.5) | copy-start | bytes 786436
  76.0 2.1 %copy-start.13 = (bf16[256,512]{1,0:T(8,128)(2,1)}, bf16[256,512]{1,0:T(8,128)(2,1)S(1)}, u32[]{:S(2)}) copy-start(bf16[256,512]{1,0:T(8,128)(2,1)S(1)} %collective-permute-done.6) | copy-start | bytes 786436
  76.0 35.8 %collective-permute-start.13 = (bf16[128,4096]{1,0:T(8,128)(2,1)S(1)}, bf16[128,4096]{1,0:T(8,128)(2,1)}, u32[]{:S(2)}, u32[]{:S(2)}) collective-permute-start(bf16[128,4096]{1,0:T(8,128)(2,1)S(1)} %fusion.1.refs_0_), channel_id=1, source_target_pairs={{0,96},{16,112},{32,0},{48,16},{64,32},{80,48},{96,64},{112,80},{1... | collective-permute-start | bytes 3145736 | tf_op jit(solution)/shard_map/ppermute | solution.py:27
  77.9 31.1 %collective-permute-start.11 = (bf16[128,4096]{1,0:T(8,128)(2,1)S(1)}, bf16[128,4096]{1,0:T(8,128)(2,1)S(1)}, u32[]{:S(2)}, u32[]{:S(2)}) collective-permute-start(bf16[128,4096]{1,0:T(8,128)(2,1)S(1)} %fusion.1.refs_0_), channel_id=1, source_target_pairs={{0,32},{16,48},{32,64},{48,80},{64,96},{80,112},{96,0},{112,16},{1... | collective-permute-start | bytes 3145736 | tf_op jit(solution)/shard_map/ppermute | solution.py:27
  78.2 8.3 %collective-permute-start.7 = (bf16[2048,256]{1,0:T(8,128)(2,1)S(1)}, bf16[2048,256]{1,0:T(8,128)(2,1)S(1)}, u32[]{:S(2)}, u32[]{:S(2)}) collective-permute-start(bf16[2048,256]{1,0:T(8,128)(2,1)S(1)} %pad_maximum_fusion), channel_id=1, source_target_pairs={{0,1},{1,0},{2,3},{3,2},{4,5},{5,4},{6,7},{7,6},{8,9},{9,8},{10,11... | collective-permute-start | bytes 3145736 | tf_op jit(solution)/shard_map/ppermute | solution.py:40
  82.8 50.5 %collective-permute-start.16 = (bf16[256,4096]{1,0:T(8,128)(2,1)}, bf16[256,4096]{1,0:T(8,128)(2,1)}, u32[]{:S(2)}, u32[]{:S(2)}) collective-permute-start(bf16[256,4096]{1,0:T(8,128)(2,1)} %maximum_maximum_fusion), channel_id=1, source_target_pairs={{0,16},{16,0},{32,48},{48,32},{64,80},{80,64},{96,112},{112,96},{1... | collective-permute-start | bytes 6291464 | tf_op jit(solution)/shard_map/ppermute | solution.py:31
  99.1 12.7 %copy-start.16 = (bf16[4096]{0:T(1024)(128)(2,1)S(1)}, bf16[4096]{0:T(1024)(128)(2,1)}, u32[]{:S(2)}) copy-start(bf16[4096]{0:T(1024)(128)(2,1)} %param.17) | copy-start | bytes 24580
  99.2 5.6 %collective-permute-start.8 = (bf16[256,128]{1,0:T(8,128)(2,1)S(1)}, bf16[256,128]{1,0:T(8,128)(2,1)S(1)}, u32[]{:S(2)}, u32[]{:S(2)}) collective-permute-start(bf16[256,128]{1,0:T(8,128)(2,1)S(1)} %get-tuple-element.73), channel_id=1, source_target_pairs={{0,12},{1,13},{2,14},{3,15},{4,0},{5,1},{6,2},{7,3},{8,4},{9,5},{1... | collective-permute-start | bytes 196616 | tf_op jit(solution)/shard_map/ppermute | solution.py:36
  99.9 6.0 %collective-permute-start.9 = (bf16[256,128]{1,0:T(8,128)(2,1)S(1)}, bf16[256,128]{1,0:T(8,128)(2,1)S(1)}, u32[]{:S(2)}, u32[]{:S(2)}) collective-permute-start(bf16[256,128]{1,0:T(8,128)(2,1)S(1)} %get-tuple-element.72), channel_id=1, source_target_pairs={{0,8},{1,9},{2,10},{3,11},{4,12},{5,13},{6,14},{7,15},{8,0},{9,1},... | collective-permute-start | bytes 196616 | tf_op jit(solution)/shard_map/ppermute | solution.py:36
  104.8 4.3 %collective-permute-start.10 = (bf16[256,128]{1,0:T(8,128)(2,1)S(1)}, bf16[256,128]{1,0:T(8,128)(2,1)S(1)}, u32[]{:S(2)}, u32[]{:S(2)}) collective-permute-start(bf16[256,128]{1,0:T(8,128)(2,1)S(1)} %get-tuple-element.71), channel_id=1, source_target_pairs={{0,4},{1,5},{2,6},{3,7},{4,8},{5,9},{6,10},{7,11},{8,12},{9,13},{1... | collective-permute-start | bytes 196616 | tf_op jit(solution)/shard_map/ppermute | solution.py:36
  109.9 1.0 copy-start.2
  110.9 15.8 %collective-permute-start.12 = (bf16[64,4096]{1,0:T(8,128)(2,1)}, bf16[64,4096]{1,0:T(8,128)(2,1)S(1)}, u32[]{:S(2)}, u32[]{:S(2)}) collective-permute-start(bf16[64,4096]{1,0:T(8,128)(2,1)} %slice.82), channel_id=1, source_target_pairs={{0,32},{16,48},{32,64},{48,80},{64,96},{80,112},{96,0},{112,16},{1... | collective-permute-start | bytes 1572872 | tf_op jit(solution)/shard_map/ppermute | solution.py:27
  113.0 14.6 %collective-permute-start.14 = (bf16[64,4096]{1,0:T(8,128)(2,1)S(1)}, bf16[64,4096]{1,0:T(8,128)(2,1)S(1)}, u32[]{:S(2)}, u32[]{:S(2)}) collective-permute-start(bf16[64,4096]{1,0:T(8,128)(2,1)S(1)} %slice.83), channel_id=1, source_target_pairs={{0,96},{16,112},{32,0},{48,16},{64,32},{80,48},{96,64},{112,80},{1... | collective-permute-start | bytes 1572872 | tf_op jit(solution)/shard_map/ppermute | solution.py:27
  127.6 10.0 %copy-start.1 = (bf16[4096,512]{1,0:T(8,128)(2,1)S(1)}, bf16[4096,512]{1,0:T(8,128)(2,1)}, u32[]{:S(2)}) copy-start(bf16[4096,512]{1,0:T(8,128)(2,1)} %w_ref.1) | copy-start | bytes 12582916
  127.6 27.9 %collective-permute-start.15 = (bf16[128,4096]{1,0:T(8,128)(2,1)S(1)}, bf16[128,4096]{1,0:T(8,128)(2,1)S(1)}, u32[]{:S(2)}, u32[]{:S(2)}) collective-permute-start(bf16[128,4096]{1,0:T(8,128)(2,1)S(1)} %constant_dynamic-update-slice_fusion.refs_2_), channel_id=1, source_target_pairs={{0,16},{16,0},{32,48},{48,32},{64,80},{80,64},{96,112},{112,96},{1... | collective-permute-start | bytes 3145736 | tf_op jit(solution)/shard_map/ppermute | solution.py:31
  135.1 24.8 %collective-permute-start.18 = (bf16[128,4096]{1,0:T(8,128)(2,1)S(1)}, bf16[128,4096]{1,0:T(8,128)(2,1)S(1)}, u32[]{:S(2)}, u32[]{:S(2)}) collective-permute-start(bf16[128,4096]{1,0:T(8,128)(2,1)S(1)} %get-tuple-element.64.refs_0_), channel_id=1, source_target_pairs={{0,96},{16,112},{32,0},{48,16},{64,32},{80,48},{96,64},{112,80},{1... | collective-permute-start | bytes 3145736 | tf_op jit(solution)/shard_map/ppermute | solution.py:27
  137.6 25.7 %collective-permute-start.19 = (bf16[128,4096]{1,0:T(8,128)(2,1)S(1)}, bf16[128,4096]{1,0:T(8,128)(2,1)S(1)}, u32[]{:S(2)}, u32[]{:S(2)}) collective-permute-start(bf16[128,4096]{1,0:T(8,128)(2,1)S(1)} %get-tuple-element.64.refs_0_), channel_id=1, source_target_pairs={{0,32},{16,48},{32,64},{48,80},{64,96},{80,112},{96,0},{112,16},{1... | collective-permute-start | bytes 3145736 | tf_op jit(solution)/shard_map/ppermute | solution.py:27
  137.6 7.9 %copy-start.3 = (bf16[128,4096]{1,0:T(8,128)(2,1)S(1)}, bf16[128,4096]{1,0:T(8,128)(2,1)}, u32[]{:S(2)}) copy-start(bf16[128,4096]{1,0:T(8,128)(2,1)} %copy-done.2) | copy-start | bytes 3145732
  141.0 14.3 %collective-permute-start.17 = (bf16[64,512]{1,0:T(8,128)(2,1)S(1)}, bf16[64,512]{1,0:T(8,128)(2,1)S(1)}, u32[]{:S(2)}, u32[]{:S(2)}) collective-permute-start(bf16[64,512]{1,0:T(8,128)(2,1)S(1)} %slice.115), channel_id=1, source_target_pairs={{1,0},{2,1},{3,2},{4,3},{5,4},{6,5},{7,6},{8,7},{9,8},{10,9},{11,1... | collective-permute-start | bytes 196616 | tf_op jit(solution)/shard_map/ppermute | solution.py:46
  145.5 3.4 %copy-start = (bf16[512,8,2,512]{3,1,2,0:T(8,128)(2,1)S(1)}, bf16[512,8,2,512]{3,1,2,0:T(8,128)(2,1)}, u32[]{:S(2)}) copy-start(bf16[512,8,2,512]{3,1,2,0:T(8,128)(2,1)} %copy.18) | copy-start | bytes 25165828
  148.9 6.6 %copy-start.6 = (bf16[512,4096]{1,0:T(8,128)(2,1)S(1)}, bf16[512,4096]{1,0:T(8,128)(2,1)}, u32[]{:S(2)}) copy-start(bf16[512,4096]{1,0:T(8,128)(2,1)} %param.22) | copy-start | bytes 12582916
  155.4 7.9 %copy-start.4 = (s32[4]{0:T(128)S(1)}, s32[4]{0:T(128)}, u32[]{:S(2)}) copy-start(s32[4]{0:T(128)} %counts.1) | copy-start | bytes 52
  163.3 10.4 %copy-start.5 = (bf16[512,4096]{1,0:T(8,128)(2,1)S(1)}, bf16[512,4096]{1,0:T(8,128)(2,1)}, u32[]{:S(2)}) copy-start(bf16[512,4096]{1,0:T(8,128)(2,1)} %param.23) | copy-start | bytes 12582916
  171.8 6.5 %collective-permute-start.20 = (bf16[64,512]{1,0:T(8,128)(2,1)S(1)}, bf16[64,512]{1,0:T(8,128)(2,1)S(1)}, u32[]{:S(2)}, u32[]{:S(2)}) collective-permute-start(bf16[64,512]{1,0:T(8,128)(2,1)S(1)} %get-tuple-element.44), channel_id=1, source_target_pairs={{0,1},{1,2},{2,3},{3,4},{4,5},{5,6},{6,7},{7,8},{8,9},{9,10},{10,1... | collective-permute-start | bytes 196616 | tf_op jit(solution)/shard_map/ppermute | solution.py:46
  179.0 1.3 copy-start.7
  181.3 15.1 %collective-permute-start.21 = (bf16[128,1024]{1,0:T(8,128)(2,1)}, bf16[128,1024]{1,0:T(8,128)(2,1)}, u32[]{:S(2)}, u32[]{:S(2)}) collective-permute-start(bf16[128,1024]{1,0:T(8,128)(2,1)} %get-tuple-element.53), channel_id=1, source_target_pairs={{0,32},{16,48},{32,64},{48,80},{64,96},{80,112},{96,0},{112,16},{1... | collective-permute-start | bytes 786440 | tf_op jit(solution)/shard_map/ppermute | solution.py:27
  181.3 15.1 %collective-permute-start.22 = (bf16[128,1024]{1,0:T(8,128)(2,1)}, bf16[128,1024]{1,0:T(8,128)(2,1)}, u32[]{:S(2)}, u32[]{:S(2)}) collective-permute-start(bf16[128,1024]{1,0:T(8,128)(2,1)} %get-tuple-element.55), channel_id=1, source_target_pairs={{0,96},{16,112},{32,0},{48,16},{64,32},{80,48},{96,64},{112,80},{1... | collective-permute-start | bytes 786440 | tf_op jit(solution)/shard_map/ppermute | solution.py:27
  184.5 11.8 %collective-permute-start.23 = (bf16[128,1024]{1,0:T(8,128)(2,1)S(1)}, bf16[128,1024]{1,0:T(8,128)(2,1)}, u32[]{:S(2)}, u32[]{:S(2)}) collective-permute-start(bf16[128,1024]{1,0:T(8,128)(2,1)S(1)} %get-tuple-element.54), channel_id=1, source_target_pairs={{0,64},{16,80},{32,96},{48,112},{64,0},{80,16},{96,32},{112,48},{1... | collective-permute-start | bytes 786440 | tf_op jit(solution)/shard_map/ppermute | solution.py:27
  184.5 15.4 %collective-permute-start.25 = (bf16[128,2048]{1,0:T(8,128)(2,1)S(1)}, bf16[128,2048]{1,0:T(8,128)(2,1)S(1)}, u32[]{:S(2)}, u32[]{:S(2)}) collective-permute-start(bf16[128,2048]{1,0:T(8,128)(2,1)S(1)} %pad_maximum_fusion.2), channel_id=1, source_target_pairs={{0,16},{16,0},{32,48},{48,32},{64,80},{80,64},{96,112},{112,96},{1... | collective-permute-start | bytes 1572872 | tf_op jit(solution)/shard_map/ppermute | solution.py:31
  197.8 7.2 %collective-permute-start.24 = (bf16[128,512]{1,0:T(8,128)(2,1)S(1)}, bf16[128,512]{1,0:T(8,128)(2,1)S(1)}, u32[]{:S(2)}, u32[]{:S(2)}) collective-permute-start(bf16[128,512]{1,0:T(8,128)(2,1)S(1)} %dynamic-slice_convert_fusion.6), channel_id=1, source_target_pairs={{0,16},{16,0},{32,48},{48,32},{64,80},{80,64},{96,112},{112,96},{1... | collective-permute-start | bytes 393224 | tf_op jit(solution)/shard_map/ppermute | solution.py:31
  199.9 10.1 %copy-start.10 = (bf16[256,512]{1,0:T(8,128)(2,1)S(1)}, bf16[256,512]{1,0:T(8,128)(2,1)}, u32[]{:S(2)}) copy-start(bf16[256,512]{1,0:T(8,128)(2,1)} %param.16) | copy-start | bytes 786436
  200.2 6.9 %collective-permute-start.26 = (bf16[128,512]{1,0:T(8,128)(2,1)S(1)}, bf16[128,512]{1,0:T(8,128)(2,1)S(1)}, u32[]{:S(2)}, u32[]{:S(2)}) collective-permute-start(bf16[128,512]{1,0:T(8,128)(2,1)S(1)} %get-tuple-element.66), channel_id=1, source_target_pairs={{0,32},{16,48},{32,64},{48,80},{64,96},{80,112},{96,0},{112,16},{1... | collective-permute-start | bytes 393224 | tf_op jit(solution)/shard_map/ppermute | solution.py:27
  201.1 6.0 %collective-permute-start.27 = (bf16[128,512]{1,0:T(8,128)(2,1)S(1)}, bf16[128,512]{1,0:T(8,128)(2,1)S(1)}, u32[]{:S(2)}, u32[]{:S(2)}) collective-permute-start(bf16[128,512]{1,0:T(8,128)(2,1)S(1)} %get-tuple-element.68), channel_id=1, source_target_pairs={{0,96},{16,112},{32,0},{48,16},{64,32},{80,48},{96,64},{112,80},{1... | collective-permute-start | bytes 393224 | tf_op jit(solution)/shard_map/ppermute | solution.py:27
  203.5 6.5 %collective-permute-start.28 = (bf16[128,512]{1,0:T(8,128)(2,1)S(1)}, bf16[128,512]{1,0:T(8,128)(2,1)S(1)}, u32[]{:S(2)}, u32[]{:S(2)}) collective-permute-start(bf16[128,512]{1,0:T(8,128)(2,1)S(1)} %get-tuple-element.67), channel_id=1, source_target_pairs={{0,64},{16,80},{32,96},{48,112},{64,0},{80,16},{96,32},{112,48},{1... | collective-permute-start | bytes 393224 | tf_op jit(solution)/shard_map/ppermute | solution.py:27

commit v2 on v1

--- a/solution.py
+++ b/solution.py
@@ -310,7 +310,7 @@
         tail_ref[:, cols] = context[queries - SPAN :]
 
 
-def rows_scratch(normed, weight, steps=8):
+def rows_scratch(normed, weight, steps=4):
     key_rows = sum(piece.shape[0] for piece in normed)
     depth, width = weight.shape
     return [
@@ -366,25 +366,26 @@
     enc = lax.axis_index("enc")
     y, z = enc // 2, enc % 2
     part = low_far.shape[1] // NY
-
-    def pair(a, k):
-        return lax.dynamic_slice_in_dim(a, (y + k) % NY * 2 * part, 2 * part, 1)
-
     low_got = swap_z_hi(low_far)
-    top_got = [along_y(pair(top, k).astype(BF), k) for k in (1, 3, 2)]
+
+    def pair(k):
+        return lax.dynamic_slice_in_dim(top, (y + k) % NY * 2 * part, 2 * part, 1)
+
+    top_sum, *top_pairs = lax.optimization_barrier([pair(0)] + [pair(k).astype(BF) for k in (1, 3, 2)])
+    top_got = [along_y(block, k) for block, k in zip(top_pairs, (1, 3, 2))]
     low_sum = low + low_got.astype(F32)
 
     def column(k):
         return lax.dynamic_slice_in_dim(low_sum, (y + k) % NY * part, part, 1)
 
-    last_got = [along_y(column(k).astype(BF), k) for k in (1, 3, 2)]
-    top_sum = pair(top, 0)
+    low_out, *low_parts = lax.optimization_barrier([column(0)] + [column(k).astype(BF) for k in (1, 3, 2)])
+    last_got = [along_y(block, k) for block, k in zip(low_parts, (1, 3, 2))]
+    top_got = after(top_got, *low_parts)
     for got in top_got:
         top_sum = top_sum + got.astype(F32)
     far = lax.dynamic_slice_in_dim(top_sum, (1 - z) * part, part, 1)
     near = lax.dynamic_slice_in_dim(top_sum, z * part, part, 1)
     top_out = near + swap_z_hi(far.astype(BF)).astype(F32)
-    low_out = column(0)
     for got in last_got:
         low_out = low_out + got.astype(F32)
     return jnp.concatenate([top_out, low_out], axis=0)

time: 212 us -> 209 us (0.986)
    ppermute x4, waiting for transfers between devices: 3.94 us -> 12.1 us  [swap_z_hi(): return lax.ppermute(block, 'enc', [(e, e ^ 1) for e in range(2 * NY)])]
    ppermute x15, waiting for transfers between devices: 34.5 us -> 30.7 us  [along_y(): return lax.ppermute(block, 'enc', route)]
    ppermute x2, waiting for transfers between devices: 3.66 us -> 0.31 us  [next_ctx(): return lax.ppermute(block, 'ctx', route)]
    unnamed x40 -> x38, local copies, waits for them, and re-layouts: 22.6 us -> 21.2 us
  transfers between devices with their start and end apart: 31 -> 31, of which waited for: 15 -> 19; matrix products, arithmetic and copies ran while one was open for 16% -> 16% of each run, Pallas kernels for 11% -> 11%
where the time goes in v2:
time: 209 us; the launch traced here: 208 us
  waiting for transfers between devices  65.9 us (32%)
  starting transfers between devices  62.5 us (30%)
  local copies, waits for them, and re-layouts  37.8 us (18%)
  Pallas kernels  30.3 us (14%)
  other arithmetic  7.43 us (4%)
  matrix products  2.71 us (1%)
    ppermute x15, waiting for transfers between devices, along_y(): return lax.ppermute(block, 'enc', route)  30.7 us
    unnamed x38, local copies, waits for them, and re-layouts  21.2 us
    ppermute x15, starting transfers between devices, along_y(): return lax.ppermute(block, 'enc', route)  20.1 us
    pallas_call x1, Pallas kernels, causal_attention(): pl.pallas_call(causal_kernel, grid_spec=pltpu.PrefetchScalarGridSpec(num_...  12.5 us
    all_to_all x1, waiting for transfers between devices, answer(): lax.all_to_all(found, ('enc', 'ctx'), split_axis=0, concat_axis=0, tiled=...  12.2 us
    ppermute x4, waiting for transfers between devices, swap_z_hi(): return lax.ppermute(block, 'enc', [(e, e ^ 1) for e in range(2 * NY)])  12.1 us
    ppermute x4, starting transfers between devices, swap_z_hi(): return lax.ppermute(block, 'enc', [(e, e ^ 1) for e in range(2 * NY)])  10.9 us
    all_to_all x1, starting transfers between devices, per_device(): lax.all_to_all(request, ('enc', 'ctx'), split_axis=0, concat_axis=0, tile...  10.8 us
  transfers between devices with their start and end apart: 31, of which 19 were waited for; matrix products, arithmetic and copies ran while one was open for 16% of the time, Pallas kernels for 11%

profile of v2, /device:TPU:6, one launch (start us, length us, event | category | flops | bytes accessed | tf_op | source)
XLA Modules:
  0.0 207.7 jit_solution(8898700228219732106)
XLA Ops:
  2.1 1.1 constant_dynamic-slice_fusion.6
  3.8 2.6 %collective-permute-start.1 = (bf16[256,384]{1,0:T(8,128)(2,1)S(1)}, bf16[256,384]{1,0:T(8,128)(2,1)S(1)}, u32[]{:S(2)}, u32[]{:S(2)}) collective-permute-start(bf16[256,384]{1,0:T(8,128)(2,1)S(1)} %pad_maximum_fusion.6), channel_id=1, source_target_pairs={{0,8},{1,9},{2,10},{3,11},{4,12},{5,13},{6,14},{7,15},{8,0},{9,1},... | collective-permute-start | bytes 589832 | tf_op jit(solution)/shard_map/ppermute | solution.py:36
  7.2 10.8 %all-to-all-start = ((s32[128,1,2]{2,1,0:T(1,128)}), s32[128,1,2]{2,1,0:T(1,128)S(1)}, u32[]{:S(2)}, u32[]{:S(2)}) async-start(s32[128,1,2]{2,1,0:T(1,128)} %bitcast.4), calls=%async_computation | async-start | bytes 131072 | tf_op jit(solution)/shard_map/all_to_all | solution.py:414
  18.0 5.4 %copy.16 = bf16[64,8,32,128]{3,2,1,0:T(8,128)(2,1)} copy(bf16[64,8,32,128]{3,1,2,0:T(8,128)(2,1)} %bitcast.37) | data formatting | bytes 8388608
  23.4 2.9 %all-to-all-done = s32[128,1,2]{2,1,0:T(1,128)S(1)} async-done(((s32[128,1,2]{2,1,0:T(1,128)}), s32[128,1,2]{2,1,0:T(1,128)S(1)}, u32[]{:S(2)}, u32[]{:S(2)}) %all-to-all-start) | async-done | bytes 1056 | tf_op jit(solution)/shard_map/all_to_all | solution.py:414
  28.0 4.4 %gather_fusion = bf16[256,32,128]{2,1,0:T(8,128)(2,1)} fusion(bf16[512,32,128]{2,1,0:T(8,128)(2,1)} %bitcast.34, s32[1024]{0:T(1024)S(1)} %pad_clamp_fusion.1), kind=kCustom, calls=%fused_computation | custom fusion | bytes 4195328 | tf_op jit(solution)/shard_map/gather | solution.py:86
  32.4 7.3 %all-to-all-start.1 = ((bf16[256,32,128]{2,1,0:T(8,128)(2,1)}), bf16[256,32,128]{2,1,0:T(8,128)(2,1)}, u32[]{:S(2)}, u32[]{:S(2)}) async-start(bf16[256,32,128]{2,1,0:T(8,128)(2,1)} %gather_fusion), calls=%async_computation.1 | async-start | bytes 4194304 | tf_op jit(solution)/shard_map/all_to_all | solution.py:90
  40.1 2.8 %collective-permute-start.4 = (bf16[256,512]{1,0:T(8,128)(2,1)S(1)}, bf16[256,512]{1,0:T(8,128)(2,1)S(1)}, u32[]{:S(2)}, u32[]{:S(2)}) collective-permute-start(bf16[256,512]{1,0:T(8,128)(2,1)S(1)} %copy-done.7), channel_id=1, source_target_pairs={{0,96},{16,112},{32,0},{48,16},{64,32},{80,48},{96,64},{112,80},{1... | collective-permute-start | bytes 786440 | tf_op jit(solution)/shard_map/ppermute | solution.py:27
  44.6 9.4 %copy.18 = bf16[512,8,2,512]{3,1,2,0:T(8,128)(2,1)} copy(bf16[512,8,2,512]{3,2,1,0:T(2,128)(2,1)} %bitcast.36) | data formatting | bytes 16777216
  54.0 1.7 collective-permute-start.3
  55.8 12.2 %all-to-all-done.1 = bf16[256,32,128]{2,1,0:T(8,128)(2,1)} async-done(((bf16[256,32,128]{2,1,0:T(8,128)(2,1)}), bf16[256,32,128]{2,1,0:T(8,128)(2,1)}, u32[]{:S(2)}, u32[]{:S(2)}) %all-to-all-start.1) | async-done | bytes 2097184 | tf_op jit(solution)/shard_map/all_to_all | solution.py:90
  68.0 2.4 %gather_fusion.1 = bf16[128,32,128]{2,1,0:T(8,128)(2,1)S(1)} fusion(bf16[256,32,128]{2,1,0:T(8,128)(2,1)} %all-to-all-done.1, s32[1024]{0:T(1024)S(1)} %pad_clamp_fusion), kind=kCustom, calls=%fused_computation.1 | custom fusion | bytes 2097664 | tf_op jit(solution)/shard_map/gather | solution.py:91
  70.4 1.0 multiply_reduce_fusion
  71.7 1.8 fusion.1.refs_0_
  73.6 2.4 %collective-permute-done.6 = bf16[256,512]{1,0:T(8,128)(2,1)S(1)} collective-permute-done((bf16[256,512]{1,0:T(8,128)(2,1)S(1)}, bf16[256,512]{1,0:T(8,128)(2,1)S(1)}, u32[]{:S(2)}, u32[]{:S(2)}) %collective-permute-start.6) | collective-permute-done | bytes 262176 | tf_op jit(solution)/shard_map/ppermute | solution.py:27
  76.0 1.9 collective-permute-start.13
  81.4 1.5 maximum_maximum_fusion
  82.8 3.7 %collective-permute-start.16 = (bf16[256,4096]{1,0:T(8,128)(2,1)}, bf16[256,4096]{1,0:T(8,128)(2,1)}, u32[]{:S(2)}, u32[]{:S(2)}) collective-permute-start(bf16[256,4096]{1,0:T(8,128)(2,1)} %maximum_maximum_fusion), channel_id=1, source_target_pairs={{0,16},{16,0},{32,48},{48,32},{64,80},{80,64},{96,112},{112,96},{1... | collective-permute-start | bytes 6291464 | tf_op jit(solution)/shard_map/ppermute | solution.py:31
  86.5 12.5 %shard_map.127 = bf16[1024,128]{1,0:T(8,128)(2,1)S(1)} custom-call(s32[4]{0:T(128)S(1)} %get-tuple-element.111.q_blocks, s32[16]{0:T(128)S(1)} %pad_add_fusion.k_blocks, bf16[1024,128]{1,0:T(8,128)(2,1)S(1)} %pad_maximum_fusion.3.q_ref, bf16[1024,256]{1,0:T(8,128)(2,1)S(1)} %pad_maximum_fusion.1.near_ref, ...), custom_call_target="tpu_custom_call" | custom-call | flops 68719476736 | bytes 268435456 | tf_op jit(solution)/shard_map/pallas_call | solution.py:137
  99.9 1.4 collective-permute-start.9
  101.3 3.4 %collective-permute-done.8 = bf16[256,128]{1,0:T(8,128)(2,1)S(1)} collective-permute-done((bf16[256,128]{1,0:T(8,128)(2,1)S(1)}, bf16[256,128]{1,0:T(8,128)(2,1)S(1)}, u32[]{:S(2)}, u32[]{:S(2)}) %collective-permute-start.8) | collective-permute-done | bytes 65568 | tf_op jit(solution)/shard_map/ppermute | solution.py:36
  104.8 1.1 collective-permute-done.9
  105.9 3.1 %collective-permute-done.10 = bf16[256,128]{1,0:T(8,128)(2,1)S(1)} collective-permute-done((bf16[256,128]{1,0:T(8,128)(2,1)S(1)}, bf16[256,128]{1,0:T(8,128)(2,1)S(1)}, u32[]{:S(2)}, u32[]{:S(2)}) %collective-permute-start.10) | collective-permute-done | bytes 65568 | tf_op jit(solution)/shard_map/ppermute | solution.py:36
  112.0 1.1 slice.83
  113.0 2.4 %collective-permute-start.14 = (bf16[64,4096]{1,0:T(8,128)(2,1)S(1)}, bf16[64,4096]{1,0:T(8,128)(2,1)S(1)}, u32[]{:S(2)}, u32[]{:S(2)}) collective-permute-start(bf16[64,4096]{1,0:T(8,128)(2,1)S(1)} %slice.83), channel_id=1, source_target_pairs={{0,96},{16,112},{32,0},{48,16},{64,32},{80,48},{96,64},{112,80},{1... | collective-permute-start | bytes 1572872 | tf_op jit(solution)/shard_map/ppermute | solution.py:27
  115.5 11.2 %collective-permute-done.12 = bf16[64,4096]{1,0:T(8,128)(2,1)S(1)} collective-permute-done((bf16[64,4096]{1,0:T(8,128)(2,1)}, bf16[64,4096]{1,0:T(8,128)(2,1)S(1)}, u32[]{:S(2)}, u32[]{:S(2)}) %collective-permute-start.12) | collective-permute-done | bytes 524320 | tf_op jit(solution)/shard_map/ppermute | solution.py:27
  127.7 1.8 collective-permute-start.15
  129.5 3.8 %collective-permute-done.16 = bf16[256,4096]{1,0:T(8,128)(2,1)} collective-permute-done((bf16[256,4096]{1,0:T(8,128)(2,1)}, bf16[256,4096]{1,0:T(8,128)(2,1)}, u32[]{:S(2)}, u32[]{:S(2)}) %collective-permute-start.16) | collective-permute-done | bytes 2097184 | tf_op jit(solution)/shard_map/ppermute | solution.py:31
  133.3 1.7 fusion.16
  135.1 2.5 %collective-permute-start.18 = (bf16[128,4096]{1,0:T(8,128)(2,1)S(1)}, bf16[128,4096]{1,0:T(8,128)(2,1)S(1)}, u32[]{:S(2)}, u32[]{:S(2)}) collective-permute-start(bf16[128,4096]{1,0:T(8,128)(2,1)S(1)} %get-tuple-element.86.refs_0_), channel_id=1, source_target_pairs={{0,96},{16,112},{32,0},{48,16},{64,32},{80,48},{96,64},{112,80},{1... | collective-permute-start | bytes 3145736 | tf_op jit(solution)/shard_map/ppermute | solution.py:27
  137.6 3.4 %shard_map.128 = bf16[256,512]{1,0:T(8,128)(2,1)S(1)} custom-call(s32[8]{0:T(128)S(1)} %pad_add_fusion.1.order, f32[8,512]{1,0:T(8,128)S(1)} %reshape.199.gain_ref, bf16[4096,512]{1,0:T(8,128)(2,1)S(1)} %copy-done.1, bf16[256,2048]{1,0:T(8,128)(2,1)S(1)} %constant_dynamic-update-slice_fusion.2.refs_0_, bf16[128,4096]{1,0:T(8,128)(2,1)S(1)} %get-tuple-element.87.refs_1_), custom_call_target="tpu_custom_call" | custom-call | flops 1024 | bytes 1024 | tf_op jit(solution)/shard_map/pallas_call | solution.py:231
  141.0 4.4 %collective-permute-start.17 = (bf16[64,512]{1,0:T(8,128)(2,1)S(1)}, bf16[64,512]{1,0:T(8,128)(2,1)S(1)}, u32[]{:S(2)}, u32[]{:S(2)}) collective-permute-start(bf16[64,512]{1,0:T(8,128)(2,1)S(1)} %slice.115), channel_id=1, source_target_pairs={{1,0},{2,1},{3,2},{4,3},{5,4},{6,5},{7,6},{8,7},{9,8},{10,9},{11,1... | collective-permute-start | bytes 196616 | tf_op jit(solution)/shard_map/ppermute | solution.py:46
  145.5 3.4 %copy-done = bf16[512,8,2,512]{3,1,2,0:T(8,128)(2,1)S(1)} copy-done((bf16[512,8,2,512]{3,1,2,0:T(8,128)(2,1)S(1)}, bf16[512,8,2,512]{3,1,2,0:T(8,128)(2,1)}, u32[]{:S(2)}) %copy-start) | copy-done | bytes 8388632
  148.9 6.2 %shard_map.129.kv_ref = bf16[512,1024]{1,0:T(8,128)(2,1)S(1)} custom-call(bf16[4096,1024]{1,0:T(8,128)(2,1)S(1)} %bitcast.32, bf16[128,4096]{1,0:T(8,128)(2,1)S(1)} %fusion.1.refs_0_, bf16[128,4096]{1,0:T(8,128)(2,1)} %collective-permute-done.13.refs_1_, bf16[128,4096]{1,0:T(8,128)(2,1)S(1)} %constant_dynamic-update-slice_fusion.refs_2_, ...), custom_call_target="tpu_custom_call" | custom-call | flops 68719476736 | bytes 268435456 | tf_op jit(solution)/shard_map/pallas_call | solution.py:328
  155.5 1.3 fusion.19
  156.7 3.2 %collective-permute-done.18.refs_1_ = bf16[128,4096]{1,0:T(8,128)(2,1)S(1)} collective-permute-done((bf16[128,4096]{1,0:T(8,128)(2,1)S(1)}, bf16[128,4096]{1,0:T(8,128)(2,1)S(1)}, u32[]{:S(2)}, u32[]{:S(2)}) %collective-permute-start.18) | collective-permute-done | bytes 1048608 | tf_op jit(solution)/shard_map/ppermute | solution.py:27
  159.9 3.4 %collective-permute-done.19.refs_3_ = bf16[128,4096]{1,0:T(8,128)(2,1)S(1)} collective-permute-done((bf16[128,4096]{1,0:T(8,128)(2,1)S(1)}, bf16[128,4096]{1,0:T(8,128)(2,1)S(1)}, u32[]{:S(2)}, u32[]{:S(2)}) %collective-permute-start.19) | collective-permute-done | bytes 1048608 | tf_op jit(solution)/shard_map/ppermute | solution.py:27
  163.3 8.2 %shard_map.130 = (bf16[256,512]{1,0:T(8,128)(2,1)S(1)}, bf16[64,512]{1,0:T(8,128)(2,1)S(1)}) custom-call(s32[4]{0:T(128)S(1)} %copy-done.4, bf16[256,512]{1,0:T(8,128)(2,1)S(1)} %pad_maximum_fusion.4.q_ref, bf16[512,1024]{1,0:T(8,128)(2,1)S(1)} %shard_map.129.kv_ref, bf16[4096,1024]{1,0:T(8,128)(2,1)S(1)} %bitcast.33, ...), custom_call_target="tpu_custom_call" | custom-call | flops 1024 | bytes 1024 | tf_op jit(solution)/shard_map/pallas_call | solution.py:343
  171.5 1.9 collective-permute-start.20
  174.3 3.3 %collective-permute-start.22 = (bf16[128,2048]{1,0:T(8,128)(2,1)S(1)}, bf16[128,2048]{1,0:T(8,128)(2,1)S(1)}, u32[]{:S(2)}, u32[]{:S(2)}) collective-permute-start(bf16[128,2048]{1,0:T(8,128)(2,1)S(1)} %pad_maximum_fusion.2), channel_id=1, source_target_pairs={{0,16},{16,0},{32,48},{48,32},{64,80},{80,64},{96,112},{112,96},{1... | collective-permute-start | bytes 1572872 | tf_op jit(solution)/shard_map/ppermute | solution.py:31
  179.1 3.2 %collective-permute-start.23 = (bf16[128,1024]{1,0:T(8,128)(2,1)S(1)}, bf16[128,1024]{1,0:T(8,128)(2,1)S(1)}, u32[]{:S(2)}, u32[]{:S(2)}) collective-permute-start(bf16[128,1024]{1,0:T(8,128)(2,1)S(1)} %get-tuple-element.64), channel_id=1, source_target_pairs={{0,96},{16,112},{32,0},{48,16},{64,32},{80,48},{96,64},{112,80},{1... | collective-permute-start | bytes 786440 | tf_op jit(solution)/shard_map/ppermute | solution.py:27
  182.3 7.4 %collective-permute-done.22 = bf16[128,2048]{1,0:T(8,128)(2,1)S(1)} collective-permute-done((bf16[128,2048]{1,0:T(8,128)(2,1)S(1)}, bf16[128,2048]{1,0:T(8,128)(2,1)S(1)}, u32[]{:S(2)}, u32[]{:S(2)}) %collective-permute-start.22) | collective-permute-done | bytes 524320 | tf_op jit(solution)/shard_map/ppermute | solution.py:31
  190.0 4.8 %collective-permute-done.21 = bf16[128,1024]{1,0:T(8,128)(2,1)S(1)} collective-permute-done((bf16[128,1024]{1,0:T(8,128)(2,1)S(1)}, bf16[128,1024]{1,0:T(8,128)(2,1)S(1)}, u32[]{:S(2)}, u32[]{:S(2)}) %collective-permute-start.21) | collective-permute-done | bytes 262176 | tf_op jit(solution)/shard_map/ppermute | solution.py:27
  194.9 2.2 %collective-permute-start.25 = (bf16[128,512]{1,0:T(8,128)(2,1)S(1)}, bf16[128,512]{1,0:T(8,128)(2,1)S(1)}, u32[]{:S(2)}, u32[]{:S(2)}) collective-permute-start(bf16[128,512]{1,0:T(8,128)(2,1)S(1)} %dynamic-slice_convert_fusion.3), channel_id=1, source_target_pairs={{0,16},{16,0},{32,48},{48,32},{64,80},{80,64},{96,112},{112,96},{1... | collective-permute-start | bytes 393224 | tf_op jit(solution)/shard_map/ppermute | solution.py:31
  198.0 2.4 %collective-permute-start.27 = (bf16[128,512]{1,0:T(8,128)(2,1)S(1)}, bf16[128,512]{1,0:T(8,128)(2,1)S(1)}, u32[]{:S(2)}, u32[]{:S(2)}) collective-permute-start(bf16[128,512]{1,0:T(8,128)(2,1)S(1)} %get-tuple-element.61), channel_id=1, source_target_pairs={{0,96},{16,112},{32,0},{48,16},{64,32},{80,48},{96,64},{112,80},{1... | collective-permute-start | bytes 393224 | tf_op jit(solution)/shard_map/ppermute | solution.py:27
  200.4 1.2 collective-permute-start.28
  202.1 2.2 %collective-permute-done.26 = bf16[128,512]{1,0:T(8,128)(2,1)S(1)} collective-permute-done((bf16[128,512]{1,0:T(8,128)(2,1)S(1)}, bf16[128,512]{1,0:T(8,128)(2,1)S(1)}, u32[]{:S(2)}, u32[]{:S(2)}) %collective-permute-start.26) | collective-permute-done | bytes 131104 | tf_op jit(solution)/shard_map/ppermute | solution.py:27
  205.3 1.6 collective-permute-done.28
  (130 shorter events, 21.7 us)
Async XLA Ops:
  3.3 24.6 %collective-permute-start = (bf16[256,384]{1,0:T(8,128)(2,1)S(1)}, bf16[256,384]{1,0:T(8,128)(2,1)S(1)}, u32[]{:S(2)}, u32[]{:S(2)}) collective-permute-start(bf16[256,384]{1,0:T(8,128)(2,1)S(1)} %pad_maximum_fusion.5), channel_id=1, source_target_pairs={{0,4},{1,5},{2,6},{3,7},{4,8},{5,9},{6,10},{7,11},{8,12},{9,13},{1... | collective-permute-start | bytes 589832 | tf_op jit(solution)/shard_map/ppermute | solution.py:36
  3.8 24.1 %collective-permute-start.1 = (bf16[256,384]{1,0:T(8,128)(2,1)S(1)}, bf16[256,384]{1,0:T(8,128)(2,1)S(1)}, u32[]{:S(2)}, u32[]{:S(2)}) collective-permute-start(bf16[256,384]{1,0:T(8,128)(2,1)S(1)} %pad_maximum_fusion.6), channel_id=1, source_target_pairs={{0,8},{1,9},{2,10},{3,11},{4,12},{5,13},{6,14},{7,15},{8,0},{9,1},... | collective-permute-start | bytes 589832 | tf_op jit(solution)/shard_map/ppermute | solution.py:36
  6.4 21.5 %collective-permute-start.2 = (bf16[256,384]{1,0:T(8,128)(2,1)S(1)}, bf16[256,384]{1,0:T(8,128)(2,1)S(1)}, u32[]{:S(2)}, u32[]{:S(2)}) collective-permute-start(bf16[256,384]{1,0:T(8,128)(2,1)S(1)} %pad_maximum_fusion.7), channel_id=1, source_target_pairs={{0,12},{1,13},{2,14},{3,15},{4,0},{5,1},{6,2},{7,3},{8,4},{9,5},{1... | collective-permute-start | bytes 589832 | tf_op jit(solution)/shard_map/ppermute | solution.py:36
  7.2 19.2 %all-to-all-start = ((s32[128,1,2]{2,1,0:T(1,128)}), s32[128,1,2]{2,1,0:T(1,128)S(1)}, u32[]{:S(2)}, u32[]{:S(2)}) async-start(s32[128,1,2]{2,1,0:T(1,128)} %bitcast.4), calls=%async_computation | async-start | bytes 131072 | tf_op jit(solution)/shard_map/all_to_all | solution.py:414
  32.4 7.3 %copy-start.13 = (s32[4,2,16]{2,1,0:T(2,128)S(1)}, s32[4,2,16]{2,1,0:T(2,128)}, u32[]{:S(2)}) copy-start(s32[4,2,16]{2,1,0:T(2,128)} %param.24) | copy-start | bytes 1540
  32.4 7.5 %copy-start.14 = (bf16[4096]{0:T(1024)(128)(2,1)S(1)}, bf16[4096]{0:T(1024)(128)(2,1)}, u32[]{:S(2)}) copy-start(bf16[4096]{0:T(1024)(128)(2,1)} %param.18) | copy-start | bytes 24580
  32.4 7.8 %copy-start.7 = (bf16[256,512]{1,0:T(8,128)(2,1)S(1)}, bf16[256,512]{1,0:T(8,128)(2,1)}, u32[]{:S(2)}) copy-start(bf16[256,512]{1,0:T(8,128)(2,1)} %param.16) | copy-start | bytes 786436
  32.4 35.7 %all-to-all-start.1 = ((bf16[256,32,128]{2,1,0:T(8,128)(2,1)}), bf16[256,32,128]{2,1,0:T(8,128)(2,1)}, u32[]{:S(2)}, u32[]{:S(2)}) async-start(bf16[256,32,128]{2,1,0:T(8,128)(2,1)} %gather_fusion), calls=%async_computation.1 | async-start | bytes 4194304 | tf_op jit(solution)/shard_map/all_to_all | solution.py:90
  40.1 33.5 %collective-permute-start.4 = (bf16[256,512]{1,0:T(8,128)(2,1)S(1)}, bf16[256,512]{1,0:T(8,128)(2,1)S(1)}, u32[]{:S(2)}, u32[]{:S(2)}) collective-permute-start(bf16[256,512]{1,0:T(8,128)(2,1)S(1)} %copy-done.7), channel_id=1, source_target_pairs={{0,96},{16,112},{32,0},{48,16},{64,32},{80,48},{96,64},{112,80},{1... | collective-permute-start | bytes 786440 | tf_op jit(solution)/shard_map/ppermute | solution.py:27
  43.0 30.6 %collective-permute-start.5 = (bf16[256,512]{1,0:T(8,128)(2,1)S(1)}, bf16[256,512]{1,0:T(8,128)(2,1)S(1)}, u32[]{:S(2)}, u32[]{:S(2)}) collective-permute-start(bf16[256,512]{1,0:T(8,128)(2,1)S(1)} %copy-done.7), channel_id=1, source_target_pairs={{0,64},{16,80},{32,96},{48,112},{64,0},{80,16},{96,32},{112,48},{1... | collective-permute-start | bytes 786440 | tf_op jit(solution)/shard_map/ppermute | solution.py:27
  43.7 32.3 %collective-permute-start.6 = (bf16[256,512]{1,0:T(8,128)(2,1)S(1)}, bf16[256,512]{1,0:T(8,128)(2,1)S(1)}, u32[]{:S(2)}, u32[]{:S(2)}) collective-permute-start(bf16[256,512]{1,0:T(8,128)(2,1)S(1)} %copy-done.7), channel_id=1, source_target_pairs={{0,32},{16,48},{32,64},{48,80},{64,96},{80,112},{96,0},{112,16},{1... | collective-permute-start | bytes 786440 | tf_op jit(solution)/shard_map/ppermute | solution.py:27
  54.0 22.0 %collective-permute-start.3 = (bf16[1024,256]{1,0:T(8,128)(2,1)S(1)}, bf16[1024,256]{1,0:T(8,128)(2,1)S(1)}, u32[]{:S(2)}, u32[]{:S(2)}) collective-permute-start(bf16[1024,256]{1,0:T(8,128)(2,1)S(1)} %pad_maximum_fusion.1.near_ref), channel_id=1, source_target_pairs={{0,2},{1,3},{2,0},{3,1},{4,6},{5,7},{6,4},{7,5},{8,10},{9,11},{10,... | collective-permute-start | bytes 1572872 | tf_op jit(solution)/shard_map/ppermute | solution.py:40
  71.7 6.5 %copy-start.8 = (bf16[256,512]{1,0:T(8,128)(2,1)S(1)}, bf16[256,512]{1,0:T(8,128)(2,1)}, u32[]{:S(2)}) copy-start(bf16[256,512]{1,0:T(8,128)(2,1)} %param.16) | copy-start | bytes 786436
  73.6 4.5 %copy-start.10 = (bf16[256,512]{1,0:T(8,128)(2,1)}, bf16[256,512]{1,0:T(8,128)(2,1)S(1)}, u32[]{:S(2)}) copy-start(bf16[256,512]{1,0:T(8,128)(2,1)S(1)} %collective-permute-done.4) | copy-start | bytes 786436
  73.6 4.5 %copy-start.11 = (bf16[256,512]{1,0:T(8,128)(2,1)}, bf16[256,512]{1,0:T(8,128)(2,1)S(1)}, u32[]{:S(2)}) copy-start(bf16[256,512]{1,0:T(8,128)(2,1)S(1)} %collective-permute-done.5) | copy-start | bytes 786436
  76.0 2.1 %copy-start.12 = (bf16[256,512]{1,0:T(8,128)(2,1)}, bf16[256,512]{1,0:T(8,128)(2,1)S(1)}, u32[]{:S(2)}) copy-start(bf16[256,512]{1,0:T(8,128)(2,1)S(1)} %collective-permute-done.6) | copy-start | bytes 786436
  76.0 35.9 %collective-permute-start.13 = (bf16[128,4096]{1,0:T(8,128)(2,1)S(1)}, bf16[128,4096]{1,0:T(8,128)(2,1)}, u32[]{:S(2)}, u32[]{:S(2)}) collective-permute-start(bf16[128,4096]{1,0:T(8,128)(2,1)S(1)} %fusion.1.refs_0_), channel_id=1, source_target_pairs={{0,96},{16,112},{32,0},{48,16},{64,32},{80,48},{96,64},{112,80},{1... | collective-permute-start | bytes 3145736 | tf_op jit(solution)/shard_map/ppermute | solution.py:27
  77.9 31.1 %collective-permute-start.11 = (bf16[128,4096]{1,0:T(8,128)(2,1)S(1)}, bf16[128,4096]{1,0:T(8,128)(2,1)S(1)}, u32[]{:S(2)}, u32[]{:S(2)}) collective-permute-start(bf16[128,4096]{1,0:T(8,128)(2,1)S(1)} %fusion.1.refs_0_), channel_id=1, source_target_pairs={{0,32},{16,48},{32,64},{48,80},{64,96},{80,112},{96,0},{112,16},{1... | collective-permute-start | bytes 3145736 | tf_op jit(solution)/shard_map/ppermute | solution.py:27
  78.2 8.3 %collective-permute-start.7 = (bf16[2048,256]{1,0:T(8,128)(2,1)S(1)}, bf16[2048,256]{1,0:T(8,128)(2,1)S(1)}, u32[]{:S(2)}, u32[]{:S(2)}) collective-permute-start(bf16[2048,256]{1,0:T(8,128)(2,1)S(1)} %pad_maximum_fusion), channel_id=1, source_target_pairs={{0,1},{1,0},{2,3},{3,2},{4,5},{5,4},{6,7},{7,6},{8,9},{9,8},{10,11... | collective-permute-start | bytes 3145736 | tf_op jit(solution)/shard_map/ppermute | solution.py:40
  82.8 50.5 %collective-permute-start.16 = (bf16[256,4096]{1,0:T(8,128)(2,1)}, bf16[256,4096]{1,0:T(8,128)(2,1)}, u32[]{:S(2)}, u32[]{:S(2)}) collective-permute-start(bf16[256,4096]{1,0:T(8,128)(2,1)} %maximum_maximum_fusion), channel_id=1, source_target_pairs={{0,16},{16,0},{32,48},{48,32},{64,80},{80,64},{96,112},{112,96},{1... | collective-permute-start | bytes 6291464 | tf_op jit(solution)/shard_map/ppermute | solution.py:31
  99.1 12.8 %copy-start.15 = (bf16[4096]{0:T(1024)(128)(2,1)S(1)}, bf16[4096]{0:T(1024)(128)(2,1)}, u32[]{:S(2)}) copy-start(bf16[4096]{0:T(1024)(128)(2,1)} %param.17) | copy-start | bytes 24580
  99.1 5.6 %collective-permute-start.8 = (bf16[256,128]{1,0:T(8,128)(2,1)S(1)}, bf16[256,128]{1,0:T(8,128)(2,1)S(1)}, u32[]{:S(2)}, u32[]{:S(2)}) collective-permute-start(bf16[256,128]{1,0:T(8,128)(2,1)S(1)} %get-tuple-element.95), channel_id=1, source_target_pairs={{0,12},{1,13},{2,14},{3,15},{4,0},{5,1},{6,2},{7,3},{8,4},{9,5},{1... | collective-permute-start | bytes 196616 | tf_op jit(solution)/shard_map/ppermute | solution.py:36
  99.9 6.0 %collective-permute-start.9 = (bf16[256,128]{1,0:T(8,128)(2,1)S(1)}, bf16[256,128]{1,0:T(8,128)(2,1)S(1)}, u32[]{:S(2)}, u32[]{:S(2)}) collective-permute-start(bf16[256,128]{1,0:T(8,128)(2,1)S(1)} %get-tuple-element.94), channel_id=1, source_target_pairs={{0,8},{1,9},{2,10},{3,11},{4,12},{5,13},{6,14},{7,15},{8,0},{9,1},... | collective-permute-start | bytes 196616 | tf_op jit(solution)/shard_map/ppermute | solution.py:36
  104.8 4.3 %collective-permute-start.10 = (bf16[256,128]{1,0:T(8,128)(2,1)S(1)}, bf16[256,128]{1,0:T(8,128)(2,1)S(1)}, u32[]{:S(2)}, u32[]{:S(2)}) collective-permute-start(bf16[256,128]{1,0:T(8,128)(2,1)S(1)} %get-tuple-element.93), channel_id=1, source_target_pairs={{0,4},{1,5},{2,6},{3,7},{4,8},{5,9},{6,10},{7,11},{8,12},{9,13},{1... | collective-permute-start | bytes 196616 | tf_op jit(solution)/shard_map/ppermute | solution.py:36
  109.9 1.0 copy-start.2
  110.9 15.8 %collective-permute-start.12 = (bf16[64,4096]{1,0:T(8,128)(2,1)}, bf16[64,4096]{1,0:T(8,128)(2,1)S(1)}, u32[]{:S(2)}, u32[]{:S(2)}) collective-permute-start(bf16[64,4096]{1,0:T(8,128)(2,1)} %slice.82), channel_id=1, source_target_pairs={{0,32},{16,48},{32,64},{48,80},{64,96},{80,112},{96,0},{112,16},{1... | collective-permute-start | bytes 1572872 | tf_op jit(solution)/shard_map/ppermute | solution.py:27
  113.0 14.6 %collective-permute-start.14 = (bf16[64,4096]{1,0:T(8,128)(2,1)S(1)}, bf16[64,4096]{1,0:T(8,128)(2,1)S(1)}, u32[]{:S(2)}, u32[]{:S(2)}) collective-permute-start(bf16[64,4096]{1,0:T(8,128)(2,1)S(1)} %slice.83), channel_id=1, source_target_pairs={{0,96},{16,112},{32,0},{48,16},{64,32},{80,48},{96,64},{112,80},{1... | collective-permute-start | bytes 1572872 | tf_op jit(solution)/shard_map/ppermute | solution.py:27
  127.7 9.9 %copy-start.1 = (bf16[4096,512]{1,0:T(8,128)(2,1)S(1)}, bf16[4096,512]{1,0:T(8,128)(2,1)}, u32[]{:S(2)}) copy-start(bf16[4096,512]{1,0:T(8,128)(2,1)} %w_ref.1) | copy-start | bytes 12582916
  127.7 27.8 %collective-permute-start.15 = (bf16[128,4096]{1,0:T(8,128)(2,1)S(1)}, bf16[128,4096]{1,0:T(8,128)(2,1)S(1)}, u32[]{:S(2)}, u32[]{:S(2)}) collective-permute-start(bf16[128,4096]{1,0:T(8,128)(2,1)S(1)} %constant_dynamic-update-slice_fusion.refs_2_), channel_id=1, source_target_pairs={{0,16},{16,0},{32,48},{48,32},{64,80},{80,64},{96,112},{112,96},{1... | collective-permute-start | bytes 3145736 | tf_op jit(solution)/shard_map/ppermute | solution.py:31
  135.1 24.8 %collective-permute-start.18 = (bf16[128,4096]{1,0:T(8,128)(2,1)S(1)}, bf16[128,4096]{1,0:T(8,128)(2,1)S(1)}, u32[]{:S(2)}, u32[]{:S(2)}) collective-permute-start(bf16[128,4096]{1,0:T(8,128)(2,1)S(1)} %get-tuple-element.86.refs_0_), channel_id=1, source_target_pairs={{0,96},{16,112},{32,0},{48,16},{64,32},{80,48},{96,64},{112,80},{1... | collective-permute-start | bytes 3145736 | tf_op jit(solution)/shard_map/ppermute | solution.py:27
  137.6 25.7 %collective-permute-start.19 = (bf16[128,4096]{1,0:T(8,128)(2,1)S(1)}, bf16[128,4096]{1,0:T(8,128)(2,1)S(1)}, u32[]{:S(2)}, u32[]{:S(2)}) collective-permute-start(bf16[128,4096]{1,0:T(8,128)(2,1)S(1)} %get-tuple-element.86.refs_0_), channel_id=1, source_target_pairs={{0,32},{16,48},{32,64},{48,80},{64,96},{80,112},{96,0},{112,16},{1... | collective-permute-start | bytes 3145736 | tf_op jit(solution)/shard_map/ppermute | solution.py:27
  137.6 7.9 %copy-start.3 = (bf16[128,4096]{1,0:T(8,128)(2,1)S(1)}, bf16[128,4096]{1,0:T(8,128)(2,1)}, u32[]{:S(2)}) copy-start(bf16[128,4096]{1,0:T(8,128)(2,1)} %copy-done.2) | copy-start | bytes 3145732
  141.0 14.1 %collective-permute-start.17 = (bf16[64,512]{1,0:T(8,128)(2,1)S(1)}, bf16[64,512]{1,0:T(8,128)(2,1)S(1)}, u32[]{:S(2)}, u32[]{:S(2)}) collective-permute-start(bf16[64,512]{1,0:T(8,128)(2,1)S(1)} %slice.115), channel_id=1, source_target_pairs={{1,0},{2,1},{3,2},{4,3},{5,4},{6,5},{7,6},{8,7},{9,8},{10,9},{11,1... | collective-permute-start | bytes 196616 | tf_op jit(solution)/shard_map/ppermute | solution.py:46
  145.5 3.4 %copy-start = (bf16[512,8,2,512]{3,1,2,0:T(8,128)(2,1)S(1)}, bf16[512,8,2,512]{3,1,2,0:T(8,128)(2,1)}, u32[]{:S(2)}) copy-start(bf16[512,8,2,512]{3,1,2,0:T(8,128)(2,1)} %copy.18) | copy-start | bytes 25165828
  148.9 6.6 %copy-start.6 = (bf16[512,4096]{1,0:T(8,128)(2,1)S(1)}, bf16[512,4096]{1,0:T(8,128)(2,1)}, u32[]{:S(2)}) copy-start(bf16[512,4096]{1,0:T(8,128)(2,1)} %param.22) | copy-start | bytes 12582916
  155.1 8.2 %copy-start.4 = (s32[4]{0:T(128)S(1)}, s32[4]{0:T(128)}, u32[]{:S(2)}) copy-start(s32[4]{0:T(128)} %counts.1) | copy-start | bytes 52
  163.3 10.1 %copy-start.5 = (bf16[512,4096]{1,0:T(8,128)(2,1)S(1)}, bf16[512,4096]{1,0:T(8,128)(2,1)}, u32[]{:S(2)}) copy-start(bf16[512,4096]{1,0:T(8,128)(2,1)} %param.23) | copy-start | bytes 12582916
  171.5 6.5 %collective-permute-start.20 = (bf16[64,512]{1,0:T(8,128)(2,1)S(1)}, bf16[64,512]{1,0:T(8,128)(2,1)S(1)}, u32[]{:S(2)}, u32[]{:S(2)}) collective-permute-start(bf16[64,512]{1,0:T(8,128)(2,1)S(1)} %get-tuple-element.55), channel_id=1, source_target_pairs={{0,1},{1,2},{2,3},{3,4},{4,5},{5,6},{6,7},{7,8},{8,9},{9,10},{10,1... | collective-permute-start | bytes 196616 | tf_op jit(solution)/shard_map/ppermute | solution.py:46
  174.3 15.4 %collective-permute-start.22 = (bf16[128,2048]{1,0:T(8,128)(2,1)S(1)}, bf16[128,2048]{1,0:T(8,128)(2,1)S(1)}, u32[]{:S(2)}, u32[]{:S(2)}) collective-permute-start(bf16[128,2048]{1,0:T(8,128)(2,1)S(1)} %pad_maximum_fusion.2), channel_id=1, source_target_pairs={{0,16},{16,0},{32,48},{48,32},{64,80},{80,64},{96,112},{112,96},{1... | collective-permute-start | bytes 1572872 | tf_op jit(solution)/shard_map/ppermute | solution.py:31
  179.0 15.8 %collective-permute-start.21 = (bf16[128,1024]{1,0:T(8,128)(2,1)S(1)}, bf16[128,1024]{1,0:T(8,128)(2,1)S(1)}, u32[]{:S(2)}, u32[]{:S(2)}) collective-permute-start(bf16[128,1024]{1,0:T(8,128)(2,1)S(1)} %get-tuple-element.59), channel_id=1, source_target_pairs={{0,32},{16,48},{32,64},{48,80},{64,96},{80,112},{96,0},{112,16},{1... | collective-permute-start | bytes 786440 | tf_op jit(solution)/shard_map/ppermute | solution.py:27
  179.1 15.7 %collective-permute-start.23 = (bf16[128,1024]{1,0:T(8,128)(2,1)S(1)}, bf16[128,1024]{1,0:T(8,128)(2,1)S(1)}, u32[]{:S(2)}, u32[]{:S(2)}) collective-permute-start(bf16[128,1024]{1,0:T(8,128)(2,1)S(1)} %get-tuple-element.64), channel_id=1, source_target_pairs={{0,96},{16,112},{32,0},{48,16},{64,32},{80,48},{96,64},{112,80},{1... | collective-permute-start | bytes 786440 | tf_op jit(solution)/shard_map/ppermute | solution.py:27
  182.3 12.5 %collective-permute-start.24 = (bf16[128,1024]{1,0:T(8,128)(2,1)S(1)}, bf16[128,1024]{1,0:T(8,128)(2,1)S(1)}, u32[]{:S(2)}, u32[]{:S(2)}) collective-permute-start(bf16[128,1024]{1,0:T(8,128)(2,1)S(1)} %get-tuple-element.66), channel_id=1, source_target_pairs={{0,64},{16,80},{32,96},{48,112},{64,0},{80,16},{96,32},{112,48},{1... | collective-permute-start | bytes 786440 | tf_op jit(solution)/shard_map/ppermute | solution.py:27
  189.9 17.0 %copy-start.9 = (bf16[256,512]{1,0:T(8,128)(2,1)S(1)}, bf16[256,512]{1,0:T(8,128)(2,1)}, u32[]{:S(2)}) copy-start(bf16[256,512]{1,0:T(8,128)(2,1)} %param.16) | copy-start | bytes 786436
  194.9 7.1 %collective-permute-start.25 = (bf16[128,512]{1,0:T(8,128)(2,1)S(1)}, bf16[128,512]{1,0:T(8,128)(2,1)S(1)}, u32[]{:S(2)}, u32[]{:S(2)}) collective-permute-start(bf16[128,512]{1,0:T(8,128)(2,1)S(1)} %dynamic-slice_convert_fusion.3), channel_id=1, source_target_pairs={{0,16},{16,0},{32,48},{48,32},{64,80},{80,64},{96,112},{112,96},{1... | collective-permute-start | bytes 393224 | tf_op jit(solution)/shard_map/ppermute | solution.py:31
  197.1 7.2 %collective-permute-start.26 = (bf16[128,512]{1,0:T(8,128)(2,1)S(1)}, bf16[128,512]{1,0:T(8,128)(2,1)S(1)}, u32[]{:S(2)}, u32[]{:S(2)}) collective-permute-start(bf16[128,512]{1,0:T(8,128)(2,1)S(1)} %get-tuple-element.60), channel_id=1, source_target_pairs={{0,32},{16,48},{32,64},{48,80},{64,96},{80,112},{96,0},{112,16},{1... | collective-permute-start | bytes 393224 | tf_op jit(solution)/shard_map/ppermute | solution.py:27
  198.0 7.3 %collective-permute-start.27 = (bf16[128,512]{1,0:T(8,128)(2,1)S(1)}, bf16[128,512]{1,0:T(8,128)(2,1)S(1)}, u32[]{:S(2)}, u32[]{:S(2)}) collective-permute-start(bf16[128,512]{1,0:T(8,128)(2,1)S(1)} %get-tuple-element.61), channel_id=1, source_target_pairs={{0,96},{16,112},{32,0},{48,16},{64,32},{80,48},{96,64},{112,80},{1... | collective-permute-start | bytes 393224 | tf_op jit(solution)/shard_map/ppermute | solution.py:27
  200.4 6.5 %collective-permute-start.28 = (bf16[128,512]{1,0:T(8,128)(2,1)S(1)}, bf16[128,512]{1,0:T(8,128)(2,1)S(1)}, u32[]{:S(2)}, u32[]{:S(2)}) collective-permute-start(bf16[128,512]{1,0:T(8,128)(2,1)S(1)} %get-tuple-element.62), channel_id=1, source_target_pairs={{0,64},{16,80},{32,96},{48,112},{64,0},{80,16},{96,32},{112,48},{1... | collective-permute-start | bytes 393224 | tf_op jit(solution)/shard_map/ppermute | solution.py:27

commit v3 on v2

--- a/solution.py
+++ b/solution.py
@@ -59,7 +59,7 @@
     far = along_y(onward[0][:half], 1), along_y(onward[1][half:], -1)
     far = jnp.concatenate(far, axis=0)
     side_above, side_below = along_y(side, -1), along_y(side, 1)
-    return (block, above, far, below), (side, side_above, swap_z_hi(far), side_below), swapped[2 * half :]
+    return (block, above, far, below), (side, side_above, swap_z_hi(far), side_below), swapped
 
 
 def rms_norm(rows, gain):
@@ -170,11 +170,10 @@
     return [head(0)] + [along_x(head(k), k) for k in (1, 2, 3)]
 
 
-def near_attention(pieces, near, side):
-    rows = pieces[0].shape[0]
+def near_attention(queries, near, side):
+    rows = queries.shape[0] // NX
     ctx = lax.axis_index("ctx")
     x, rest = ctx // 4, ctx % 4
-    queries = jnp.concatenate([p[:, :HD] for p in pieces], axis=0)
     far = swap_rest(jnp.concatenate([near, side], axis=0), 1)
     source_x = jnp.stack([(x - k) % NX for k in range(4)]).astype(jnp.int32)
     q_blocks = source_x * 4 + rest
@@ -209,8 +208,9 @@
         col = k % NY * width
         if k < NY:
             return near_ref[:, col : col + width].astype(F32)
-        low = NY * width + col
-        return jnp.concatenate([far_ref[:, col : col + width], far_ref[:, low : low + width]], axis=0).astype(F32)
+        low, first = NY * width + col, far_ref.shape[0] // 2
+        parts = [far_ref[first:, col : col + width], far_ref[first:, low : low + width]]
+        return jnp.concatenate(parts, axis=0).astype(F32)
 
     square = jnp.zeros((out_ref.shape[0], 1), F32)
     for k in range(count):
@@ -414,6 +414,7 @@
     asked = lax.all_to_all(request, ("enc", "ctx"), split_axis=0, concat_axis=0, tiled=True).reshape(-1)
     dealt = deal_heads(*after((self_queries, self_keys, self_values), request))
     near = jnp.concatenate([p[:, HD:] for p in dealt], axis=0)
+    dealt = jnp.concatenate([p[:, :HD] for p in dealt], axis=0)
     found = lookup(after(asked, near), store_table)
     near, hidden, cross_kv_weight = after((near, hidden_in, cross_kv_weight), found)
     side = swap_rest(near, 2)
@@ -421,7 +422,7 @@
     kv_weight = cross_kv_weight.reshape(-1, 2 * local_width)
 
     own_rows = rms_norm(answer(found, destination), store_gain)
-    own_rows = after(own_rows, kv_weight, side, *hidden)
+    own_rows = after(own_rows, kv_weight, side, dealt, *hidden)
     near, side, hidden = after((near, side, hidden), own_rows)
     near_context = near_attention(dealt, near, side)
     self_context = return_heads(near_context)

time: 209 us -> 204 us (0.976)
  waiting for transfers between devices: 65.9 us -> 61.8 us
    ppermute x15, waiting for transfers between devices: 30.7 us -> 24.2 us  [along_y(): return lax.ppermute(block, 'enc', route)]
    ppermute x4, waiting for transfers between devices: 12.1 us -> 16.6 us  [swap_z_hi(): return lax.ppermute(block, 'enc', [(e, e ^ 1) for e in range(2 * NY)])]
    ppermute x4, starting transfers between devices: 10.9 us -> 7.57 us  [swap_z_hi(): return lax.ppermute(block, 'enc', [(e, e ^ 1) for e in range(2 * NY)])]
    all_to_all x1, waiting for transfers between devices: 12.2 us -> 9.31 us  [answer(): lax.all_to_all(found, ('enc', 'ctx'), split_axis=0, concat_axis=0, tiled=...]
    ppermute x15, starting transfers between devices: 20.1 us -> 22.2 us  [along_y(): return lax.ppermute(block, 'enc', route)]
    unnamed x38 -> x42, local copies, waits for them, and re-layouts: 21.2 us -> 21.1 us
  transfers between devices with their start and end apart: 31 -> 31, of which waited for: 19 -> 15; matrix products, arithmetic and copies ran while one was open for 16% -> 17% of each run, Pallas kernels for 11% -> 11%
where the time goes in v3:
time: 204 us; the launch traced here: 203 us
  waiting for transfers between devices  61.8 us (30%)
  starting transfers between devices  60.7 us (30%)
  local copies, waits for them, and re-layouts  36.9 us (18%)
  Pallas kernels  30.6 us (15%)
  other arithmetic  9.21 us (5%)
  matrix products  2.77 us (1%)
    ppermute x15, waiting for transfers between devices, along_y(): return lax.ppermute(block, 'enc', route)  24.2 us
    ppermute x15, starting transfers between devices, along_y(): return lax.ppermute(block, 'enc', route)  22.2 us
    unnamed x42, local copies, waits for them, and re-layouts  21.1 us
    ppermute x4, waiting for transfers between devices, swap_z_hi(): return lax.ppermute(block, 'enc', [(e, e ^ 1) for e in range(2 * NY)])  16.6 us
    pallas_call x1, Pallas kernels, causal_attention(): pl.pallas_call(causal_kernel, grid_spec=pltpu.PrefetchScalarGridSpec(num_...  12.5 us
    all_to_all x1, starting transfers between devices, per_device(): lax.all_to_all(request, ('enc', 'ctx'), split_axis=0, concat_axis=0, tile...  10.8 us
    all_to_all x1, waiting for transfers between devices, answer(): lax.all_to_all(found, ('enc', 'ctx'), split_axis=0, concat_axis=0, tiled=...  9.31 us
    ppermute x6, waiting for transfers between devices, along_x(): return lax.ppermute(block, 'ctx', route)  8.23 us
  transfers between devices with their start and end apart: 31, of which 15 were waited for; matrix products, arithmetic and copies ran while one was open for 17% of the time, Pallas kernels for 11%

profile of v3, /device:TPU:6, one launch (start us, length us, event | category | flops | bytes accessed | tf_op | source)
XLA Modules:
  0.0 202.9 jit_solution(1635400174438124950)
XLA Ops:
  2.1 1.1 constant_dynamic-slice_fusion.6
  3.8 2.6 %collective-permute-start.1 = (bf16[256,384]{1,0:T(8,128)(2,1)S(1)}, bf16[256,384]{1,0:T(8,128)(2,1)S(1)}, u32[]{:S(2)}, u32[]{:S(2)}) collective-permute-start(bf16[256,384]{1,0:T(8,128)(2,1)S(1)} %pad_maximum_fusion.6), channel_id=1, source_target_pairs={{0,8},{1,9},{2,10},{3,11},{4,12},{5,13},{6,14},{7,15},{8,0},{9,1},... | collective-permute-start | bytes 589832 | tf_op jit(solution)/shard_map/ppermute | solution.py:36
  7.2 10.8 %all-to-all-start = ((s32[128,1,2]{2,1,0:T(1,128)}), s32[128,1,2]{2,1,0:T(1,128)S(1)}, u32[]{:S(2)}, u32[]{:S(2)}) async-start(s32[128,1,2]{2,1,0:T(1,128)} %bitcast.4), calls=%async_computation | async-start | bytes 131072 | tf_op jit(solution)/shard_map/all_to_all | solution.py:414
  18.0 5.4 %copy.16 = bf16[64,8,32,128]{3,2,1,0:T(8,128)(2,1)} copy(bf16[64,8,32,128]{3,1,2,0:T(8,128)(2,1)} %bitcast.37) | data formatting | bytes 8388608
  23.4 2.9 %all-to-all-done = s32[128,1,2]{2,1,0:T(1,128)S(1)} async-done(((s32[128,1,2]{2,1,0:T(1,128)}), s32[128,1,2]{2,1,0:T(1,128)S(1)}, u32[]{:S(2)}, u32[]{:S(2)}) %all-to-all-start) | async-done | bytes 1056 | tf_op jit(solution)/shard_map/all_to_all | solution.py:414
  28.7 4.5 %gather_fusion = bf16[256,32,128]{2,1,0:T(8,128)(2,1)} fusion(bf16[512,32,128]{2,1,0:T(8,128)(2,1)} %bitcast.34, s32[1024]{0:T(1024)S(1)} %pad_clamp_fusion.1), kind=kCustom, calls=%fused_computation | custom fusion | bytes 4195328 | tf_op jit(solution)/shard_map/gather | solution.py:86
  33.2 7.3 %all-to-all-start.1 = ((bf16[256,32,128]{2,1,0:T(8,128)(2,1)}), bf16[256,32,128]{2,1,0:T(8,128)(2,1)}, u32[]{:S(2)}, u32[]{:S(2)}) async-start(bf16[256,32,128]{2,1,0:T(8,128)(2,1)} %gather_fusion), calls=%async_computation.1 | async-start | bytes 4194304 | tf_op jit(solution)/shard_map/all_to_all | solution.py:90
  41.1 1.5 collective-permute-start.6
  42.6 2.8 %collective-permute-start.5 = (bf16[256,512]{1,0:T(8,128)(2,1)S(1)}, bf16[256,512]{1,0:T(8,128)(2,1)S(1)}, u32[]{:S(2)}, u32[]{:S(2)}) collective-permute-start(bf16[256,512]{1,0:T(8,128)(2,1)S(1)} %copy-done.11), channel_id=1, source_target_pairs={{0,64},{16,80},{32,96},{48,112},{64,0},{80,16},{96,32},{112,48},{1... | collective-permute-start | bytes 786440 | tf_op jit(solution)/shard_map/ppermute | solution.py:27
  45.4 1.4 collective-permute-start.4
  46.8 1.7 collective-permute-start.3
  48.5 9.4 %copy.18 = bf16[512,8,2,512]{3,1,2,0:T(8,128)(2,1)} copy(bf16[512,8,2,512]{3,2,1,0:T(2,128)(2,1)} %bitcast.36) | data formatting | bytes 16777216
  59.6 9.3 %all-to-all-done.1 = bf16[256,32,128]{2,1,0:T(8,128)(2,1)} async-done(((bf16[256,32,128]{2,1,0:T(8,128)(2,1)}), bf16[256,32,128]{2,1,0:T(8,128)(2,1)}, u32[]{:S(2)}, u32[]{:S(2)}) %all-to-all-start.1) | async-done | bytes 2097184 | tf_op jit(solution)/shard_map/all_to_all | solution.py:90
  68.9 2.4 %gather_fusion.1 = bf16[128,32,128]{2,1,0:T(8,128)(2,1)S(1)} fusion(bf16[256,32,128]{2,1,0:T(8,128)(2,1)} %all-to-all-done.1, s32[1024]{0:T(1024)S(1)} %pad_clamp_fusion), kind=kCustom, calls=%fused_computation.1 | custom fusion | bytes 2097664 | tf_op jit(solution)/shard_map/gather | solution.py:91
  72.6 2.3 %fusion.1.refs_0_ = bf16[128,4096]{1,0:T(8,128)(2,1)} fusion(f32[16,8,32,128]{3,2,1,0:T(8,128)S(1)} %convert.24, f32[4096]{0:T(1024)S(1)} %convert_element_type.76, f32[128]{0:T(128)S(1)} %add_rsqrt_fusion), kind=kLoop, calls=%fused_computation.4 | loop fusion | flops 1572864 | bytes 3162624 | tf_op jit(solution)/shard_map/convert_element_type | solution.py:68
  74.9 2.2 %collective-permute-done.5 = bf16[256,512]{1,0:T(8,128)(2,1)S(1)} collective-permute-done((bf16[256,512]{1,0:T(8,128)(2,1)S(1)}, bf16[256,512]{1,0:T(8,128)(2,1)S(1)}, u32[]{:S(2)}, u32[]{:S(2)}) %collective-permute-start.5) | collective-permute-done | bytes 262176 | tf_op jit(solution)/shard_map/ppermute | solution.py:27
  77.1 1.7 collective-permute-start.13
  79.7 2.8 %maximum_maximum_fusion = bf16[256,4096]{1,0:T(8,128)(2,1)} fusion(bf16[128,2048]{1,0:T(8,128)(2,1)S(1)} %get-tuple-element.90, bf16[128,2048]{1,0:T(8,128)(2,1)S(1)} %get-tuple-element.89, bf16[128,4096]{1,0:T(8,128)(2,1)} %fusion.1.refs_0_), kind=kLoop, calls=%fused_computation.7 | loop fusion | flops 6291456 | bytes 4194304 | tf_op jit(solution)/shard_map/concatenate | solution.py:56
  82.4 3.5 %collective-permute-start.16 = (bf16[256,4096]{1,0:T(8,128)(2,1)}, bf16[256,4096]{1,0:T(8,128)(2,1)S(1)}, u32[]{:S(2)}, u32[]{:S(2)}) collective-permute-start(bf16[256,4096]{1,0:T(8,128)(2,1)} %maximum_maximum_fusion), channel_id=1, source_target_pairs={{0,16},{16,0},{32,48},{48,32},{64,80},{80,64},{96,112},{112,96},{1... | collective-permute-start | bytes 6291464 | tf_op jit(solution)/shard_map/ppermute | solution.py:31
  86.0 12.5 %shard_map.127 = bf16[1024,128]{1,0:T(8,128)(2,1)S(1)} custom-call(s32[4]{0:T(128)S(1)} %get-tuple-element.109.q_blocks, s32[16]{0:T(128)S(1)} %pad_add_fusion.k_blocks, bf16[1024,128]{1,0:T(8,128)(2,1)S(1)} %pad_maximum_fusion.3.q_ref, bf16[1024,256]{1,0:T(8,128)(2,1)S(1)} %copy-done.3, bf16[1024,256]{1,0:T(8,128)(2,1)S(1)} %copy-done.5, ...), custom_call_target="tpu_custom_call" | custom-call | flops 68719476736 | bytes 268435456 | tf_op jit(solution)/shard_map/pallas_call | solution.py:137
  99.5 2.4 %collective-permute-start.10 = (bf16[256,128]{1,0:T(8,128)(2,1)S(1)}, bf16[256,128]{1,0:T(8,128)(2,1)S(1)}, u32[]{:S(2)}, u32[]{:S(2)}) collective-permute-start(bf16[256,128]{1,0:T(8,128)(2,1)S(1)} %get-tuple-element.91), channel_id=1, source_target_pairs={{0,4},{1,5},{2,6},{3,7},{4,8},{5,9},{6,10},{7,11},{8,12},{9,13},{1... | collective-permute-start | bytes 196616 | tf_op jit(solution)/shard_map/ppermute | solution.py:36
  101.9 2.3 %collective-permute-done.8 = bf16[256,128]{1,0:T(8,128)(2,1)S(1)} collective-permute-done((bf16[256,128]{1,0:T(8,128)(2,1)S(1)}, bf16[256,128]{1,0:T(8,128)(2,1)S(1)}, u32[]{:S(2)}, u32[]{:S(2)}) %collective-permute-start.8) | collective-permute-done | bytes 65568 | tf_op jit(solution)/shard_map/ppermute | solution.py:36
  104.5 5.9 %collective-permute-done.9 = bf16[256,128]{1,0:T(8,128)(2,1)S(1)} collective-permute-done((bf16[256,128]{1,0:T(8,128)(2,1)S(1)}, bf16[256,128]{1,0:T(8,128)(2,1)S(1)}, u32[]{:S(2)}, u32[]{:S(2)}) %collective-permute-start.9) | collective-permute-done | bytes 65568 | tf_op jit(solution)/shard_map/ppermute | solution.py:36
  112.5 1.1 slice.80
  113.6 3.3 %collective-permute-start.14 = (bf16[64,4096]{1,0:T(8,128)(2,1)S(1)}, bf16[64,4096]{1,0:T(8,128)(2,1)S(1)}, u32[]{:S(2)}, u32[]{:S(2)}) collective-permute-start(bf16[64,4096]{1,0:T(8,128)(2,1)S(1)} %slice.80), channel_id=1, source_target_pairs={{0,96},{16,112},{32,0},{48,16},{64,32},{80,48},{96,64},{112,80},{1... | collective-permute-start | bytes 1572872 | tf_op jit(solution)/shard_map/ppermute | solution.py:27
  116.9 10.7 %collective-permute-done.12 = bf16[64,4096]{1,0:T(8,128)(2,1)} collective-permute-done((bf16[64,4096]{1,0:T(8,128)(2,1)}, bf16[64,4096]{1,0:T(8,128)(2,1)}, u32[]{:S(2)}, u32[]{:S(2)}) %collective-permute-start.12) | collective-permute-done | bytes 524320 | tf_op jit(solution)/shard_map/ppermute | solution.py:27
  127.6 1.1 constant_dynamic-update-slice_fusion.1
  129.1 3.6 %collective-permute-done.16.refs_1_ = bf16[256,4096]{1,0:T(8,128)(2,1)S(1)} collective-permute-done((bf16[256,4096]{1,0:T(8,128)(2,1)}, bf16[256,4096]{1,0:T(8,128)(2,1)S(1)}, u32[]{:S(2)}, u32[]{:S(2)}) %collective-permute-start.16) | collective-permute-done | bytes 2097184 | tf_op jit(solution)/shard_map/ppermute | solution.py:31
  133.3 2.7 %collective-permute-start.18 = (bf16[128,4096]{1,0:T(8,128)(2,1)S(1)}, bf16[128,4096]{1,0:T(8,128)(2,1)S(1)}, u32[]{:S(2)}, u32[]{:S(2)}) collective-permute-start(bf16[128,4096]{1,0:T(8,128)(2,1)S(1)} %slice.112.refs_0_), channel_id=1, source_target_pairs={{0,96},{16,112},{32,0},{48,16},{64,32},{80,48},{96,64},{112,80},{1... | collective-permute-start | bytes 3145736 | tf_op jit(solution)/shard_map/ppermute | solution.py:27
  136.1 3.4 %shard_map.128 = bf16[256,512]{1,0:T(8,128)(2,1)S(1)} custom-call(s32[8]{0:T(128)S(1)} %pad_add_fusion.1.order, f32[8,512]{1,0:T(8,128)S(1)} %reshape.199.gain_ref, bf16[4096,512]{1,0:T(8,128)(2,1)S(1)} %copy-done.1, bf16[256,2048]{1,0:T(8,128)(2,1)S(1)} %constant_dynamic-update-slice_fusion.2.refs_0_, bf16[256,4096]{1,0:T(8,128)(2,1)S(1)} %collective-permute-done.16.refs_1_), custom_call_target="tpu_custom_call" | custom-call | flops 1024 | bytes 1024 | tf_op jit(solution)/shard_map/pallas_call | solution.py:231
  139.5 2.4 %collective-permute-start.17 = (bf16[64,512]{1,0:T(8,128)(2,1)S(1)}, bf16[64,512]{1,0:T(8,128)(2,1)S(1)}, u32[]{:S(2)}, u32[]{:S(2)}) collective-permute-start(bf16[64,512]{1,0:T(8,128)(2,1)S(1)} %slice.110), channel_id=1, source_target_pairs={{1,0},{2,1},{3,2},{4,3},{5,4},{6,5},{7,6},{8,7},{9,8},{10,9},{11,1... | collective-permute-start | bytes 196616 | tf_op jit(solution)/shard_map/ppermute | solution.py:46
  141.9 3.4 %copy-done = bf16[512,8,2,512]{3,1,2,0:T(8,128)(2,1)S(1)} copy-done((bf16[512,8,2,512]{3,1,2,0:T(8,128)(2,1)S(1)}, bf16[512,8,2,512]{3,1,2,0:T(8,128)(2,1)}, u32[]{:S(2)}) %copy-start) | copy-done | bytes 8388632
  145.3 6.4 %shard_map.129.kv_ref = bf16[512,1024]{1,0:T(8,128)(2,1)S(1)} custom-call(bf16[4096,1024]{1,0:T(8,128)(2,1)S(1)} %bitcast.32, bf16[128,4096]{1,0:T(8,128)(2,1)} %fusion.1.refs_0_, bf16[128,4096]{1,0:T(8,128)(2,1)} %collective-permute-done.13.refs_1_, bf16[128,4096]{1,0:T(8,128)(2,1)S(1)} %constant_dynamic-update-slice_fusion.refs_2_, ...), custom_call_target="tpu_custom_call" | custom-call | flops 68719476736 | bytes 268435456 | tf_op jit(solution)/shard_map/pallas_call | solution.py:328
  151.8 3.1 %collective-permute-done.15.refs_2_ = bf16[128,4096]{1,0:T(8,128)(2,1)S(1)} collective-permute-done((bf16[128,4096]{1,0:T(8,128)(2,1)S(1)}, bf16[128,4096]{1,0:T(8,128)(2,1)S(1)}, u32[]{:S(2)}, u32[]{:S(2)}) %collective-permute-start.15) | collective-permute-done | bytes 1048608 | tf_op jit(solution)/shard_map/ppermute | solution.py:31
  154.9 1.3 fusion.18
  156.3 2.6 %collective-permute-done.19.refs_3_ = bf16[128,4096]{1,0:T(8,128)(2,1)S(1)} collective-permute-done((bf16[128,4096]{1,0:T(8,128)(2,1)S(1)}, bf16[128,4096]{1,0:T(8,128)(2,1)S(1)}, u32[]{:S(2)}, u32[]{:S(2)}) %collective-permute-start.19) | collective-permute-done | bytes 1048608 | tf_op jit(solution)/shard_map/ppermute | solution.py:27
  158.8 8.2 %shard_map.130 = (bf16[256,512]{1,0:T(8,128)(2,1)S(1)}, bf16[64,512]{1,0:T(8,128)(2,1)S(1)}) custom-call(s32[4]{0:T(128)S(1)} %copy-done.8, bf16[256,512]{1,0:T(8,128)(2,1)S(1)} %pad_maximum_fusion.4.q_ref, bf16[512,1024]{1,0:T(8,128)(2,1)S(1)} %shard_map.129.kv_ref, bf16[4096,1024]{1,0:T(8,128)(2,1)S(1)} %bitcast.33, bf16[128,4096]{1,0:T(8,128)(2,1)S(1)} %slice.112.refs_0_, ...), custom_call_target="tpu_custom_call" | custom-call | flops 1024 | bytes 1024 | tf_op jit(solution)/shard_map/pallas_call | solution.py:343
  167.1 1.9 collective-permute-start.20
  169.9 3.1 %collective-permute-start.22 = (bf16[128,2048]{1,0:T(8,128)(2,1)S(1)}, bf16[128,2048]{1,0:T(8,128)(2,1)S(1)}, u32[]{:S(2)}, u32[]{:S(2)}) collective-permute-start(bf16[128,2048]{1,0:T(8,128)(2,1)S(1)} %pad_maximum_fusion.2), channel_id=1, source_target_pairs={{0,16},{16,0},{32,48},{48,32},{64,80},{80,64},{96,112},{112,96},{1... | collective-permute-start | bytes 1572872 | tf_op jit(solution)/shard_map/ppermute | solution.py:31
  175.2 2.7 %collective-permute-start.23 = (bf16[128,1024]{1,0:T(8,128)(2,1)S(1)}, bf16[128,1024]{1,0:T(8,128)(2,1)S(1)}, u32[]{:S(2)}, u32[]{:S(2)}) collective-permute-start(bf16[128,1024]{1,0:T(8,128)(2,1)S(1)} %get-tuple-element.64), channel_id=1, source_target_pairs={{0,96},{16,112},{32,0},{48,16},{64,32},{80,48},{96,64},{112,80},{1... | collective-permute-start | bytes 786440 | tf_op jit(solution)/shard_map/ppermute | solution.py:27
  177.9 1.2 collective-permute-start.24
  179.1 6.9 %collective-permute-done.22 = bf16[128,2048]{1,0:T(8,128)(2,1)S(1)} collective-permute-done((bf16[128,2048]{1,0:T(8,128)(2,1)S(1)}, bf16[128,2048]{1,0:T(8,128)(2,1)S(1)}, u32[]{:S(2)}, u32[]{:S(2)}) %collective-permute-start.22) | collective-permute-done | bytes 524320 | tf_op jit(solution)/shard_map/ppermute | solution.py:31
  186.2 5.4 %collective-permute-done.24 = bf16[128,1024]{1,0:T(8,128)(2,1)S(1)} collective-permute-done((bf16[128,1024]{1,0:T(8,128)(2,1)S(1)}, bf16[128,1024]{1,0:T(8,128)(2,1)S(1)}, u32[]{:S(2)}, u32[]{:S(2)}) %collective-permute-start.24) | collective-permute-done | bytes 262176 | tf_op jit(solution)/shard_map/ppermute | solution.py:27
  192.4 1.1 collective-permute-start.26
  193.5 2.1 %collective-permute-start.27 = (bf16[128,512]{1,0:T(8,128)(2,1)S(1)}, bf16[128,512]{1,0:T(8,128)(2,1)S(1)}, u32[]{:S(2)}, u32[]{:S(2)}) collective-permute-start(bf16[128,512]{1,0:T(8,128)(2,1)S(1)} %get-tuple-element.61), channel_id=1, source_target_pairs={{0,96},{16,112},{32,0},{48,16},{64,32},{80,48},{96,64},{112,80},{1... | collective-permute-start | bytes 393224 | tf_op jit(solution)/shard_map/ppermute | solution.py:27
  195.7 3.0 %collective-permute-done.25 = bf16[128,512]{1,0:T(8,128)(2,1)S(1)} collective-permute-done((bf16[128,512]{1,0:T(8,128)(2,1)S(1)}, bf16[128,512]{1,0:T(8,128)(2,1)S(1)}, u32[]{:S(2)}, u32[]{:S(2)}) %collective-permute-start.25) | collective-permute-done | bytes 131104 | tf_op jit(solution)/shard_map/ppermute | solution.py:31
  198.7 1.9 collective-permute-done.27
  200.6 1.5 collective-permute-done.28
  (134 shorter events, 19.0 us)
Async XLA Ops:
  3.3 24.6 %collective-permute-start = (bf16[256,384]{1,0:T(8,128)(2,1)S(1)}, bf16[256,384]{1,0:T(8,128)(2,1)S(1)}, u32[]{:S(2)}, u32[]{:S(2)}) collective-permute-start(bf16[256,384]{1,0:T(8,128)(2,1)S(1)} %pad_maximum_fusion.5), channel_id=1, source_target_pairs={{0,4},{1,5},{2,6},{3,7},{4,8},{5,9},{6,10},{7,11},{8,12},{9,13},{1... | collective-permute-start | bytes 589832 | tf_op jit(solution)/shard_map/ppermute | solution.py:36
  3.8 24.1 %collective-permute-start.1 = (bf16[256,384]{1,0:T(8,128)(2,1)S(1)}, bf16[256,384]{1,0:T(8,128)(2,1)S(1)}, u32[]{:S(2)}, u32[]{:S(2)}) collective-permute-start(bf16[256,384]{1,0:T(8,128)(2,1)S(1)} %pad_maximum_fusion.6), channel_id=1, source_target_pairs={{0,8},{1,9},{2,10},{3,11},{4,12},{5,13},{6,14},{7,15},{8,0},{9,1},... | collective-permute-start | bytes 589832 | tf_op jit(solution)/shard_map/ppermute | solution.py:36
  6.4 21.5 %collective-permute-start.2 = (bf16[256,384]{1,0:T(8,128)(2,1)S(1)}, bf16[256,384]{1,0:T(8,128)(2,1)S(1)}, u32[]{:S(2)}, u32[]{:S(2)}) collective-permute-start(bf16[256,384]{1,0:T(8,128)(2,1)S(1)} %pad_maximum_fusion.7), channel_id=1, source_target_pairs={{0,12},{1,13},{2,14},{3,15},{4,0},{5,1},{6,2},{7,3},{8,4},{9,5},{1... | collective-permute-start | bytes 589832 | tf_op jit(solution)/shard_map/ppermute | solution.py:36
  7.2 19.2 %all-to-all-start = ((s32[128,1,2]{2,1,0:T(1,128)}), s32[128,1,2]{2,1,0:T(1,128)S(1)}, u32[]{:S(2)}, u32[]{:S(2)}) async-start(s32[128,1,2]{2,1,0:T(1,128)} %bitcast.4), calls=%async_computation | async-start | bytes 131072 | tf_op jit(solution)/shard_map/all_to_all | solution.py:414
  27.9 0.7 copy-start.14
  28.7 50.6 %copy-start.2 = (bf16[1024,256]{1,0:T(8,128)(2,1)}, bf16[1024,256]{1,0:T(8,128)(2,1)S(1)}, u32[]{:S(2)}) copy-start(bf16[1024,256]{1,0:T(8,128)(2,1)S(1)} %pad_maximum_fusion.1.near_ref) | copy-start | bytes 1572868
  33.2 7.4 %copy-start.15 = (s32[4,2,16]{2,1,0:T(2,128)S(1)}, s32[4,2,16]{2,1,0:T(2,128)}, u32[]{:S(2)}) copy-start(s32[4,2,16]{2,1,0:T(2,128)} %param.24) | copy-start | bytes 1540
  33.2 7.5 %copy-start.16 = (bf16[4096]{0:T(1024)(128)(2,1)S(1)}, bf16[4096]{0:T(1024)(128)(2,1)}, u32[]{:S(2)}) copy-start(bf16[4096]{0:T(1024)(128)(2,1)} %param.18) | copy-start | bytes 24580
  33.2 7.8 %copy-start.11 = (bf16[256,512]{1,0:T(8,128)(2,1)S(1)}, bf16[256,512]{1,0:T(8,128)(2,1)}, u32[]{:S(2)}) copy-start(bf16[256,512]{1,0:T(8,128)(2,1)} %param.16) | copy-start | bytes 786436
  33.2 35.7 %all-to-all-start.1 = ((bf16[256,32,128]{2,1,0:T(8,128)(2,1)}), bf16[256,32,128]{2,1,0:T(8,128)(2,1)}, u32[]{:S(2)}, u32[]{:S(2)}) async-start(bf16[256,32,128]{2,1,0:T(8,128)(2,1)} %gather_fusion), calls=%async_computation.1 | async-start | bytes 4194304 | tf_op jit(solution)/shard_map/all_to_all | solution.py:90
  41.1 33.9 %collective-permute-start.6 = (bf16[256,512]{1,0:T(8,128)(2,1)S(1)}, bf16[256,512]{1,0:T(8,128)(2,1)S(1)}, u32[]{:S(2)}, u32[]{:S(2)}) collective-permute-start(bf16[256,512]{1,0:T(8,128)(2,1)S(1)} %copy-done.11), channel_id=1, source_target_pairs={{0,32},{16,48},{32,64},{48,80},{64,96},{80,112},{96,0},{112,16},{1... | collective-permute-start | bytes 786440 | tf_op jit(solution)/shard_map/ppermute | solution.py:27
  42.6 34.5 %collective-permute-start.5 = (bf16[256,512]{1,0:T(8,128)(2,1)S(1)}, bf16[256,512]{1,0:T(8,128)(2,1)S(1)}, u32[]{:S(2)}, u32[]{:S(2)}) collective-permute-start(bf16[256,512]{1,0:T(8,128)(2,1)S(1)} %copy-done.11), channel_id=1, source_target_pairs={{0,64},{16,80},{32,96},{48,112},{64,0},{80,16},{96,32},{112,48},{1... | collective-permute-start | bytes 786440 | tf_op jit(solution)/shard_map/ppermute | solution.py:27
  45.4 31.7 %collective-permute-start.4 = (bf16[256,512]{1,0:T(8,128)(2,1)S(1)}, bf16[256,512]{1,0:T(8,128)(2,1)S(1)}, u32[]{:S(2)}, u32[]{:S(2)}) collective-permute-start(bf16[256,512]{1,0:T(8,128)(2,1)S(1)} %copy-done.11), channel_id=1, source_target_pairs={{0,96},{16,112},{32,0},{48,16},{64,32},{80,48},{96,64},{112,80},{1... | collective-permute-start | bytes 786440 | tf_op jit(solution)/shard_map/ppermute | solution.py:27
  46.8 30.3 %collective-permute-start.3 = (bf16[1024,256]{1,0:T(8,128)(2,1)S(1)}, bf16[1024,256]{1,0:T(8,128)(2,1)S(1)}, u32[]{:S(2)}, u32[]{:S(2)}) collective-permute-start(bf16[1024,256]{1,0:T(8,128)(2,1)S(1)} %pad_maximum_fusion.1.near_ref), channel_id=1, source_target_pairs={{0,2},{1,3},{2,0},{3,1},{4,6},{5,7},{6,4},{7,5},{8,10},{9,11},{10,... | collective-permute-start | bytes 1572872 | tf_op jit(solution)/shard_map/ppermute | solution.py:40
  77.1 2.4 %copy-start.4 = (bf16[1024,256]{1,0:T(8,128)(2,1)}, bf16[1024,256]{1,0:T(8,128)(2,1)S(1)}, u32[]{:S(2)}) copy-start(bf16[1024,256]{1,0:T(8,128)(2,1)S(1)} %collective-permute-done.3.side_ref) | copy-start | bytes 1572868
  77.1 35.4 %collective-permute-start.13 = (bf16[128,4096]{1,0:T(8,128)(2,1)}, bf16[128,4096]{1,0:T(8,128)(2,1)}, u32[]{:S(2)}, u32[]{:S(2)}) collective-permute-start(bf16[128,4096]{1,0:T(8,128)(2,1)} %fusion.1.refs_0_), channel_id=1, source_target_pairs={{0,96},{16,112},{32,0},{48,16},{64,32},{80,48},{96,64},{112,80},{1... | collective-permute-start | bytes 3145736 | tf_op jit(solution)/shard_map/ppermute | solution.py:27
  78.8 31.7 %collective-permute-start.11 = (bf16[128,4096]{1,0:T(8,128)(2,1)}, bf16[128,4096]{1,0:T(8,128)(2,1)S(1)}, u32[]{:S(2)}, u32[]{:S(2)}) collective-permute-start(bf16[128,4096]{1,0:T(8,128)(2,1)} %fusion.1.refs_0_), channel_id=1, source_target_pairs={{0,32},{16,48},{32,64},{48,80},{64,96},{80,112},{96,0},{112,16},{1... | collective-permute-start | bytes 3145736 | tf_op jit(solution)/shard_map/ppermute | solution.py:27
  79.3 6.7 %collective-permute-start.7 = (bf16[2048,256]{1,0:T(8,128)(2,1)S(1)}, bf16[2048,256]{1,0:T(8,128)(2,1)S(1)}, u32[]{:S(2)}, u32[]{:S(2)}) collective-permute-start(bf16[2048,256]{1,0:T(8,128)(2,1)S(1)} %pad_maximum_fusion), channel_id=1, source_target_pairs={{0,1},{1,0},{2,3},{3,2},{4,5},{5,4},{6,7},{7,6},{8,9},{9,8},{10,11... | collective-permute-start | bytes 3145736 | tf_op jit(solution)/shard_map/ppermute | solution.py:40
  79.6 6.4 %copy-start.3 = (bf16[1024,256]{1,0:T(8,128)(2,1)S(1)}, bf16[1024,256]{1,0:T(8,128)(2,1)}, u32[]{:S(2)}) copy-start(bf16[1024,256]{1,0:T(8,128)(2,1)} %copy-done.2) | copy-start | bytes 1572868
  79.6 6.3 %copy-start.5 = (bf16[1024,256]{1,0:T(8,128)(2,1)S(1)}, bf16[1024,256]{1,0:T(8,128)(2,1)}, u32[]{:S(2)}) copy-start(bf16[1024,256]{1,0:T(8,128)(2,1)} %copy-done.4) | copy-start | bytes 1572868
  82.4 50.2 %collective-permute-start.16 = (bf16[256,4096]{1,0:T(8,128)(2,1)}, bf16[256,4096]{1,0:T(8,128)(2,1)S(1)}, u32[]{:S(2)}, u32[]{:S(2)}) collective-permute-start(bf16[256,4096]{1,0:T(8,128)(2,1)} %maximum_maximum_fusion), channel_id=1, source_target_pairs={{0,16},{16,0},{32,48},{48,32},{64,80},{80,64},{96,112},{112,96},{1... | collective-permute-start | bytes 6291464 | tf_op jit(solution)/shard_map/ppermute | solution.py:31
  98.5 13.9 %copy-start.17 = (bf16[4096]{0:T(1024)(128)(2,1)S(1)}, bf16[4096]{0:T(1024)(128)(2,1)}, u32[]{:S(2)}) copy-start(bf16[4096]{0:T(1024)(128)(2,1)} %param.17) | copy-start | bytes 24580
  98.6 5.6 %collective-permute-start.8 = (bf16[256,128]{1,0:T(8,128)(2,1)S(1)}, bf16[256,128]{1,0:T(8,128)(2,1)S(1)}, u32[]{:S(2)}, u32[]{:S(2)}) collective-permute-start(bf16[256,128]{1,0:T(8,128)(2,1)S(1)} %get-tuple-element.93), channel_id=1, source_target_pairs={{0,12},{1,13},{2,14},{3,15},{4,0},{5,1},{6,2},{7,3},{8,4},{9,5},{1... | collective-permute-start | bytes 196616 | tf_op jit(solution)/shard_map/ppermute | solution.py:36
  99.5 11.0 %collective-permute-start.10 = (bf16[256,128]{1,0:T(8,128)(2,1)S(1)}, bf16[256,128]{1,0:T(8,128)(2,1)S(1)}, u32[]{:S(2)}, u32[]{:S(2)}) collective-permute-start(bf16[256,128]{1,0:T(8,128)(2,1)S(1)} %get-tuple-element.91), channel_id=1, source_target_pairs={{0,4},{1,5},{2,6},{3,7},{4,8},{5,9},{6,10},{7,11},{8,12},{9,13},{1... | collective-permute-start | bytes 196616 | tf_op jit(solution)/shard_map/ppermute | solution.py:36
  104.2 6.3 %collective-permute-start.9 = (bf16[256,128]{1,0:T(8,128)(2,1)S(1)}, bf16[256,128]{1,0:T(8,128)(2,1)S(1)}, u32[]{:S(2)}, u32[]{:S(2)}) collective-permute-start(bf16[256,128]{1,0:T(8,128)(2,1)S(1)} %get-tuple-element.92), channel_id=1, source_target_pairs={{0,8},{1,9},{2,10},{3,11},{4,12},{5,13},{6,14},{7,15},{8,0},{9,1},... | collective-permute-start | bytes 196616 | tf_op jit(solution)/shard_map/ppermute | solution.py:36
  111.4 1.0 copy-start.6
  112.4 15.3 %collective-permute-start.12 = (bf16[64,4096]{1,0:T(8,128)(2,1)}, bf16[64,4096]{1,0:T(8,128)(2,1)}, u32[]{:S(2)}, u32[]{:S(2)}) collective-permute-start(bf16[64,4096]{1,0:T(8,128)(2,1)} %slice.79), channel_id=1, source_target_pairs={{0,32},{16,48},{32,64},{48,80},{64,96},{80,112},{96,0},{112,16},{1... | collective-permute-start | bytes 1572872 | tf_op jit(solution)/shard_map/ppermute | solution.py:27
  113.6 15.1 %collective-permute-start.14 = (bf16[64,4096]{1,0:T(8,128)(2,1)S(1)}, bf16[64,4096]{1,0:T(8,128)(2,1)S(1)}, u32[]{:S(2)}, u32[]{:S(2)}) collective-permute-start(bf16[64,4096]{1,0:T(8,128)(2,1)S(1)} %slice.80), channel_id=1, source_target_pairs={{0,96},{16,112},{32,0},{48,16},{64,32},{80,48},{96,64},{112,80},{1... | collective-permute-start | bytes 1572872 | tf_op jit(solution)/shard_map/ppermute | solution.py:27
  116.8 19.2 %copy-start.1 = (bf16[4096,512]{1,0:T(8,128)(2,1)S(1)}, bf16[4096,512]{1,0:T(8,128)(2,1)}, u32[]{:S(2)}) copy-start(bf16[4096,512]{1,0:T(8,128)(2,1)} %w_ref.1) | copy-start | bytes 12582916
  128.8 26.2 %collective-permute-start.15 = (bf16[128,4096]{1,0:T(8,128)(2,1)S(1)}, bf16[128,4096]{1,0:T(8,128)(2,1)S(1)}, u32[]{:S(2)}, u32[]{:S(2)}) collective-permute-start(bf16[128,4096]{1,0:T(8,128)(2,1)S(1)} %constant_dynamic-update-slice_fusion.refs_2_), channel_id=1, source_target_pairs={{0,16},{16,0},{32,48},{48,32},{64,80},{80,64},{96,112},{112,96},{1... | collective-permute-start | bytes 3145736 | tf_op jit(solution)/shard_map/ppermute | solution.py:31
  132.7 9.2 %copy-start.7 = (bf16[128,4096]{1,0:T(8,128)(2,1)S(1)}, bf16[128,4096]{1,0:T(8,128)(2,1)}, u32[]{:S(2)}) copy-start(bf16[128,4096]{1,0:T(8,128)(2,1)} %copy-done.6) | copy-start | bytes 3145732
  132.8 26.1 %collective-permute-start.19 = (bf16[128,4096]{1,0:T(8,128)(2,1)S(1)}, bf16[128,4096]{1,0:T(8,128)(2,1)S(1)}, u32[]{:S(2)}, u32[]{:S(2)}) collective-permute-start(bf16[128,4096]{1,0:T(8,128)(2,1)S(1)} %slice.112.refs_0_), channel_id=1, source_target_pairs={{0,32},{16,48},{32,64},{48,80},{64,96},{80,112},{96,0},{112,16},{1... | collective-permute-start | bytes 3145736 | tf_op jit(solution)/shard_map/ppermute | solution.py:27
  133.3 25.5 %collective-permute-start.18 = (bf16[128,4096]{1,0:T(8,128)(2,1)S(1)}, bf16[128,4096]{1,0:T(8,128)(2,1)S(1)}, u32[]{:S(2)}, u32[]{:S(2)}) collective-permute-start(bf16[128,4096]{1,0:T(8,128)(2,1)S(1)} %slice.112.refs_0_), channel_id=1, source_target_pairs={{0,96},{16,112},{32,0},{48,16},{64,32},{80,48},{96,64},{112,80},{1... | collective-permute-start | bytes 3145736 | tf_op jit(solution)/shard_map/ppermute | solution.py:27
  139.5 12.3 %collective-permute-start.17 = (bf16[64,512]{1,0:T(8,128)(2,1)S(1)}, bf16[64,512]{1,0:T(8,128)(2,1)S(1)}, u32[]{:S(2)}, u32[]{:S(2)}) collective-permute-start(bf16[64,512]{1,0:T(8,128)(2,1)S(1)} %slice.110), channel_id=1, source_target_pairs={{1,0},{2,1},{3,2},{4,3},{5,4},{6,5},{7,6},{8,7},{9,8},{10,9},{11,1... | collective-permute-start | bytes 196616 | tf_op jit(solution)/shard_map/ppermute | solution.py:46
  141.9 3.4 %copy-start = (bf16[512,8,2,512]{3,1,2,0:T(8,128)(2,1)S(1)}, bf16[512,8,2,512]{3,1,2,0:T(8,128)(2,1)}, u32[]{:S(2)}) copy-start(bf16[512,8,2,512]{3,1,2,0:T(8,128)(2,1)} %copy.18) | copy-start | bytes 25165828
  145.3 9.6 %copy-start.10 = (bf16[512,4096]{1,0:T(8,128)(2,1)S(1)}, bf16[512,4096]{1,0:T(8,128)(2,1)}, u32[]{:S(2)}) copy-start(bf16[512,4096]{1,0:T(8,128)(2,1)} %param.22) | copy-start | bytes 12582916
  151.8 7.0 %copy-start.8 = (s32[4]{0:T(128)S(1)}, s32[4]{0:T(128)}, u32[]{:S(2)}) copy-start(s32[4]{0:T(128)} %counts.1) | copy-start | bytes 52
  158.8 10.2 %copy-start.9 = (bf16[512,4096]{1,0:T(8,128)(2,1)S(1)}, bf16[512,4096]{1,0:T(8,128)(2,1)}, u32[]{:S(2)}) copy-start(bf16[512,4096]{1,0:T(8,128)(2,1)} %param.23) | copy-start | bytes 12582916
  167.1 6.6 %collective-permute-start.20 = (bf16[64,512]{1,0:T(8,128)(2,1)S(1)}, bf16[64,512]{1,0:T(8,128)(2,1)S(1)}, u32[]{:S(2)}, u32[]{:S(2)}) collective-permute-start(bf16[64,512]{1,0:T(8,128)(2,1)S(1)} %get-tuple-element.55), channel_id=1, source_target_pairs={{0,1},{1,2},{2,3},{3,4},{4,5},{5,6},{6,7},{7,8},{8,9},{9,10},{10,1... | collective-permute-start | bytes 196616 | tf_op jit(solution)/shard_map/ppermute | solution.py:46
  169.9 16.1 %collective-permute-start.22 = (bf16[128,2048]{1,0:T(8,128)(2,1)S(1)}, bf16[128,2048]{1,0:T(8,128)(2,1)S(1)}, u32[]{:S(2)}, u32[]{:S(2)}) collective-permute-start(bf16[128,2048]{1,0:T(8,128)(2,1)S(1)} %pad_maximum_fusion.2), channel_id=1, source_target_pairs={{0,16},{16,0},{32,48},{48,32},{64,80},{80,64},{96,112},{112,96},{1... | collective-permute-start | bytes 1572872 | tf_op jit(solution)/shard_map/ppermute | solution.py:31
  174.6 17.0 %collective-permute-start.21 = (bf16[128,1024]{1,0:T(8,128)(2,1)S(1)}, bf16[128,1024]{1,0:T(8,128)(2,1)S(1)}, u32[]{:S(2)}, u32[]{:S(2)}) collective-permute-start(bf16[128,1024]{1,0:T(8,128)(2,1)S(1)} %get-tuple-element.59), channel_id=1, source_target_pairs={{0,32},{16,48},{32,64},{48,80},{64,96},{80,112},{96,0},{112,16},{1... | collective-permute-start | bytes 786440 | tf_op jit(solution)/shard_map/ppermute | solution.py:27
  175.2 16.5 %collective-permute-start.23 = (bf16[128,1024]{1,0:T(8,128)(2,1)S(1)}, bf16[128,1024]{1,0:T(8,128)(2,1)S(1)}, u32[]{:S(2)}, u32[]{:S(2)}) collective-permute-start(bf16[128,1024]{1,0:T(8,128)(2,1)S(1)} %get-tuple-element.64), channel_id=1, source_target_pairs={{0,96},{16,112},{32,0},{48,16},{64,32},{80,48},{96,64},{112,80},{1... | collective-permute-start | bytes 786440 | tf_op jit(solution)/shard_map/ppermute | solution.py:27
  177.9 13.7 %collective-permute-start.24 = (bf16[128,1024]{1,0:T(8,128)(2,1)S(1)}, bf16[128,1024]{1,0:T(8,128)(2,1)S(1)}, u32[]{:S(2)}, u32[]{:S(2)}) collective-permute-start(bf16[128,1024]{1,0:T(8,128)(2,1)S(1)} %get-tuple-element.66), channel_id=1, source_target_pairs={{0,64},{16,80},{32,96},{48,112},{64,0},{80,16},{96,32},{112,48},{1... | collective-permute-start | bytes 786440 | tf_op jit(solution)/shard_map/ppermute | solution.py:27
  186.1 16.0 %copy-start.12 = (bf16[256,512]{1,0:T(8,128)(2,1)S(1)}, bf16[256,512]{1,0:T(8,128)(2,1)}, u32[]{:S(2)}) copy-start(bf16[256,512]{1,0:T(8,128)(2,1)} %param.16) | copy-start | bytes 786436
  191.8 6.9 %collective-permute-start.25 = (bf16[128,512]{1,0:T(8,128)(2,1)S(1)}, bf16[128,512]{1,0:T(8,128)(2,1)S(1)}, u32[]{:S(2)}, u32[]{:S(2)}) collective-permute-start(bf16[128,512]{1,0:T(8,128)(2,1)S(1)} %dynamic-slice_convert_fusion.3), channel_id=1, source_target_pairs={{0,16},{16,0},{32,48},{48,32},{64,80},{80,64},{96,112},{112,96},{1... | collective-permute-start | bytes 393224 | tf_op jit(solution)/shard_map/ppermute | solution.py:31
  192.4 6.4 %collective-permute-start.26 = (bf16[128,512]{1,0:T(8,128)(2,1)S(1)}, bf16[128,512]{1,0:T(8,128)(2,1)S(1)}, u32[]{:S(2)}, u32[]{:S(2)}) collective-permute-start(bf16[128,512]{1,0:T(8,128)(2,1)S(1)} %get-tuple-element.60), channel_id=1, source_target_pairs={{0,32},{16,48},{32,64},{48,80},{64,96},{80,112},{96,0},{112,16},{1... | collective-permute-start | bytes 393224 | tf_op jit(solution)/shard_map/ppermute | solution.py:27
  193.5 7.1 %collective-permute-start.27 = (bf16[128,512]{1,0:T(8,128)(2,1)S(1)}, bf16[128,512]{1,0:T(8,128)(2,1)S(1)}, u32[]{:S(2)}, u32[]{:S(2)}) collective-permute-start(bf16[128,512]{1,0:T(8,128)(2,1)S(1)} %get-tuple-element.61), channel_id=1, source_target_pairs={{0,96},{16,112},{32,0},{48,16},{64,32},{80,48},{96,64},{112,80},{1... | collective-permute-start | bytes 393224 | tf_op jit(solution)/shard_map/ppermute | solution.py:27
  195.6 6.5 %collective-permute-start.28 = (bf16[128,512]{1,0:T(8,128)(2,1)S(1)}, bf16[128,512]{1,0:T(8,128)(2,1)S(1)}, u32[]{:S(2)}, u32[]{:S(2)}) collective-permute-start(bf16[128,512]{1,0:T(8,128)(2,1)S(1)} %get-tuple-element.62), channel_id=1, source_target_pairs={{0,64},{16,80},{32,96},{48,112},{64,0},{80,16},{96,32},{112,48},{1... | collective-permute-start | bytes 393224 | tf_op jit(solution)/shard_map/ppermute | solution.py:27
  (1 other events, 0.7 us)
